TPU v7x, 128 devices: a whole 4x4x4 slice. The times are simulated.
128 devices in a mesh: seg: 8 (over y, core), col: 16 (over x, z).
Axes of the slice: x: 4, y: 4, z: 4, core: 2. Of those that a mesh axis runs over, the one named last changes fastest.
Arguments:
- segment_state: float32 [16, 2, 32, 32768], P('seg', None, None, 'col'), may hold values from -6 to 6
- light: float32 [16, 32, 32768], P('seg', None, 'col'), may hold values from 0.05 to 1
- mixing: float32 [16, 6, 32, 32768], P('seg', None, None, 'col'), may hold values from 0.04 to 0.3
- kappa: float32 [16, 32, 32768], P('seg', None, 'col'), may hold values from 0.05 to 2
- neighbour_columns: int32 [32768, 6], P('col'), may hold values from 0 to 32767, as said below
- wet_levels: int32 [32768], P('col'), may hold values from 1 to 32
- basis: float32 [4, 16, 2, 32, 32768], P(None, 'seg', None, None, 'col'), may hold values from -0.0009765625 to 0.0009765625
Outputs:
- residual: float32 [16, 2, 32, 32768], P('seg', None, None, 'col')
- new_vector: float32 [16, 2, 32, 32768], P('seg', None, None, 'col')
- coefficients: float32 [5], replicated
Inputs may be any that keep to these rules, and one draw needn't show every extreme that they name: `neighbour_columns`: entry 0 of each row is the column itself; every entry lies within 512 columns of its own column, counted cyclically over all 32768 columns, and that distance is reached on both sides by the first and last column of every block of 2048 columns.
All inputs are finite; a program needn't handle non-finite values.
Results may differ from a plain program's by a relative error of at most 0.00013.
Values sent between devices are 32-bit elements; how exact they have to be, the bound alone decides.
No kernel may reach another device: no remote copies, remote signals or barrier semaphores. Data moves between devices by JAX's collectives and lax.ppermute only.
A program may use at most 128 MiB of HBM per device.

v0:
```python
import jax
import jax.numpy as jnp
from jax import lax
from jax.sharding import PartitionSpec as P

uptake_rate = 0.6
half_saturation = 0.3
remin_rate = 0.2
dissolved_share = 0.7
epsilon = 1e-06


def extended_2(cells, sides, width):
    for axis, dim in sides:
        count = lax.axis_size(axis)
        head = lax.slice_in_dim(cells, 0, width, axis=dim)
        tail = lax.slice_in_dim(cells, cells.shape[dim] - width, cells.shape[dim], axis=dim)
        cells = jnp.concatenate(
            [
                lax.ppermute(tail, axis, [(i, (i + 1) % count) for i in range(count)]),
                cells,
                lax.ppermute(head, axis, [((i + 1) % count, i) for i in range(count)]),
            ],
            axis=dim,
        )
    return cells


def from_behind(block, axis, distance):
    devices = range(lax.axis_size(axis))
    route = [((i - distance) % len(devices), i) for i in devices]
    return lax.ppermute(block, axis, route)


def sources(field, light):
    phosphate = field[:, 0]
    organic = field[:, 1]
    squared = phosphate * phosphate
    uptake = uptake_rate * light * squared / (squared + half_saturation)
    return jnp.stack(
        [remin_rate * organic - uptake, dissolved_share * uptake - remin_rate * organic], axis=1
    )


def couplings(kappa, wet_flags):
    depth_index = lax.broadcasted_iota(jnp.int32, wet_flags.shape, 0)
    upper = jnp.where((depth_index >= 1) & wet_flags, kappa, jnp.float32(0.0))
    lower = jnp.concatenate([upper[:, 1:], jnp.zeros_like(upper[:, :1])], axis=1)
    return (upper[:, None], lower[:, None])


def vertical_solve(source, upper, lower):
    number = source.shape[-2]
    diagonal = 1.0 + upper + lower
    ratio = -lower[..., 0, :] / diagonal[..., 0, :]
    value = source[..., 0, :] / diagonal[..., 0, :]
    ratios = [ratio]
    values = [value]
    for layer in range(1, number):
        pivot = diagonal[..., layer, :] + upper[..., layer, :] * ratio
        ratio = -lower[..., layer, :] / pivot
        value = (source[..., layer, :] + upper[..., layer, :] * value) / pivot
        ratios.append(ratio)
        values.append(value)
    result = values[-1]
    solved = [result]
    for layer in range(number - 2, -1, -1):
        result = values[layer] - ratios[layer] * result
        solved.append(result)
    return jnp.stack(solved[::-1], axis=-2)


def transport(extended, table, mixing_rows):
    segs, tracers, levels, spread_cols = extended.shape
    width = table.shape[0]
    column_rows = extended.reshape(segs * tracers * levels, spread_cols).T
    total = None
    for neighbour in range(table.shape[1]):
        picked = jnp.take(column_rows, table[:, neighbour], axis=0).reshape(
            width, segs, tracers, levels
        )
        term = mixing_rows[neighbour][:, :, None, :] * picked
        total = term if total is None else total + term
    return total.reshape(width, segs * tracers * levels).T.reshape(segs, tracers, levels, width)


def surroundings(field):
    return extended_2(field, (("col", 3),), field.shape[3])


def combine(weights, basis):
    return jnp.einsum("m,msjlc->sjlc", weights, basis, precision=lax.Precision.HIGHEST)


def projections(basis, vector):
    return jnp.sum(basis * vector[None], axis=(1, 2, 3, 4))


def per_device(segment_state, light, mixing, kappa, neighbour_columns, wet_levels, basis):
    width = segment_state.shape[3]
    start = lax.axis_index("col") * width
    every_column = lax.axis_size("col") * width
    table = (neighbour_columns - start + width) % every_column
    mixing_rows = jnp.transpose(mixing, (1, 3, 0, 2))
    depth_index = lax.broadcasted_iota(jnp.int32, (segment_state.shape[2], width), 0)
    wet_flags = depth_index < wet_levels[None, :]
    wet_float = wet_flags.astype(jnp.float32)
    upper, lower = couplings(kappa, wet_flags)
    field = segment_state
    for turn in range(2):
        extended = surroundings(field)
        sourced = transport(extended, table, mixing_rows) + sources(field, light)
        field = vertical_solve(sourced, upper, lower) * wet_float
    incoming = from_behind(field[-1], "seg", 1)
    previous = jnp.concatenate([incoming[None], field[:-1]], axis=0)
    residual = wet_float * (segment_state - previous)
    count = (
        lax.axis_size("seg")
        * segment_state.shape[0]
        * segment_state.shape[1]
        * segment_state.shape[2]
        * lax.axis_size("col")
        * width
    )
    first = lax.psum(projections(basis, residual), ("seg", "col"))
    middle = residual - combine(first, basis)
    second = lax.psum(projections(basis, middle), ("seg", "col"))
    ortho = middle - combine(second, basis)
    squares = lax.psum(jnp.sum(ortho * ortho), ("seg", "col"))
    spread = jnp.sqrt(squares / count + epsilon)
    new_vector = ortho / spread
    coefficients = jnp.concatenate([first + second, spread[None]])
    return (residual, new_vector, coefficients)


def solution(mesh):
    return jax.shard_map(
        per_device,
        mesh=mesh,
        in_specs=(
            P("seg", None, None, "col"),
            P("seg", None, "col"),
            P("seg", None, None, "col"),
            P("seg", None, "col"),
            P("col", None),
            P("col"),
            P(None, "seg", None, None, "col"),
        ),
        out_specs=(P("seg", None, None, "col"), P("seg", None, None, "col"), P()),
        check_vma=False,
    )
```

profile of v0, /device:TPU:0, one launch (start us, length us, event | category | flops | bytes accessed | tf_op | source)
XLA Modules:
  0.0 457.8 jit_solution(8521703132048550764)
XLA Ops:
  0.6 6.4 %collective-permute-start.1 = (f32[2,2,32,2048]{3,2,1,0:T(8,128)}, f32[2,2,32,2048]{3,2,1,0:T(8,128)}, u32[]{:S(2)}, u32[]{:S(2)}) collective-permute-start(f32[2,2,32,2048]{3,2,1,0:T(8,128)} %param.9), channel_id=1, source_target_pairs={{1,0},{2,1},{3,2},{4,3},{5,4},{6,5},{7,6},{8,7},{9,8},{10,9},{11,1... | collective-permute-start | bytes 3145736 | tf_op jit(solution)/shard_map/ppermute | solution.py:22
  13.6 1.5 pad_bitcast_fusion
  15.1 1.2 slice_bitcast_fusion.6
  27.5 1.3 copy.263
  28.9 1.1 mul.7202
  30.0 1.3 copy.188
  31.4 1.4 copy.187
  32.9 1.4 copy.186
  34.4 1.3 copy.185
  35.7 1.3 mul.7186
  37.0 1.3 copy.184
  38.3 2.5 fusion.87
  40.9 1.2 subtract_bitcast_fusion.3
  42.1 3.5 pad_maximum_fusion
  45.6 2.9 copy.182
  48.5 8.4 %gather_fusion.5 = f32[2048,128]{1,0:T(8,128)} fusion(f32[6144,128]{1,0:T(8,128)S(1)} %bitcast.578, s32[2048]{0:T(1024)} %get-tuple-element.287), kind=kCustom, calls=%fused_computation.5.clone | custom fusion | bytes 2105344 | tf_op jit(solution)/shard_map/jit(_take)/gather | solution.py:79
  56.8 8.3 %gather_fusion.4 = f32[2048,128]{1,0:T(8,128)} fusion(f32[6144,128]{1,0:T(8,128)S(1)} %bitcast.579, s32[2048]{0:T(1024)} %get-tuple-element.286), kind=kCustom, calls=%fused_computation.4.clone | custom fusion | bytes 2105344 | tf_op jit(solution)/shard_map/jit(_take)/gather | solution.py:79
  65.1 8.3 %gather_fusion.3 = f32[2048,128]{1,0:T(8,128)} fusion(f32[6144,128]{1,0:T(8,128)S(1)} %bitcast.580, s32[2048]{0:T(1024)} %get-tuple-element.285), kind=kCustom, calls=%fused_computation.3.clone | custom fusion | bytes 2105344 | tf_op jit(solution)/shard_map/jit(_take)/gather | solution.py:79
  73.5 8.3 %gather_fusion.2 = f32[2048,128]{1,0:T(8,128)} fusion(f32[6144,128]{1,0:T(8,128)S(1)} %bitcast.581, s32[2048]{0:T(1024)} %get-tuple-element.284), kind=kCustom, calls=%fused_computation.2.clone | custom fusion | bytes 2105344 | tf_op jit(solution)/shard_map/jit(_take)/gather | solution.py:79
  81.8 8.3 %gather_fusion.1 = f32[2048,128]{1,0:T(8,128)} fusion(f32[6144,128]{1,0:T(8,128)S(1)} %bitcast.582, s32[2048]{0:T(1024)} %get-tuple-element.283), kind=kCustom, calls=%fused_computation.1.clone | custom fusion | bytes 2105344 | tf_op jit(solution)/shard_map/jit(_take)/gather | solution.py:79
  90.1 8.3 %gather_fusion = f32[2048,128]{1,0:T(8,128)} fusion(f32[6144,128]{1,0:T(8,128)S(1)} %bitcast.583, s32[2048]{0:T(1024)} %get-tuple-element.288), kind=kCustom, calls=%fused_computation.clone | custom fusion | bytes 2105344 | tf_op jit(solution)/shard_map/jit(_take)/gather | solution.py:79
  98.4 7.7 %fusion.12 = f32[128,2048]{0,1:T(8,128)S(1)} fusion(f32[2048,128]{1,0:T(8,128)} %copy.188, f32[2048,128]{1,0:T(8,128)} %gather_fusion.5, f32[2048,128]{1,0:T(8,128)} %copy.187, f32[2048,128]{1,0:T(8,128)} %gather_fusion.4, f32[2048,128]{1,0:T(8,128)} %copy.186, f32[2048,128]{1,0:T(8,128)} %gather_fusion.3, f32[2048,128]{1,0:T(8,128)} %copy.185, ...), kind=kLoop, calls=%fused_computation.40 | loop fusion | flops 4456448 | bytes 13643776 | tf_op jit(solution)/shard_map/transpose | solution.py:84
  107.4 3.5 broadcast_multiply_fusion.2
  111.2 1.3 multiply_subtract_fusion.31
  114.2 5.4 %collective-permute-start.3 = (f32[2,2,32,2048]{3,1,2,0:T(2,128)S(1)}, f32[2,2,32,2048]{3,1,2,0:T(2,128)S(1)}, u32[]{:S(2)}, u32[]{:S(2)}) collective-permute-start(f32[2,2,32,2048]{3,1,2,0:T(2,128)S(1)} %broadcast_multiply_fusion), channel_id=1, source_target_pairs={{1,0},{2,1},{3,2},{4,3},{5,4},{6,5},{7,6},{8,7},{9,8},{10,9},{11,1... | collective-permute-start | bytes 3145736 | tf_op jit(solution)/shard_map/ppermute | solution.py:22
  120.4 1.5 subtract_bitcast_fusion.1
  121.9 19.5 %collective-permute-done.3 = f32[2,2,32,2048]{3,1,2,0:T(2,128)S(1)} collective-permute-done((f32[2,2,32,2048]{3,1,2,0:T(2,128)S(1)}, f32[2,2,32,2048]{3,1,2,0:T(2,128)S(1)}, u32[]{:S(2)}, u32[]{:S(2)}) %collective-permute-start.3) | collective-permute-done | bytes 1048608 | tf_op jit(solution)/shard_map/ppermute | solution.py:22
  141.4 5.5 %collective-permute-done.2 = f32[2,2,32,2048]{3,1,2,0:T(2,128)S(1)} collective-permute-done((f32[2,2,32,2048]{3,1,2,0:T(2,128)S(1)}, f32[2,2,32,2048]{3,1,2,0:T(2,128)S(1)}, u32[]{:S(2)}, u32[]{:S(2)}) %collective-permute-start.2) | collective-permute-done | bytes 1048608 | tf_op jit(solution)/shard_map/ppermute | solution.py:20
  147.0 1.9 pad_maximum_fusion.1
  148.9 3.5 copy.261
  152.4 2.4 copy.262
  154.7 8.4 %gather_fusion.11 = f32[2048,128]{1,0:T(8,128)} fusion(f32[6144,128]{1,0:T(8,128)S(1)} %bitcast.572, s32[2048]{0:T(1024)} %get-tuple-element.287), kind=kCustom, calls=%fused_computation.11.clone | custom fusion | bytes 2105344 | tf_op jit(solution)/shard_map/jit(_take)/gather | solution.py:79
  163.1 8.3 %gather_fusion.10 = f32[2048,128]{1,0:T(8,128)} fusion(f32[6144,128]{1,0:T(8,128)S(1)} %bitcast.573, s32[2048]{0:T(1024)} %get-tuple-element.286), kind=kCustom, calls=%fused_computation.10.clone | custom fusion | bytes 2105344 | tf_op jit(solution)/shard_map/jit(_take)/gather | solution.py:79
  171.4 8.3 %gather_fusion.9 = f32[2048,128]{1,0:T(8,128)} fusion(f32[6144,128]{1,0:T(8,128)S(1)} %bitcast.574, s32[2048]{0:T(1024)} %get-tuple-element.285), kind=kCustom, calls=%fused_computation.9.clone | custom fusion | bytes 2105344 | tf_op jit(solution)/shard_map/jit(_take)/gather | solution.py:79
  179.7 8.3 %gather_fusion.8 = f32[2048,128]{1,0:T(8,128)} fusion(f32[6144,128]{1,0:T(8,128)S(1)} %bitcast.575, s32[2048]{0:T(1024)} %get-tuple-element.284), kind=kCustom, calls=%fused_computation.8.clone | custom fusion | bytes 2105344 | tf_op jit(solution)/shard_map/jit(_take)/gather | solution.py:79
  188.0 8.3 %gather_fusion.7 = f32[2048,128]{1,0:T(8,128)} fusion(f32[6144,128]{1,0:T(8,128)S(1)} %bitcast.576, s32[2048]{0:T(1024)} %get-tuple-element.283), kind=kCustom, calls=%fused_computation.7.clone | custom fusion | bytes 2105344 | tf_op jit(solution)/shard_map/jit(_take)/gather | solution.py:79
  196.3 8.3 %gather_fusion.6 = f32[2048,128]{1,0:T(8,128)} fusion(f32[6144,128]{1,0:T(8,128)S(1)} %bitcast.577, s32[2048]{0:T(1024)} %get-tuple-element.288), kind=kCustom, calls=%fused_computation.6.clone | custom fusion | bytes 2105344 | tf_op jit(solution)/shard_map/jit(_take)/gather | solution.py:79
  204.6 7.7 %fusion.6 = f32[128,2048]{0,1:T(8,128)S(1)} fusion(f32[2048,128]{1,0:T(8,128)} %copy.188, f32[2048,128]{1,0:T(8,128)} %gather_fusion.11, f32[2048,128]{1,0:T(8,128)} %copy.187, f32[2048,128]{1,0:T(8,128)} %gather_fusion.10, f32[2048,128]{1,0:T(8,128)} %copy.186, f32[2048,128]{1,0:T(8,128)} %gather_fusion.9, f32[2048,128]{1,0:T(8,128)} %copy.185, ...), kind=kLoop, calls=%fused_computation.28 | loop fusion | flops 4456448 | bytes 13643776 | tf_op jit(solution)/shard_map/transpose | solution.py:84
  213.6 3.5 fusion.25
  217.3 2.6 multiply_subtract_fusion
  219.9 4.0 stack.23
  224.2 9.8 %collective-permute-done.4 = f32[2,32,2048]{2,1,0:T(8,128)S(1)} collective-permute-done((f32[2,32,2048]{2,1,0:T(8,128)S(1)}, f32[2,32,2048]{2,1,0:T(8,128)S(1)}, u32[]{:S(2)}, u32[]{:S(2)}) %collective-permute-start.4) | collective-permute-done | bytes 524320 | tf_op jit(solution)/shard_map/ppermute | solution.py:32
  234.6 62.3 %psum.21 = f32[4]{0:T(128)S(1)} all-reduce(f32[4]{0:T(128)S(1)} %multiply_reduce_fusion.1), channel_id=1, replica_groups=mesh['seg'=8,'col'=16] {'seg','col'}, use_global_device_ids=true, to_apply=%region_1.3 | all-reduce | flops 4 | bytes 32 | tf_op jit(solution)/shard_map/psum | solution.py:125
  296.9 12.6 %fusion.2 = f32[1,2,2,32,2048]{4,0,3,2,1:T(1,128)S(1)} fusion(f32[4,2,2,32,2048]{4,3,2,1,0:T(8,128)} %param.15, f32[4]{0:T(128)S(1)} %psum.21), kind=kOutput, calls=%fused_computation.16 | convolution fusion | flops 12582912 | bytes 5242896 | tf_op jit(solution)/shard_map/m,msjlc->sjlc/dot_general | solution.py:92
  310.3 1.5 copy-done.1
  313.5 64.0 %psum.22 = f32[4]{0:T(128)S(1)} all-reduce(f32[4]{0:T(128)S(1)} %multiply_reduce_fusion), channel_id=1, replica_groups=mesh['seg'=8,'col'=16] {'seg','col'}, use_global_device_ids=true, to_apply=%region_3.5 | all-reduce | flops 4 | bytes 32 | tf_op jit(solution)/shard_map/psum | solution.py:127
  377.5 12.7 %fusion = f32[1,2,2,32,2048]{4,0,3,2,1:T(1,128)S(1)} fusion(f32[4,2,2,32,2048]{4,3,2,1,0:T(8,128)} %param.15, f32[4]{0:T(128)S(1)} %psum.22), kind=kOutput, calls=%fused_computation.14 | convolution fusion | flops 12582912 | bytes 5242896 | tf_op jit(solution)/shard_map/m,msjlc->sjlc/dot_general | solution.py:92
  392.3 62.4 %psum.23 = f32[]{:T(128)} all-reduce(f32[]{:T(128)} %multiply_reduce_fusion.2), channel_id=1, replica_groups=mesh['seg'=8,'col'=16] {'seg','col'}, use_global_device_ids=true, to_apply=%region_5.7 | all-reduce | flops 1 | bytes 8 | tf_op jit(solution)/shard_map/psum | solution.py:129
  (334 shorter events, 29.8 us)
Async XLA Ops:
  0.6 12.3 %copy-start.8 = (f32[2,32,2048]{2,1,0:T(8,128)S(1)}, f32[2,32,2048]{2,1,0:T(8,128)}, u32[]{:S(2)}) copy-start(f32[2,32,2048]{2,1,0:T(8,128)} %param.12) | copy-start | bytes 1572868
  0.6 41.4 %collective-permute-start.1 = (f32[2,2,32,2048]{3,2,1,0:T(8,128)}, f32[2,2,32,2048]{3,2,1,0:T(8,128)}, u32[]{:S(2)}, u32[]{:S(2)}) collective-permute-start(f32[2,2,32,2048]{3,2,1,0:T(8,128)} %param.9), channel_id=1, source_target_pairs={{1,0},{2,1},{3,2},{4,3},{5,4},{6,5},{7,6},{8,7},{9,8},{10,9},{11,1... | collective-permute-start | bytes 3145736 | tf_op jit(solution)/shard_map/ppermute | solution.py:22
  7.0 35.1 %collective-permute-start = (f32[2,2,32,2048]{3,2,1,0:T(8,128)}, f32[2,2,32,2048]{3,2,1,0:T(8,128)}, u32[]{:S(2)}, u32[]{:S(2)}) collective-permute-start(f32[2,2,32,2048]{3,2,1,0:T(8,128)} %param.9), channel_id=1, source_target_pairs={{0,1},{1,2},{2,3},{3,4},{4,5},{5,6},{6,7},{7,8},{8,9},{9,10},{10,1... | collective-permute-start | bytes 3145736 | tf_op jit(solution)/shard_map/ppermute | solution.py:20
  12.5 4.4 copy-start.90
  12.5 4.4 copy-start.100
  12.5 5.0 %copy-start.91 = (f32[2,1,1,2048]{3,2,0,1:T(1,128)}, f32[2,1,1,2048]{3,2,0,1:T(1,128)S(1)}, u32[]{:S(2)}) copy-start(f32[2,1,1,2048]{3,2,0,1:T(1,128)S(1)} %get-tuple-element.232) | copy-start | bytes 49156
  12.5 5.0 %copy-start.101 = (f32[2,1,1,2048]{3,2,0,1:T(1,128)}, f32[2,1,1,2048]{3,2,0,1:T(1,128)S(1)}, u32[]{:S(2)}) copy-start(f32[2,1,1,2048]{3,2,0,1:T(1,128)S(1)} %get-tuple-element.242) | copy-start | bytes 49156
  12.5 5.6 %copy-start.92 = (f32[2,1,1,2048]{3,2,0,1:T(1,128)}, f32[2,1,1,2048]{3,2,0,1:T(1,128)S(1)}, u32[]{:S(2)}) copy-start(f32[2,1,1,2048]{3,2,0,1:T(1,128)S(1)} %get-tuple-element.233) | copy-start | bytes 49156
  12.5 5.6 %copy-start.93 = (f32[2,1,1,2048]{3,2,0,1:T(1,128)}, f32[2,1,1,2048]{3,2,0,1:T(1,128)S(1)}, u32[]{:S(2)}) copy-start(f32[2,1,1,2048]{3,2,0,1:T(1,128)S(1)} %get-tuple-element.234) | copy-start | bytes 49156
  12.5 6.2 %copy-start.94 = (f32[2,1,1,2048]{3,2,0,1:T(1,128)}, f32[2,1,1,2048]{3,2,0,1:T(1,128)S(1)}, u32[]{:S(2)}) copy-start(f32[2,1,1,2048]{3,2,0,1:T(1,128)S(1)} %get-tuple-element.235) | copy-start | bytes 49156
  12.5 6.2 %copy-start.95 = (f32[2,1,1,2048]{3,2,0,1:T(1,128)}, f32[2,1,1,2048]{3,2,0,1:T(1,128)S(1)}, u32[]{:S(2)}) copy-start(f32[2,1,1,2048]{3,2,0,1:T(1,128)S(1)} %get-tuple-element.236) | copy-start | bytes 49156
  12.5 6.8 %copy-start.96 = (f32[2,1,1,2048]{3,2,0,1:T(1,128)}, f32[2,1,1,2048]{3,2,0,1:T(1,128)S(1)}, u32[]{:S(2)}) copy-start(f32[2,1,1,2048]{3,2,0,1:T(1,128)S(1)} %get-tuple-element.237) | copy-start | bytes 49156
  12.6 6.8 %copy-start.97 = (f32[2,1,1,2048]{3,2,0,1:T(1,128)}, f32[2,1,1,2048]{3,2,0,1:T(1,128)S(1)}, u32[]{:S(2)}) copy-start(f32[2,1,1,2048]{3,2,0,1:T(1,128)S(1)} %get-tuple-element.238) | copy-start | bytes 49156
  12.6 7.4 %copy-start.98 = (f32[2,1,1,2048]{3,2,0,1:T(1,128)}, f32[2,1,1,2048]{3,2,0,1:T(1,128)S(1)}, u32[]{:S(2)}) copy-start(f32[2,1,1,2048]{3,2,0,1:T(1,128)S(1)} %get-tuple-element.239) | copy-start | bytes 49156
  12.6 7.4 %copy-start.99 = (f32[2,1,1,2048]{3,2,0,1:T(1,128)}, f32[2,1,1,2048]{3,2,0,1:T(1,128)S(1)}, u32[]{:S(2)}) copy-start(f32[2,1,1,2048]{3,2,0,1:T(1,128)S(1)} %get-tuple-element.240) | copy-start | bytes 49156
  12.9 7.7 %copy-start.103 = (f32[2,1,1,2048]{3,2,0,1:T(1,128)}, f32[2,1,1,2048]{3,2,0,1:T(1,128)S(1)}, u32[]{:S(2)}) copy-start(f32[2,1,1,2048]{3,2,0,1:T(1,128)S(1)} %get-tuple-element.213) | copy-start | bytes 49156
  12.9 7.7 %copy-start.104 = (f32[2,1,1,2048]{3,2,0,1:T(1,128)}, f32[2,1,1,2048]{3,2,0,1:T(1,128)S(1)}, u32[]{:S(2)}) copy-start(f32[2,1,1,2048]{3,2,0,1:T(1,128)S(1)} %get-tuple-element.214) | copy-start | bytes 49156
  12.9 8.3 %copy-start.105 = (f32[2,1,1,2048]{3,2,0,1:T(1,128)}, f32[2,1,1,2048]{3,2,0,1:T(1,128)S(1)}, u32[]{:S(2)}) copy-start(f32[2,1,1,2048]{3,2,0,1:T(1,128)S(1)} %get-tuple-element.215) | copy-start | bytes 49156
  12.9 8.3 %copy-start.106 = (f32[2,1,1,2048]{3,2,0,1:T(1,128)}, f32[2,1,1,2048]{3,2,0,1:T(1,128)S(1)}, u32[]{:S(2)}) copy-start(f32[2,1,1,2048]{3,2,0,1:T(1,128)S(1)} %get-tuple-element.216) | copy-start | bytes 49156
  12.9 8.9 %copy-start.107 = (f32[2,1,1,2048]{3,2,0,1:T(1,128)}, f32[2,1,1,2048]{3,2,0,1:T(1,128)S(1)}, u32[]{:S(2)}) copy-start(f32[2,1,1,2048]{3,2,0,1:T(1,128)S(1)} %get-tuple-element.217) | copy-start | bytes 49156
  12.9 8.9 %copy-start.108 = (f32[2,1,1,2048]{3,2,0,1:T(1,128)}, f32[2,1,1,2048]{3,2,0,1:T(1,128)S(1)}, u32[]{:S(2)}) copy-start(f32[2,1,1,2048]{3,2,0,1:T(1,128)S(1)} %get-tuple-element.218) | copy-start | bytes 49156
  13.0 9.5 %copy-start.109 = (f32[2,1,1,2048]{3,2,0,1:T(1,128)}, f32[2,1,1,2048]{3,2,0,1:T(1,128)S(1)}, u32[]{:S(2)}) copy-start(f32[2,1,1,2048]{3,2,0,1:T(1,128)S(1)} %get-tuple-element.219) | copy-start | bytes 49156
  13.0 9.5 %copy-start.110 = (f32[2,1,1,2048]{3,2,0,1:T(1,128)}, f32[2,1,1,2048]{3,2,0,1:T(1,128)S(1)}, u32[]{:S(2)}) copy-start(f32[2,1,1,2048]{3,2,0,1:T(1,128)S(1)} %get-tuple-element.220) | copy-start | bytes 49156
  13.0 10.1 %copy-start.111 = (f32[2,1,1,2048]{3,2,0,1:T(1,128)}, f32[2,1,1,2048]{3,2,0,1:T(1,128)S(1)}, u32[]{:S(2)}) copy-start(f32[2,1,1,2048]{3,2,0,1:T(1,128)S(1)} %get-tuple-element.221) | copy-start | bytes 49156
  13.0 10.1 %copy-start.112 = (f32[2,1,1,2048]{3,2,0,1:T(1,128)}, f32[2,1,1,2048]{3,2,0,1:T(1,128)S(1)}, u32[]{:S(2)}) copy-start(f32[2,1,1,2048]{3,2,0,1:T(1,128)S(1)} %get-tuple-element.222) | copy-start | bytes 49156
  13.0 10.7 %copy-start.113 = (f32[2,1,1,2048]{3,2,0,1:T(1,128)}, f32[2,1,1,2048]{3,2,0,1:T(1,128)S(1)}, u32[]{:S(2)}) copy-start(f32[2,1,1,2048]{3,2,0,1:T(1,128)S(1)} %get-tuple-element.223) | copy-start | bytes 49156
  13.0 10.7 %copy-start.114 = (f32[2,1,1,2048]{3,2,0,1:T(1,128)}, f32[2,1,1,2048]{3,2,0,1:T(1,128)S(1)}, u32[]{:S(2)}) copy-start(f32[2,1,1,2048]{3,2,0,1:T(1,128)S(1)} %get-tuple-element.224) | copy-start | bytes 49156
  13.0 11.4 %copy-start.115 = (f32[2,1,1,2048]{3,2,0,1:T(1,128)}, f32[2,1,1,2048]{3,2,0,1:T(1,128)S(1)}, u32[]{:S(2)}) copy-start(f32[2,1,1,2048]{3,2,0,1:T(1,128)S(1)} %get-tuple-element.225) | copy-start | bytes 49156
  13.0 11.3 %copy-start.116 = (f32[2,1,1,2048]{3,2,0,1:T(1,128)}, f32[2,1,1,2048]{3,2,0,1:T(1,128)S(1)}, u32[]{:S(2)}) copy-start(f32[2,1,1,2048]{3,2,0,1:T(1,128)S(1)} %get-tuple-element.226) | copy-start | bytes 49156
  13.0 12.0 %copy-start.117 = (f32[2,1,1,2048]{3,2,0,1:T(1,128)}, f32[2,1,1,2048]{3,2,0,1:T(1,128)S(1)}, u32[]{:S(2)}) copy-start(f32[2,1,1,2048]{3,2,0,1:T(1,128)S(1)} %get-tuple-element.227) | copy-start | bytes 49156
  13.0 11.9 %copy-start.118 = (f32[2,1,1,2048]{3,2,0,1:T(1,128)}, f32[2,1,1,2048]{3,2,0,1:T(1,128)S(1)}, u32[]{:S(2)}) copy-start(f32[2,1,1,2048]{3,2,0,1:T(1,128)S(1)} %get-tuple-element.228) | copy-start | bytes 49156
  13.1 12.6 %copy-start.119 = (f32[2,1,1,2048]{3,2,0,1:T(1,128)}, f32[2,1,1,2048]{3,2,0,1:T(1,128)S(1)}, u32[]{:S(2)}) copy-start(f32[2,1,1,2048]{3,2,0,1:T(1,128)S(1)} %get-tuple-element.229) | copy-start | bytes 49156
  13.1 12.6 %copy-start.120 = (f32[2,1,1,2048]{3,2,0,1:T(1,128)}, f32[2,1,1,2048]{3,2,0,1:T(1,128)S(1)}, u32[]{:S(2)}) copy-start(f32[2,1,1,2048]{3,2,0,1:T(1,128)S(1)} %get-tuple-element.230) | copy-start | bytes 49156
  13.1 13.2 %copy-start.102 = (f32[2,1,1,2048]{3,2,0,1:T(1,128)}, f32[2,1,1,2048]{3,2,0,1:T(1,128)S(1)}, u32[]{:S(2)}) copy-start(f32[2,1,1,2048]{3,2,0,1:T(1,128)S(1)} %get-tuple-element.212) | copy-start | bytes 49156
  35.7 5.1 %copy-start.2 = (f32[2,2,32,2048]{3,2,1,0:T(8,128)S(1)}, f32[2,2,32,2048]{3,2,1,0:T(8,128)}, u32[]{:S(2)}) copy-start(f32[2,2,32,2048]{3,2,1,0:T(8,128)} %param.9) | copy-start | bytes 3145732
  35.7 5.1 %copy-start.6 = (f32[2,32,2048]{2,1,0:T(8,128)S(1)}, f32[2,32,2048]{2,1,0:T(8,128)}, u32[]{:S(2)}) copy-start(f32[2,32,2048]{2,1,0:T(8,128)} %param.10) | copy-start | bytes 1572868
  98.4 8.2 %copy-start.11 = (f32[2,1,32,2048]{3,2,0,1:T(8,128)S(1)}, f32[2,1,32,2048]{3,2,0,1:T(8,128)}, u32[]{:S(2)}) copy-start(f32[2,1,32,2048]{3,2,0,1:T(8,128)} %get-tuple-element.206) | copy-start | bytes 1572868
  98.4 8.2 %copy-start.12 = (f32[2,1,32,2048]{3,2,0,1:T(8,128)S(1)}, f32[2,1,32,2048]{3,2,0,1:T(8,128)}, u32[]{:S(2)}) copy-start(f32[2,1,32,2048]{3,2,0,1:T(8,128)} %get-tuple-element.207) | copy-start | bytes 1572868
  106.6 4.4 copy-start.13
  112.7 7.7 %copy-start.7 = (f32[2,32,2048]{2,1,0:T(8,128)S(1)}, f32[2,32,2048]{2,1,0:T(8,128)}, u32[]{:S(2)}) copy-start(f32[2,32,2048]{2,1,0:T(8,128)} %param.10) | copy-start | bytes 1572868
  114.2 27.3 %collective-permute-start.3 = (f32[2,2,32,2048]{3,1,2,0:T(2,128)S(1)}, f32[2,2,32,2048]{3,1,2,0:T(2,128)S(1)}, u32[]{:S(2)}, u32[]{:S(2)}) collective-permute-start(f32[2,2,32,2048]{3,1,2,0:T(2,128)S(1)} %broadcast_multiply_fusion), channel_id=1, source_target_pairs={{1,0},{2,1},{3,2},{4,3},{5,4},{6,5},{7,6},{8,7},{9,8},{10,9},{11,1... | collective-permute-start | bytes 3145736 | tf_op jit(solution)/shard_map/ppermute | solution.py:22
  119.6 27.4 %collective-permute-start.2 = (f32[2,2,32,2048]{3,1,2,0:T(2,128)S(1)}, f32[2,2,32,2048]{3,1,2,0:T(2,128)S(1)}, u32[]{:S(2)}, u32[]{:S(2)}) collective-permute-start(f32[2,2,32,2048]{3,1,2,0:T(2,128)S(1)} %broadcast_multiply_fusion), channel_id=1, source_target_pairs={{0,1},{1,2},{2,3},{3,4},{4,5},{5,6},{6,7},{7,8},{8,9},{9,10},{10,1... | collective-permute-start | bytes 3145736 | tf_op jit(solution)/shard_map/ppermute | solution.py:20
  204.6 8.4 %copy-start.9 = (f32[2,1,32,2048]{3,2,0,1:T(8,128)S(1)}, f32[2,1,32,2048]{3,2,0,1:T(8,128)}, u32[]{:S(2)}) copy-start(f32[2,1,32,2048]{3,2,0,1:T(8,128)} %get-tuple-element.204) | copy-start | bytes 1572868
  204.6 8.4 %copy-start.10 = (f32[2,1,32,2048]{3,2,0,1:T(8,128)S(1)}, f32[2,1,32,2048]{3,2,0,1:T(8,128)}, u32[]{:S(2)}) copy-start(f32[2,1,32,2048]{3,2,0,1:T(8,128)} %get-tuple-element.205) | copy-start | bytes 1572868
  219.9 14.1 %copy-start.3 = (f32[2,2,32,2048]{3,2,1,0:T(8,128)S(1)}, f32[2,2,32,2048]{3,2,1,0:T(8,128)}, u32[]{:S(2)}) copy-start(f32[2,2,32,2048]{3,2,1,0:T(8,128)} %param.9) | copy-start | bytes 3145732
  224.0 10.0 %copy-start = (f32[4,2,2,32,2048]{4,3,2,1,0:T(8,128)S(1)}, f32[4,2,2,32,2048]{4,3,2,1,0:T(8,128)}, u32[]{:S(2)}) copy-start(f32[4,2,2,32,2048]{4,3,2,1,0:T(8,128)} %param.15) | copy-start | bytes 12582916
  224.2 9.8 %collective-permute-start.4 = (f32[2,32,2048]{2,1,0:T(8,128)S(1)}, f32[2,32,2048]{2,1,0:T(8,128)S(1)}, u32[]{:S(2)}, u32[]{:S(2)}) collective-permute-start(f32[2,32,2048]{2,1,0:T(8,128)S(1)} %get-tuple-element.208), channel_id=1, source_target_pairs={{112,0},{0,16},{16,32},{32,48},{48,64},{64,80},{80,96},{96,112},{1... | collective-permute-start | bytes 1572872 | tf_op jit(solution)/shard_map/ppermute | solution.py:32
  377.5 13.8 %copy-start.4 = (f32[2,2,32,2048]{3,2,0,1:T(8,128)S(1)}, f32[2,2,32,2048]{3,2,0,1:T(8,128)}, u32[]{:S(2)}) copy-start(f32[2,2,32,2048]{3,2,0,1:T(8,128)} %fusion.4) | copy-start | bytes 3145732
  (78 other events, 220.0 us)
where the time goes:
time: 467 us; the launch traced here: 458 us
  blocking collectives  189 us (40%)
  local copies, waits for them, and re-layouts  142 us (30%)
  other arithmetic  51.6 us (11%)
  waiting for transfers between devices  34.9 us (7%)
  matrix products  25.3 us (5%)
  starting transfers between devices  11.8 us (3%)
    gather x12, local copies, waits for them, and re-layouts, transport(): jnp.take(column_rows, table[:, neighbour], axis=0)  99.8 us
    psum x1, blocking collectives, per_device(): second = lax.psum(projections(basis, middle), ('seg', 'col'))  64 us
    psum x1, blocking collectives, per_device(): squares = lax.psum(jnp.sum(ortho * ortho), ('seg', 'col'))  62.4 us
    psum x1, blocking collectives, per_device(): first = lax.psum(projections(basis, residual), ('seg', 'col'))  62.3 us
    dot_general x2, matrix products, combine(): jnp.einsum('m,msjlc->sjlc', weights, basis, precision=lax.Precision.HIGHEST)  25.3 us
    ppermute x2, waiting for transfers between devices, extended_2(): lax.ppermute(head, axis, [((i + 1) % count, i) for i in range(count)])  19.5 us
    transpose x2, other arithmetic, transport(): total.reshape(width, segs * tracers * levels)  15.3 us
    mul x13, local copies, waits for them, and re-layouts, transport(): term = mixing_rows[neighbour][:, :, None, :] * picked  12 us
  transfers between devices with their start and end apart: 5, of which 3 were waited for; matrix products, arithmetic and copies ran while one was open for 8% of the time, Pallas kernels for 0%

commit v1 on v0

v1 whole, which is shorter than its diff:
```python
import functools

import jax
import jax.numpy as jnp
from jax import lax
from jax.experimental import pallas as pl
from jax.experimental.pallas import tpu as pltpu
from jax.sharding import PartitionSpec as P

uptake_rate = 0.6
half_saturation = 0.3
remin_rate = 0.2
dissolved_share = 0.7
epsilon = 1e-06

SEGS = 2
TRACERS = 2
LEV = 32
NBR = 6
BASIS = 4
WIDTH = 2048
HALO = 512
LANE = 128
TILE = 256
BLOCKS = WIDTH // TILE
GROUPS = WIDTH // HALO
CHUNKS = HALO // LANE
ROWS = SEGS * TRACERS * LEV
GROUP_ROWS = TRACERS * CHUNKS * SEGS * LEV
VMEM = pl.BlockSpec(memory_space=pltpu.VMEM)
PARAMS = pltpu.CompilerParams(vmem_limit_bytes=56 * 1024 * 1024)
f32 = jnp.float32
bf16 = jnp.bfloat16


def shape(*dims):
    return jax.ShapeDtypeStruct(dims, f32)


def group_row(tracer, chunk, seg):
    return ((tracer * CHUNKS + chunk) * SEGS + seg) * LEV


def natural_reader(ref):
    def read(seg, tracer, start):
        return ref[seg, tracer, :, pl.ds(start, TILE)]

    return read


def group_reader(refs):
    def read(seg, tracer, start):
        ref, place = refs[start // HALO]
        chunk = start % HALO // LANE
        parts = [ref[place, pl.ds(group_row(tracer, chunk + h, seg), LEV), :] for h in range(TILE // LANE)]
        return jnp.concatenate(parts, axis=1)

    return read


def split_tile(read, start, xs_ref, place):
    for seg in range(SEGS):
        for tracer in range(TRACERS):
            value = read(seg, tracer, start)
            high = value.astype(bf16)
            low = (value - high.astype(f32)).astype(bf16)
            row = (seg * TRACERS + tracer) * LEV
            xs_ref[place, pl.ds(row, LEV), :] = high
            xs_ref[place, pl.ds(ROWS + row, LEV), :] = low


def picked(xs_ref, places, offsets, index):
    total = None
    depth = lax.broadcasted_iota(jnp.int32, (TILE, TILE), 0)
    for place, offset in zip(places, offsets):
        chosen = jnp.where(depth == index - offset, f32(1), f32(0)).astype(bf16)
        part = jnp.dot(xs_ref[place], chosen, preferred_element_type=f32)
        total = part if total is None else total + part
    return total[:ROWS] + total[ROWS:]


def moved_part(xs_ref, places, offsets, index_of, mixing_of):
    total = [None] * (SEGS * TRACERS)
    for k in range(1, NBR):
        value = picked(xs_ref, places, offsets, index_of(k))
        for seg in range(SEGS):
            mix = mixing_of(seg, k)
            for tracer in range(TRACERS):
                at = seg * TRACERS + tracer
                term = mix * value[at * LEV : (at + 1) * LEV]
                total[at] = term if total[at] is None else total[at] + term
    return total


def factorize(kappa_ref, wet_ref, by_rows_ref, inverse_ref, carry_ref, ratio_ref):
    for group in range(GROUPS):
        for chunk in range(CHUNKS):
            for seg in range(SEGS):
                lanes = pl.ds(group * HALO + chunk * LANE, LANE)
                row = (group * CHUNKS * SEGS + chunk * SEGS + seg) * LEV
                by_rows_ref[pl.ds(row, LEV), :] = kappa_ref[seg, :, lanes]
    wet = []
    for group in range(GROUPS):
        rows = []
        for chunk in range(CHUNKS):
            one = wet_ref[pl.ds(group * CHUNKS + chunk, 1), :]
            rows += [one] * SEGS
        wet.append(jnp.concatenate(rows, axis=0))
    zero = jnp.zeros((CHUNKS * SEGS, LANE), f32)

    def upper_at(group, level):
        if level == 0 or level == LEV:
            return zero
        rows = pl.ds(group * CHUNKS * SEGS * LEV + level, CHUNKS * SEGS, stride=LEV)
        return jnp.where(wet[group] > level, by_rows_ref[rows, :], 0.0)

    upper = [upper_at(group, 0) for group in range(GROUPS)]
    ratio = [zero] * GROUPS
    for level in range(LEV):
        for group in range(GROUPS):
            lower = upper_at(group, level + 1)
            pivot = (1.0 + upper[group] + lower) + upper[group] * ratio[group]
            inverse = 1.0 / pivot
            ratio[group] = -lower * inverse
            inverse_ref[group, level] = jnp.where(wet[group] > level, inverse, 0.0)
            carry_ref[group, level] = upper[group] * inverse
            ratio_ref[group, level] = ratio[group]
            upper[group] = lower


def solve(source_ref, place, inverse_ref, carry_ref, ratio_ref, group, out):
    step = CHUNKS * SEGS

    def source(tracer, level):
        return source_ref[place, pl.ds(group_row(tracer, 0, 0) + level, step, stride=LEV), :]

    value = [[None] * LEV for _ in range(TRACERS)]
    for level in range(LEV):
        inverse = inverse_ref[group, level]
        carry = carry_ref[group, level]
        for tracer in range(TRACERS):
            here = source(tracer, level) * inverse
            if level:
                here = here + carry * value[tracer][level - 1]
            value[tracer][level] = here
    for level in range(LEV - 1, -1, -1):
        ratio = ratio_ref[group, level]
        for tracer in range(TRACERS):
            if level < LEV - 1:
                value[tracer][level] = value[tracer][level] - ratio * value[tracer][level + 1]
            out(tracer, level, value[tracer][level])


def into_group(ref, place):
    def write(tracer, level, value):
        ref[place, pl.ds(group_row(tracer, 0, 0) + level, CHUNKS * SEGS, stride=LEV), :] = value

    return write


def own_part(read, read_moving, table_ref, mixing_ref, light_ref, xs_ref, acc_ref):
    for tile in range(BLOCKS):
        split_tile(read, tile * TILE, xs_ref, tile)

    def finish(block, start, total):
        for seg in range(SEGS):
            columns = pl.ds(start, TILE)
            phosphate = read_moving(seg, 0, block, start)
            organic = read_moving(seg, 1, block, start)
            squared = phosphate * phosphate
            uptake = uptake_rate * light_ref[seg, :, columns] * squared / (squared + half_saturation)
            gains = (remin_rate * organic - uptake, dissolved_share * uptake - remin_rate * organic)
            own = mixing_ref[seg, 0, :, columns]
            for tracer, value in enumerate((phosphate, organic)):
                result = own * value + total[seg * TRACERS + tracer] + gains[tracer]
                for h in range(TILE // LANE):
                    row = group_row(tracer, block % 2 * 2 + h, seg)
                    acc_ref[block // 2, pl.ds(row, LEV), :] = result[:, h * LANE : (h + 1) * LANE]

    for block in range(BLOCKS):
        start = block * TILE
        tiles = list(range(max(0, block - 2), min(BLOCKS, block + 3)))
        total = moved_part(
            xs_ref,
            tiles,
            [tile * TILE for tile in tiles],
            lambda k: table_ref[pl.ds(k, 1), pl.ds(start, TILE)],
            lambda seg, k: mixing_ref[seg, k, :, pl.ds(start, TILE)],
        )
        finish(block, start, total)


def first_own_kernel(
    state_ref, table_ref, mixing_ref, light_ref, kappa_ref, wet_ref,
    edge_ref, middle_ref, inverse_ref, carry_ref, ratio_ref,
    xs_ref, acc_ref, by_rows_ref,
):
    read = natural_reader(state_ref)
    factorize(kappa_ref, wet_ref, by_rows_ref, inverse_ref, carry_ref, ratio_ref)
    own_part(read, lambda seg, tracer, block, start: read(seg, tracer, start), table_ref, mixing_ref, light_ref, xs_ref, acc_ref)
    finish_own(edge_ref, middle_ref, inverse_ref, carry_ref, ratio_ref, acc_ref)


def finish_own(edge_ref, middle_ref, inverse_ref, carry_ref, ratio_ref, acc_ref):
    for place, group in enumerate((0, GROUPS - 1)):
        edge_ref[place] = acc_ref[group]
    for group in range(1, GROUPS - 1):
        solve(acc_ref, group, inverse_ref, carry_ref, ratio_ref, group, into_group(middle_ref, group - 1))


def second_own_kernel(
    head_ref, middle_in_ref, tail_ref, table_ref, mixing_ref, light_ref, inverse_ref, carry_ref, ratio_ref,
    edge_ref, middle_ref,
    xs_ref, acc_ref,
):
    refs = [(head_ref, 0)] + [(middle_in_ref, i) for i in range(GROUPS - 2)] + [(tail_ref, 0)]
    read = group_reader(refs)
    own_part(read, lambda seg, tracer, block, start: read(seg, tracer, start), table_ref, mixing_ref, light_ref, xs_ref, acc_ref)
    finish_own(edge_ref, middle_ref, inverse_ref, carry_ref, ratio_ref, acc_ref)


def edge_kernel(
    natural, left_ref, right_ref, table_ref, mixing_ref, edge_in_ref, inverse_ref, carry_ref, ratio_ref,
    head_ref, tail_ref,
    xs_ref, acc_ref,
):
    for side, ref in enumerate((left_ref, right_ref)):
        read = natural_reader(ref) if natural else group_reader([(ref, 0)])
        for tile in range(HALO // TILE):
            split_tile(read, tile * TILE, xs_ref, side * 2 + tile)
    acc_ref[...] = edge_in_ref[...]
    uses = ((0, 0, (0, 1)), (1, 0, (1,)), (BLOCKS - 2, 1, (2,)), (BLOCKS - 1, 1, (2, 3)))
    offsets = (-HALO, -TILE, WIDTH, WIDTH + TILE)
    for block, side, places in uses:
        start = block * TILE
        total = moved_part(
            xs_ref,
            places,
            [offsets[place] for place in places],
            lambda k: table_ref[pl.ds(k, 1), pl.ds(start, TILE)],
            lambda seg, k: mixing_ref[seg, k, :, pl.ds(start, TILE)],
        )
        for seg in range(SEGS):
            for tracer in range(TRACERS):
                value = total[seg * TRACERS + tracer]
                for h in range(TILE // LANE):
                    row = pl.ds(group_row(tracer, block % 2 * 2 + h, seg), LEV)
                    acc_ref[side, row, :] += value[:, h * LANE : (h + 1) * LANE]
    for side, (group, ref) in enumerate(((0, head_ref), (GROUPS - 1, tail_ref))):
        solve(acc_ref, side, inverse_ref, carry_ref, ratio_ref, group, into_group(ref, 0))


def first_own(state, table, mixing, light, kappa, wet):
    factors = shape(GROUPS, LEV, CHUNKS * SEGS, LANE)
    return pl.pallas_call(
        first_own_kernel,
        out_shape=(shape(2, GROUP_ROWS, LANE), shape(GROUPS - 2, GROUP_ROWS, LANE), factors, factors, factors),
        in_specs=[VMEM] * 6,
        out_specs=(VMEM,) * 5,
        scratch_shapes=[
            pltpu.VMEM((BLOCKS, 2 * ROWS, TILE), bf16),
            pltpu.VMEM((GROUPS, GROUP_ROWS, LANE), f32),
            pltpu.VMEM((GROUPS * CHUNKS * SEGS * LEV, LANE), f32),
        ],
        compiler_params=PARAMS,
        cost_estimate=pl.CostEstimate(flops=6_000_000_000, bytes_accessed=10_000_000, transcendentals=0),
        name="first_step_own",
    )(state, table, mixing, light, kappa, wet)


def second_own(head, middle, tail, table, mixing, light, factors):
    return pl.pallas_call(
        second_own_kernel,
        out_shape=(shape(2, GROUP_ROWS, LANE), shape(GROUPS - 2, GROUP_ROWS, LANE)),
        in_specs=[VMEM] * 9,
        out_specs=(VMEM,) * 2,
        scratch_shapes=[
            pltpu.VMEM((BLOCKS, 2 * ROWS, TILE), bf16),
            pltpu.VMEM((GROUPS, GROUP_ROWS, LANE), f32),
        ],
        compiler_params=PARAMS,
        cost_estimate=pl.CostEstimate(flops=6_000_000_000, bytes_accessed=10_000_000, transcendentals=0),
        name="second_step_own",
    )(head, middle, tail, table, mixing, light, *factors)


def edges(natural, left, right, table, mixing, edge, factors):
    return pl.pallas_call(
        functools.partial(edge_kernel, natural),
        out_shape=(shape(1, GROUP_ROWS, LANE), shape(1, GROUP_ROWS, LANE)),
        in_specs=[VMEM] * 8,
        out_specs=(VMEM,) * 2,
        scratch_shapes=[
            pltpu.VMEM((4, 2 * ROWS, TILE), bf16),
            pltpu.VMEM((2, GROUP_ROWS, LANE), f32),
        ],
        compiler_params=PARAMS,
        cost_estimate=pl.CostEstimate(flops=1_000_000_000, bytes_accessed=8_000_000, transcendentals=0),
        name="first_step_edges" if natural else "second_step_edges",
    )(left, right, table, mixing, edge, *factors)


def residual_kernel(state_ref, wet_ref, basis_ref, head_ref, middle_ref, tail_ref, came_ref, residual_ref, sums_ref):
    pairs = [(i, j) for i in range(BASIS) for j in range(i, BASIS)]
    sums = [jnp.zeros((8, LANE), f32) for _ in range(BASIS + 1 + len(pairs))]
    refs = [(head_ref, 0)] + [(middle_ref, i) for i in range(GROUPS - 2)] + [(tail_ref, 0)]
    level = lax.broadcasted_iota(jnp.int32, (8, LANE), 0)
    for group in range(GROUPS):
        ref, place = refs[group]
        for chunk in range(CHUNKS):
            lanes = pl.ds(group * HALO + chunk * LANE, LANE)
            wet = jnp.broadcast_to(wet_ref[pl.ds(group * CHUNKS + chunk, 1), :], (8, LANE))
            for seg in range(SEGS):
                for tracer in range(TRACERS):
                    for part in range(LEV // 8):
                        rows = pl.ds(part * 8, 8)
                        if seg:
                            before = ref[place, pl.ds(group_row(tracer, chunk, seg - 1) + part * 8, 8), :]
                        else:
                            before = came_ref[group, pl.ds((tracer * CHUNKS + chunk) * LEV + part * 8, 8), :]
                        own = state_ref[seg, tracer, rows, lanes]
                        here = jnp.where(wet > level + part * 8, own - before, 0.0)
                        residual_ref[seg, tracer, rows, lanes] = here
                        vectors = [basis_ref[i, seg, tracer, rows, lanes] for i in range(BASIS)]
                        for i in range(BASIS):
                            sums[i] = sums[i] + vectors[i] * here
                        sums[BASIS] = sums[BASIS] + here * here
                        for at, (i, j) in enumerate(pairs):
                            sums[BASIS + 1 + at] = sums[BASIS + 1 + at] + vectors[i] * vectors[j]
    rows = [jnp.sum(one, axis=0, keepdims=True) for one in sums]
    rows.append(jnp.zeros((16 - len(rows), LANE), f32))
    sums_ref[...] = jnp.concatenate(rows, axis=0)


def residuals(state, wet, basis, head, middle, tail, came):
    return pl.pallas_call(
        residual_kernel,
        out_shape=(shape(SEGS, TRACERS, LEV, WIDTH), shape(16, LANE)),
        in_specs=[VMEM] * 7,
        out_specs=(VMEM,) * 2,
        compiler_params=PARAMS,
        name="residual_and_products",
    )(state, wet, basis, head, middle, tail, came)


def scaled_kernel(count, residual_ref, basis_ref, sums_ref, new_ref, coefficients_ref):
    sums = jnp.sum(sums_ref[...], axis=1, keepdims=True)
    one = [sums[i : i + 1] for i in range(16)]
    first, square, products = one[:BASIS], one[BASIS], iter(one[BASIS + 1 :])
    gram = [[None] * BASIS for _ in range(BASIS)]
    for i in range(BASIS):
        for j in range(i, BASIS):
            gram[i][j] = gram[j][i] = next(products)
    second = [first[i] - sum(gram[i][j] * first[j] for j in range(BASIS)) for i in range(BASIS)]
    both = [first[i] + second[i] for i in range(BASIS)]
    for i in range(BASIS):
        square = square - both[i] * (2.0 * first[i] - sum(gram[i][j] * both[j] for j in range(BASIS)))
    spread = jnp.sqrt(square / count + epsilon)
    lane = lax.broadcasted_iota(jnp.int32, (8, LANE), 1)
    result = jnp.zeros((8, LANE), f32)
    for i, value in enumerate(both + [spread]):
        result = jnp.where(lane == i, value, result)
    coefficients_ref[...] = result
    scale = 1.0 / spread
    weights = [jnp.broadcast_to(-value * scale, (LEV, LANE)) for value in both]
    scale = jnp.broadcast_to(scale, (LEV, LANE))
    for seg in range(SEGS):
        for tracer in range(TRACERS):
            for chunk in range(CHUNKS):
                lanes = pl.ds(chunk * LANE, LANE)
                total = residual_ref[seg, tracer, :, lanes] * scale
                for i in range(BASIS):
                    total = total + weights[i] * basis_ref[i, seg, tracer, :, lanes]
                new_ref[seg, tracer, :, lanes] = total


def scaled(count, residual, basis, sums):
    block = pl.BlockSpec((SEGS, TRACERS, LEV, HALO), lambda g: (0, 0, 0, g))
    return pl.pallas_call(
        functools.partial(scaled_kernel, count),
        grid=(GROUPS,),
        out_shape=(shape(SEGS, TRACERS, LEV, WIDTH), shape(8, LANE)),
        in_specs=[
            block,
            pl.BlockSpec((BASIS, SEGS, TRACERS, LEV, HALO), lambda g: (0, 0, 0, 0, g)),
            pl.BlockSpec((16, LANE), lambda g: (0, 0)),
        ],
        out_specs=(block, pl.BlockSpec((8, LANE), lambda g: (0, 0))),
        compiler_params=PARAMS,
        name="orthogonal_and_scaled",
    )(residual, basis, sums)


def shifted(block, axis, distance):
    count = lax.axis_size(axis)
    return lax.ppermute(block, axis, [(i, (i + distance) % count) for i in range(count)])


def summed_everywhere(value):
    for axis in ("seg", "col"):
        count = lax.axis_size(axis)
        done = 1
        while done < count:
            flip = done if done in (1, 2, 4, 8) else done
            value = value + lax.ppermute(value, axis, [(i, i ^ FLIPS[axis][flip]) for i in range(count)])
            done *= 2
    return value


FLIPS = {"seg": {1: 1, 2: 2, 4: 6}, "col": {1: 1, 2: 3, 4: 4, 8: 12}}


def sent_segment(groups):
    count = groups.shape[0]
    parts = groups.reshape(count, TRACERS * CHUNKS, SEGS, LEV, LANE)[:, :, SEGS - 1]
    return parts.reshape(count, TRACERS * CHUNKS * LEV, LANE)


def per_device(segment_state, light, mixing, kappa, neighbour_columns, wet_levels, basis):
    start = lax.axis_index("col") * WIDTH
    every_column = lax.axis_size("col") * WIDTH
    left = shifted(segment_state[..., WIDTH - HALO :], "col", 1)
    right = shifted(segment_state[..., :HALO], "col", -1)
    table = (neighbour_columns.T - start + HALO + every_column) % every_column - HALO
    table = jnp.concatenate([table, jnp.zeros((8 - NBR, WIDTH), jnp.int32)], axis=0)
    wet = wet_levels.reshape(WIDTH // LANE, LANE)
    edge, middle, *factors = first_own(segment_state, table, mixing, light, kappa, wet)
    head, tail = edges(True, left, right, table, mixing, edge, factors)
    left = shifted(tail, "col", 1)
    right = shifted(head, "col", -1)
    edge, middle = second_own(head, middle, tail, table, mixing, light, factors)
    head, tail = edges(False, left, right, table, mixing, edge, factors)
    came = shifted(jnp.concatenate([sent_segment(head), sent_segment(middle), sent_segment(tail)]), "seg", 1)
    residual, sums = residuals(segment_state, wet, basis, head, middle, tail, came)
    count = lax.axis_size("seg") * SEGS * TRACERS * LEV * every_column
    new_vector, coefficients = scaled(count, residual, basis, summed_everywhere(sums))
    return (residual, new_vector, coefficients[0, : BASIS + 1])


def solution(mesh):
    return jax.shard_map(
        per_device,
        mesh=mesh,
        in_specs=(
            P("seg", None, None, "col"),
            P("seg", None, "col"),
            P("seg", None, None, "col"),
            P("seg", None, "col"),
            P("col", None),
            P("col"),
            P(None, "seg", None, None, "col"),
        ),
        out_specs=(P("seg", None, None, "col"), P("seg", None, None, "col"), P()),
        check_vma=False,
    )
```

time: 467 us -> 102 us (0.22); the launches traced: 458 us -> 101 us
  blocking collectives: 189 us -> 0 us
  local copies, waits for them, and re-layouts: 142 us -> 8.04 us
  other arithmetic: 51.6 us -> 2.23 us
  Pallas kernels: 0 us -> 41.9 us
  matrix products: 25.3 us -> 0 us
    psum x3 -> x0, blocking collectives: 189 us -> none  [the longest x1 64 us: per_device(): second = lax.psum(projections(basis, middle), ('seg', 'col'))]
    gather x12 -> x0, local copies, waits for them, and re-layouts: 99.8 us -> none  [transport(): jnp.take(column_rows, table[:, neighbour], axis=0)]
    pallas_call x0 -> x6, Pallas kernels: none -> 41.9 us  [the longest x1 11.2 us: first_own(): pl.pallas_call(first_own_kernel, out_shape=(shape(2, GROUP_ROWS, LANE), s...]
    dot_general x2 -> x0, matrix products: 25.3 us -> none  [combine(): jnp.einsum('m,msjlc->sjlc', weights, basis, precision=lax.Precision.HIGHEST)]
    mul x28 -> x0, local copies, waits for them, and re-layouts: 21.3 us -> none  [the longest x13 12 us: transport(): term = mixing_rows[neighbour][:, :, None, :] * picked]
    transpose x2 -> x0, other arithmetic: 15.3 us -> none  [transport(): total.reshape(width, segs * tracers * levels)]
    mul x5 -> x0, other arithmetic: 5.96 us -> none  [the longest x1 3.52 us: vertical_solve(): value = (source[..., layer, :] + upper[..., layer, :] * value) / pivot]
    concatenate x3 -> x1, other arithmetic: 5.97 us -> 0.04 us  [per_device(): jnp.concatenate([sent_segment(head), sent_segment(middle), sent_segment(t...]
  transfers between devices with their start and end apart: 5 -> 12, of which waited for: 3 -> 8; matrix products, arithmetic and copies ran while one was open for 8% -> 2% of each run, Pallas kernels for 0% -> 22%
where the time goes in v1:
time: 102 us; the launch traced here: 101 us
  Pallas kernels  41.9 us (41%)
  waiting for transfers between devices  34.5 us (34%)
  starting transfers between devices  14 us (14%)
  local copies, waits for them, and re-layouts  8.04 us (8%)
  other arithmetic  2.23 us (2%)
    ppermute x7, waiting for transfers between devices, summed_everywhere(): lax.ppermute(value, axis, [(i, i ^ FLIPS[axis][flip]) for i in range(coun...  24.7 us
    ppermute x5, starting transfers between devices, shifted(): lax.ppermute(block, axis, [(i, (i + distance) % count) for i in range(cou...  11.8 us
    pallas_call x1, Pallas kernels, first_own(): pl.pallas_call(first_own_kernel, out_shape=(shape(2, GROUP_ROWS, LANE), s...  11.2 us
    pallas_call x1, Pallas kernels, second_own(): pl.pallas_call(second_own_kernel, out_shape=(shape(2, GROUP_ROWS, LANE),...  10.6 us
    pallas_call x2, Pallas kernels, edges(): pl.pallas_call(functools.partial(edge_kernel, natural), out_shape=(shape(...  10.5 us
    ppermute x5, waiting for transfers between devices, shifted(): lax.ppermute(block, axis, [(i, (i + distance) % count) for i in range(cou...  9.81 us
    pallas_call x1, Pallas kernels, residuals(): pl.pallas_call(residual_kernel, out_shape=(shape(SEGS, TRACERS, LEV, WIDT...  4.95 us
    pallas_call x1, Pallas kernels, scaled(): pl.pallas_call(functools.partial(scaled_kernel, count), grid=(GROUPS,), o...  4.61 us
  transfers between devices with their start and end apart: 12, of which 8 were waited for; matrix products, arithmetic and copies ran while one was open for 2% of the time, Pallas kernels for 22%

profile of v1, /device:TPU:0, one launch (start us, length us, event | category | flops | bytes accessed | tf_op | source)
XLA Modules:
  0.0 101.4 jit_solution(11763079072425892769)
XLA Ops:
  0.6 1.1 %fusion.2 = (f32[2,2,32,512]{3,2,1,0:T(8,128)S(1)}, f32[2,2,32,512]{3,2,1,0:T(8,128)S(1)}) fusion(f32[2,2,32,2048]{3,2,1,0:T(8,128)} %state_ref.3), kind=kLoop, calls=%fused_computation.7 | loop fusion | bytes 1048576 | tf_op jit(solution)/shard_map/slice | solution.py:423
  1.7 2.1 %collective-permute-start = (f32[2,2,32,512]{3,2,1,0:T(8,128)S(1)}, f32[2,2,32,512]{3,2,1,0:T(8,128)S(1)}, u32[]{:S(2)}, u32[]{:S(2)}) collective-permute-start(f32[2,2,32,512]{3,2,1,0:T(8,128)S(1)} %get-tuple-element.34), channel_id=1, source_target_pairs={{0,1},{1,2},{2,3},{3,4},{4,5},{5,6},{6,7},{7,8},{8,9},{9,10},{10,1... | collective-permute-start | bytes 786440 | tf_op jit(solution)/shard_map/ppermute | solution.py:396
  3.8 4.4 %collective-permute-start.1 = (f32[2,2,32,512]{3,2,1,0:T(8,128)S(1)}, f32[2,2,32,512]{3,2,1,0:T(8,128)S(1)}, u32[]{:S(2)}, u32[]{:S(2)}) collective-permute-start(f32[2,2,32,512]{3,2,1,0:T(8,128)S(1)} %get-tuple-element.33), channel_id=1, source_target_pairs={{0,15},{1,0},{2,1},{3,2},{4,3},{5,4},{6,5},{7,6},{8,7},{9,8},{10,9... | collective-permute-start | bytes 786440 | tf_op jit(solution)/shard_map/ppermute | solution.py:396
  8.2 0.9 fusion.1
  9.1 0.6 concatenate.6.table_ref
  9.7 11.2 %first_step_own.1 = (f32[2,512,128]{2,1,0:T(8,128)}, f32[2,512,128]{2,1,0:T(8,128)}, f32[4,32,8,128]{3,2,1,0:T(8,128)}, f32[4,32,8,128]{3,2,1,0:T(8,128)}, f32[4,32,8,128]{3,2,1,0:T(8,128)}) custom-call(f32[2,2,32,2048]{3,2,1,0:T(8,128)} %state_ref.3, s32[8,2048]{1,0:T(8,128)} %concatenate.6.table_ref, f32[2,6,32,2048]{3,2,1,0:T(8,128)} %mixing_ref.7, ...), custom_call_target="tpu_custom_call" | custom-call | flops 6000000000 | bytes 10000000 | tf_op jit(solution)/shard_map/first_step_own/pallas_call | solution.py:255
  20.9 0.0 collective-permute-done.left_ref
  20.9 0.0 copy-start.1
  20.9 0.0 collective-permute-done.1.right_ref
  20.9 0.0 copy-start.2
  20.9 0.7 copy-done.1
  21.6 0.1 copy-done.2
  21.7 5.2 %first_step_edges.1 = (f32[1,512,128]{2,1,0:T(8,128)}, f32[1,512,128]{2,1,0:T(8,128)}) custom-call(f32[2,2,32,512]{3,2,1,0:T(8,128)} %copy-done.1, f32[2,2,32,512]{3,2,1,0:T(8,128)} %copy-done.2, s32[8,2048]{1,0:T(8,128)} %concatenate.6.table_ref, f32[2,6,32,2048]{3,2,1,0:T(8,128)} %mixing_ref.7, f32[2,512,128]{2,1,0:T(8,128)} %get-tuple-element.18.edge_in_ref, ...), custom_call_target="tpu_custom_call" | custom-call | flops 1000000000 | bytes 8000000 | tf_op jit(solution)/shard_map/first_step_edges/pallas_call | solution.py:288
  26.9 0.0 collective-permute-start.2
  26.9 5.3 %collective-permute-start.3 = (f32[1,512,128]{2,1,0:T(8,128)}, f32[1,512,128]{2,1,0:T(8,128)S(1)}, u32[]{:S(2)}, u32[]{:S(2)}) collective-permute-start(f32[1,512,128]{2,1,0:T(8,128)} %get-tuple-element.23.head_ref), channel_id=1, source_target_pairs={{0,15},{1,0},{2,1},{3,2},{4,3},{5,4},{6,5},{7,6},{8,7},{9,8},{10,9... | collective-permute-start | bytes 786440 | tf_op jit(solution)/shard_map/ppermute | solution.py:396
  32.3 10.6 %second_step_own.1 = (f32[2,512,128]{2,1,0:T(8,128)}, f32[2,512,128]{2,1,0:T(8,128)}) custom-call(f32[1,512,128]{2,1,0:T(8,128)} %get-tuple-element.23.head_ref, f32[2,512,128]{2,1,0:T(8,128)} %get-tuple-element.24.middle_in_ref, f32[1,512,128]{2,1,0:T(8,128)} %get-tuple-element.22.tail_ref, s32[8,2048]{1,0:T(8,128)} %concatenate.6.table_ref, ...), custom_call_target="tpu_custom_call" | custom-call | flops 6000000000 | bytes 10000000 | tf_op jit(solution)/shard_map/second_step_own/pallas_call | solution.py:272
  42.9 1.0 slice.25
  43.9 0.0 collective-permute-done.2.left_ref
  43.9 0.0 copy-start.3
  43.9 0.0 collective-permute-done.3.right_ref
  43.9 0.0 copy-start.4
  43.9 0.7 copy-done.3
  44.6 0.1 copy-done.4
  44.7 5.2 %second_step_edges.1 = (f32[1,512,128]{2,1,0:T(8,128)}, f32[1,512,128]{2,1,0:T(8,128)}) custom-call(f32[1,512,128]{2,1,0:T(8,128)} %copy-done.3, f32[1,512,128]{2,1,0:T(8,128)} %copy-done.4, s32[8,2048]{1,0:T(8,128)} %concatenate.6.table_ref, f32[2,6,32,2048]{3,2,1,0:T(8,128)} %mixing_ref.7, f32[2,512,128]{2,1,0:T(8,128)} %get-tuple-element.25.edge_in_ref, ...), custom_call_target="tpu_custom_call" | custom-call | flops 1000000000 | bytes 8000000 | tf_op jit(solution)/shard_map/second_step_edges/pallas_call | solution.py:288
  50.0 0.9 slice.24
  50.9 0.9 slice.26
  51.8 0.0 collective-permute-start.4
  51.9 9.8 %collective-permute-done.4.came_ref = f32[4,256,128]{2,1,0:T(8,128)S(1)} collective-permute-done((f32[4,256,128]{2,1,0:T(8,128)S(1)}, f32[4,256,128]{2,1,0:T(8,128)S(1)}, u32[]{:S(2)}, u32[]{:S(2)}) %collective-permute-start.4) | collective-permute-done | bytes 524320 | tf_op jit(solution)/shard_map/ppermute | solution.py:396
  61.7 0.8 copy-done
  62.5 4.9 %residual_and_products.1 = (f32[2,2,32,2048]{3,2,1,0:T(8,128)}, f32[16,128]{1,0:T(8,128)}) custom-call(f32[2,2,32,2048]{3,2,1,0:T(8,128)} %state_ref.3, s32[16,128]{1,0:T(8,128)} %bitcast.26, f32[4,2,2,32,2048]{4,3,2,1,0:T(8,128)} %basis_ref.3, f32[1,512,128]{2,1,0:T(8,128)} %get-tuple-element.26.head_ref, f32[2,512,128]{2,1,0:T(8,128)} %get-tuple-element.27.middle_ref, ...), custom_call_target="tpu_custom_call" | custom-call | tf_op jit(solution)/shard_map/residual_and_products/pallas_call | solution.py:336
  67.4 0.0 collective-permute-start.5
  67.4 1.4 %collective-permute-done.5 = f32[16,128]{1,0:T(8,128)S(1)} collective-permute-done((f32[16,128]{1,0:T(8,128)}, f32[16,128]{1,0:T(8,128)S(1)}, u32[]{:S(2)}, u32[]{:S(2)}) %collective-permute-start.5) | collective-permute-done | bytes 8224 | tf_op jit(solution)/shard_map/ppermute | solution.py:405
  68.8 0.7 add.46
  69.5 0.4 collective-permute-start.6
  69.9 3.3 %collective-permute-done.6 = f32[16,128]{1,0:T(8,128)S(1)} collective-permute-done((f32[16,128]{1,0:T(8,128)S(1)}, f32[16,128]{1,0:T(8,128)S(1)}, u32[]{:S(2)}, u32[]{:S(2)}) %collective-permute-start.6) | collective-permute-done | bytes 8224 | tf_op jit(solution)/shard_map/ppermute | solution.py:405
  73.2 1.8 %collective-permute-start.7 = (f32[16,128]{1,0:T(8,128)S(1)}, f32[16,128]{1,0:T(8,128)S(1)}, u32[]{:S(2)}, u32[]{:S(2)}) collective-permute-start(f32[16,128]{1,0:T(8,128)S(1)} %add.47), channel_id=1, source_target_pairs={{0,96},{16,112},{32,64},{48,80},{64,32},{80,48},{96,0},{112,16},{1... | collective-permute-start | bytes 24584 | tf_op jit(solution)/shard_map/ppermute | solution.py:405
  75.0 3.0 %collective-permute-done.7 = f32[16,128]{1,0:T(8,128)S(1)} collective-permute-done((f32[16,128]{1,0:T(8,128)S(1)}, f32[16,128]{1,0:T(8,128)S(1)}, u32[]{:S(2)}, u32[]{:S(2)}) %collective-permute-start.7) | collective-permute-done | bytes 8224 | tf_op jit(solution)/shard_map/ppermute | solution.py:405
  78.0 0.0 collective-permute-start.8
  78.0 3.6 %collective-permute-done.8 = f32[16,128]{1,0:T(8,128)S(1)} collective-permute-done((f32[16,128]{1,0:T(8,128)S(1)}, f32[16,128]{1,0:T(8,128)S(1)}, u32[]{:S(2)}, u32[]{:S(2)}) %collective-permute-start.8) | collective-permute-done | bytes 8224 | tf_op jit(solution)/shard_map/ppermute | solution.py:405
  81.7 0.0 collective-permute-start.9
  81.7 4.9 %collective-permute-done.9 = f32[16,128]{1,0:T(8,128)S(1)} collective-permute-done((f32[16,128]{1,0:T(8,128)S(1)}, f32[16,128]{1,0:T(8,128)S(1)}, u32[]{:S(2)}, u32[]{:S(2)}) %collective-permute-start.9) | collective-permute-done | bytes 8224 | tf_op jit(solution)/shard_map/ppermute | solution.py:405
  86.5 0.0 collective-permute-start.10
  86.5 3.6 %collective-permute-done.10 = f32[16,128]{1,0:T(8,128)S(1)} collective-permute-done((f32[16,128]{1,0:T(8,128)S(1)}, f32[16,128]{1,0:T(8,128)S(1)}, u32[]{:S(2)}, u32[]{:S(2)}) %collective-permute-start.10) | collective-permute-done | bytes 8224 | tf_op jit(solution)/shard_map/ppermute | solution.py:405
  90.2 0.0 collective-permute-start.11
  90.2 4.9 %collective-permute-done.11 = f32[16,128]{1,0:T(8,128)S(1)} collective-permute-done((f32[16,128]{1,0:T(8,128)S(1)}, f32[16,128]{1,0:T(8,128)S(1)}, u32[]{:S(2)}, u32[]{:S(2)}) %collective-permute-start.11) | collective-permute-done | bytes 8224 | tf_op jit(solution)/shard_map/ppermute | solution.py:405
  95.1 0.6 add.52.sums_ref
  95.7 4.6 %orthogonal_and_scaled.1 = (f32[2,2,32,2048]{3,2,1,0:T(8,128)}, f32[8,128]{1,0:T(8,128)}) custom-call(f32[2,2,32,2048]{3,2,1,0:T(8,128)} %get-tuple-element.15.residual_ref, f32[4,2,2,32,2048]{4,3,2,1,0:T(8,128)} %basis_ref.3, f32[16,128]{1,0:T(8,128)} %add.52.sums_ref), custom_call_target="tpu_custom_call" | custom-call | tf_op jit(solution)/shard_map/orthogonal_and_scaled/pallas_call | solution.py:379
  100.3 1.2 %slice_bitcast_fusion = f32[5]{0:T(128)} fusion(f32[8,128]{1,0:T(8,128)} %get-tuple-element.32), kind=kLoop, calls=%fused_computation.6 | loop fusion | bytes 40 | tf_op jit(solution)/shard_map/squeeze | solution.py:437
  (7 shorter events, 0.1 us)
Async XLA Ops:
  1.7 19.2 %collective-permute-start = (f32[2,2,32,512]{3,2,1,0:T(8,128)S(1)}, f32[2,2,32,512]{3,2,1,0:T(8,128)S(1)}, u32[]{:S(2)}, u32[]{:S(2)}) collective-permute-start(f32[2,2,32,512]{3,2,1,0:T(8,128)S(1)} %get-tuple-element.34), channel_id=1, source_target_pairs={{0,1},{1,2},{2,3},{3,4},{4,5},{5,6},{6,7},{7,8},{8,9},{9,10},{10,1... | collective-permute-start | bytes 786440 | tf_op jit(solution)/shard_map/ppermute | solution.py:396
  3.8 17.1 %collective-permute-start.1 = (f32[2,2,32,512]{3,2,1,0:T(8,128)S(1)}, f32[2,2,32,512]{3,2,1,0:T(8,128)S(1)}, u32[]{:S(2)}, u32[]{:S(2)}) collective-permute-start(f32[2,2,32,512]{3,2,1,0:T(8,128)S(1)} %get-tuple-element.33), channel_id=1, source_target_pairs={{0,15},{1,0},{2,1},{3,2},{4,3},{5,4},{6,5},{7,6},{8,7},{9,8},{10,9... | collective-permute-start | bytes 786440 | tf_op jit(solution)/shard_map/ppermute | solution.py:396
  20.9 0.7 copy-start.1
  20.9 0.8 copy-start.2
  26.9 17.0 %collective-permute-start.2 = (f32[1,512,128]{2,1,0:T(8,128)}, f32[1,512,128]{2,1,0:T(8,128)S(1)}, u32[]{:S(2)}, u32[]{:S(2)}) collective-permute-start(f32[1,512,128]{2,1,0:T(8,128)} %get-tuple-element.22.tail_ref), channel_id=1, source_target_pairs={{0,1},{1,2},{2,3},{3,4},{4,5},{5,6},{6,7},{7,8},{8,9},{9,10},{10,1... | collective-permute-start | bytes 786440 | tf_op jit(solution)/shard_map/ppermute | solution.py:396
  26.9 17.0 %collective-permute-start.3 = (f32[1,512,128]{2,1,0:T(8,128)}, f32[1,512,128]{2,1,0:T(8,128)S(1)}, u32[]{:S(2)}, u32[]{:S(2)}) collective-permute-start(f32[1,512,128]{2,1,0:T(8,128)} %get-tuple-element.23.head_ref), channel_id=1, source_target_pairs={{0,15},{1,0},{2,1},{3,2},{4,3},{5,4},{6,5},{7,6},{8,7},{9,8},{10,9... | collective-permute-start | bytes 786440 | tf_op jit(solution)/shard_map/ppermute | solution.py:396
  43.9 0.7 copy-start.3
  43.9 0.8 copy-start.4
  51.8 9.8 %collective-permute-start.4 = (f32[4,256,128]{2,1,0:T(8,128)S(1)}, f32[4,256,128]{2,1,0:T(8,128)S(1)}, u32[]{:S(2)}, u32[]{:S(2)}) collective-permute-start(f32[4,256,128]{2,1,0:T(8,128)S(1)} %pad_maximum_fusion), channel_id=1, source_target_pairs={{0,16},{16,32},{32,48},{48,64},{64,80},{80,96},{96,112},{112,0},{1... | collective-permute-start | bytes 1572872 | tf_op jit(solution)/shard_map/ppermute | solution.py:396
  61.7 0.8 copy-start
  67.4 1.4 %collective-permute-start.5 = (f32[16,128]{1,0:T(8,128)}, f32[16,128]{1,0:T(8,128)S(1)}, u32[]{:S(2)}, u32[]{:S(2)}) collective-permute-start(f32[16,128]{1,0:T(8,128)} %get-tuple-element.30), channel_id=1, source_target_pairs={{0,16},{16,0},{32,48},{48,32},{64,80},{80,64},{96,112},{112,96},{1... | collective-permute-start | bytes 24584 | tf_op jit(solution)/shard_map/ppermute | solution.py:405
  69.5 3.7 %collective-permute-start.6 = (f32[16,128]{1,0:T(8,128)S(1)}, f32[16,128]{1,0:T(8,128)S(1)}, u32[]{:S(2)}, u32[]{:S(2)}) collective-permute-start(f32[16,128]{1,0:T(8,128)S(1)} %add.46), channel_id=1, source_target_pairs={{0,32},{16,48},{32,0},{48,16},{64,96},{80,112},{96,64},{112,80},{1... | collective-permute-start | bytes 24584 | tf_op jit(solution)/shard_map/ppermute | solution.py:405
  73.2 4.9 %collective-permute-start.7 = (f32[16,128]{1,0:T(8,128)S(1)}, f32[16,128]{1,0:T(8,128)S(1)}, u32[]{:S(2)}, u32[]{:S(2)}) collective-permute-start(f32[16,128]{1,0:T(8,128)S(1)} %add.47), channel_id=1, source_target_pairs={{0,96},{16,112},{32,64},{48,80},{64,32},{80,48},{96,0},{112,16},{1... | collective-permute-start | bytes 24584 | tf_op jit(solution)/shard_map/ppermute | solution.py:405
  78.0 3.7 %collective-permute-start.8 = (f32[16,128]{1,0:T(8,128)S(1)}, f32[16,128]{1,0:T(8,128)S(1)}, u32[]{:S(2)}, u32[]{:S(2)}) collective-permute-start(f32[16,128]{1,0:T(8,128)S(1)} %add.48), channel_id=1, source_target_pairs={{0,1},{1,0},{2,3},{3,2},{4,5},{5,4},{6,7},{7,6},{8,9},{9,8},{10,11... | collective-permute-start | bytes 24584 | tf_op jit(solution)/shard_map/ppermute | solution.py:405
  81.7 4.9 %collective-permute-start.9 = (f32[16,128]{1,0:T(8,128)S(1)}, f32[16,128]{1,0:T(8,128)S(1)}, u32[]{:S(2)}, u32[]{:S(2)}) collective-permute-start(f32[16,128]{1,0:T(8,128)S(1)} %add.49), channel_id=1, source_target_pairs={{0,3},{1,2},{2,1},{3,0},{4,7},{5,6},{6,5},{7,4},{8,11},{9,10},{10,... | collective-permute-start | bytes 24584 | tf_op jit(solution)/shard_map/ppermute | solution.py:405
  86.5 3.7 %collective-permute-start.10 = (f32[16,128]{1,0:T(8,128)S(1)}, f32[16,128]{1,0:T(8,128)S(1)}, u32[]{:S(2)}, u32[]{:S(2)}) collective-permute-start(f32[16,128]{1,0:T(8,128)S(1)} %add.50), channel_id=1, source_target_pairs={{0,4},{1,5},{2,6},{3,7},{4,0},{5,1},{6,2},{7,3},{8,12},{9,13},{10,... | collective-permute-start | bytes 24584 | tf_op jit(solution)/shard_map/ppermute | solution.py:405
  90.2 4.9 %collective-permute-start.11 = (f32[16,128]{1,0:T(8,128)S(1)}, f32[16,128]{1,0:T(8,128)S(1)}, u32[]{:S(2)}, u32[]{:S(2)}) collective-permute-start(f32[16,128]{1,0:T(8,128)S(1)} %add.51), channel_id=1, source_target_pairs={{0,12},{1,13},{2,14},{3,15},{4,8},{5,9},{6,10},{7,11},{8,4},{9,5},... | collective-permute-start | bytes 24584 | tf_op jit(solution)/shard_map/ppermute | solution.py:405

commit v2 on v1

v2 whole, which is shorter than its diff:
```python
import functools

import jax
import jax.numpy as jnp
from jax import lax
from jax.experimental import pallas as pl
from jax.experimental.pallas import tpu as pltpu
from jax.sharding import PartitionSpec as P

uptake_rate = 0.6
half_saturation = 0.3
remin_rate = 0.2
dissolved_share = 0.7
epsilon = 1e-06

SEGS = 2
TRACERS = 2
LEV = 32
NBR = 6
BASIS = 4
WIDTH = 2048
HALO = 512
LANE = 128
TILE = 256
BLOCKS = WIDTH // TILE
GROUPS = WIDTH // HALO
CHUNKS = HALO // LANE
ROWS = SEGS * TRACERS * LEV
GROUP_ROWS = TRACERS * CHUNKS * SEGS * LEV
VMEM = pl.BlockSpec(memory_space=pltpu.VMEM)
PARAMS = pltpu.CompilerParams(vmem_limit_bytes=16 * 1024 * 1024)
ANY = pl.BlockSpec(memory_space=pl.ANY)
HBM = pl.BlockSpec(memory_space=pltpu.HBM)
f32 = jnp.float32
bf16 = jnp.bfloat16


def shape(*dims):
    return jax.ShapeDtypeStruct(dims, f32)


def group_row(tracer, chunk, seg):
    return ((tracer * CHUNKS + chunk) * SEGS + seg) * LEV


def natural_reader(ref):
    def read(seg, tracer, start):
        return ref[seg, tracer, :, pl.ds(start, TILE)]

    return read


def group_reader(refs):
    def read(seg, tracer, start):
        ref, place = refs[start // HALO]
        chunk = start % HALO // LANE
        parts = [ref[place, pl.ds(group_row(tracer, chunk + h, seg), LEV), :] for h in range(TILE // LANE)]
        return jnp.concatenate(parts, axis=1)

    return read


def split_tile(read, start, xs_ref, place):
    for seg in range(SEGS):
        for tracer in range(TRACERS):
            value = read(seg, tracer, start)
            high = value.astype(bf16)
            low = (value - high.astype(f32)).astype(bf16)
            row = (seg * TRACERS + tracer) * LEV
            xs_ref[place, pl.ds(row, LEV), :] = high
            xs_ref[place, pl.ds(ROWS + row, LEV), :] = low


def table_row(every_column, table_ref, k, start):
    columns = pl.ds(start, TILE)
    away = table_ref[pl.ds(k, 1), columns] - table_ref[pl.ds(0, 1), columns]
    away = jnp.where(away > HALO, away - every_column, away)
    away = jnp.where(away < -HALO, away + every_column, away)
    return away + lax.broadcasted_iota(jnp.int32, (1, TILE), 1) + start


def picked(xs_ref, places, offsets, index):
    total = None
    depth = lax.broadcasted_iota(jnp.int32, (TILE, TILE), 0)
    for place, offset in zip(places, offsets):
        chosen = jnp.where(depth == index - offset, f32(1), f32(0)).astype(bf16)
        part = jnp.dot(xs_ref[place], chosen, preferred_element_type=f32)
        total = part if total is None else total + part
    return total[:ROWS] + total[ROWS:]


def moved_part(xs_ref, places, offsets, index_of, mixing_of):
    total = [None] * (SEGS * TRACERS)
    for k in range(1, NBR):
        value = picked(xs_ref, places, offsets, index_of(k))
        for seg in range(SEGS):
            mix = mixing_of(seg, k)
            for tracer in range(TRACERS):
                at = seg * TRACERS + tracer
                term = mix * value[at * LEV : (at + 1) * LEV]
                total[at] = term if total[at] is None else total[at] + term
    return total


def factorize(kappa_ref, wet_ref, by_rows_ref, inverse_ref, carry_ref, ratio_ref):
    for group in range(GROUPS):
        for chunk in range(CHUNKS):
            for seg in range(SEGS):
                lanes = pl.ds(group * HALO + chunk * LANE, LANE)
                row = (group * CHUNKS * SEGS + chunk * SEGS + seg) * LEV
                by_rows_ref[pl.ds(row, LEV), :] = kappa_ref[seg, :, lanes]
    wet = []
    for group in range(GROUPS):
        rows = []
        for chunk in range(CHUNKS):
            one = wet_ref[pl.ds(group * CHUNKS + chunk, 1), :]
            rows += [one] * SEGS
        wet.append(jnp.concatenate(rows, axis=0))
    zero = jnp.zeros((CHUNKS * SEGS, LANE), f32)

    def upper_at(group, level):
        if level == 0 or level == LEV:
            return zero
        rows = pl.ds(group * CHUNKS * SEGS * LEV + level, CHUNKS * SEGS, stride=LEV)
        return jnp.where(wet[group] > level, by_rows_ref[rows, :], 0.0)

    upper = [upper_at(group, 0) for group in range(GROUPS)]
    ratio = [zero] * GROUPS
    for level in range(LEV):
        for group in range(GROUPS):
            lower = upper_at(group, level + 1)
            pivot = (1.0 + upper[group] + lower) + upper[group] * ratio[group]
            inverse = 1.0 / pivot
            ratio[group] = -lower * inverse
            inverse_ref[group, level] = jnp.where(wet[group] > level, inverse, 0.0)
            carry_ref[group, level] = upper[group] * inverse
            ratio_ref[group, level] = ratio[group]
            upper[group] = lower


def solve(source_ref, place, inverse_ref, carry_ref, ratio_ref, group, out):
    step = CHUNKS * SEGS

    def source(tracer, level):
        return source_ref[place, pl.ds(group_row(tracer, 0, 0) + level, step, stride=LEV), :]

    value = [[None] * LEV for _ in range(TRACERS)]
    for level in range(LEV):
        inverse = inverse_ref[group, level]
        carry = carry_ref[group, level]
        for tracer in range(TRACERS):
            here = source(tracer, level) * inverse
            if level:
                here = here + carry * value[tracer][level - 1]
            value[tracer][level] = here
    for level in range(LEV - 1, -1, -1):
        ratio = ratio_ref[group, level]
        for tracer in range(TRACERS):
            if level < LEV - 1:
                value[tracer][level] = value[tracer][level] - ratio * value[tracer][level + 1]
            out(tracer, level, value[tracer][level])


def into_group(ref, place):
    def write(tracer, level, value):
        ref[place, pl.ds(group_row(tracer, 0, 0) + level, CHUNKS * SEGS, stride=LEV), :] = value

    return write


def own_blocks(every_column, blocks, read, table_ref, mixing_ref, light_ref, xs_ref, acc_ref, places, ready=None):
    for block in blocks:
        if ready is not None:
            ready(block)
        start = block * TILE
        tiles = list(range(max(0, block - 2), min(BLOCKS, block + 3)))
        total = moved_part(
            xs_ref,
            tiles,
            [tile * TILE for tile in tiles],
            lambda k: table_row(every_column, table_ref, k, start),
            lambda seg, k: mixing_ref[seg, k, :, pl.ds(start, TILE)],
        )
        for seg in range(SEGS):
            columns = pl.ds(start, TILE)
            phosphate = read(seg, 0, start)
            organic = read(seg, 1, start)
            squared = phosphate * phosphate
            uptake = uptake_rate * light_ref[seg, :, columns] * squared / (squared + half_saturation)
            gains = (remin_rate * organic - uptake, dissolved_share * uptake - remin_rate * organic)
            own = mixing_ref[seg, 0, :, columns]
            for tracer, value in enumerate((phosphate, organic)):
                result = own * value + total[seg * TRACERS + tracer] + gains[tracer]
                for h in range(TILE // LANE):
                    row = group_row(tracer, block % 2 * 2 + h, seg)
                    acc_ref[places[block // 2], pl.ds(row, LEV), :] = result[:, h * LANE : (h + 1) * LANE]


EDGE_BLOCKS = (0, 1, BLOCKS - 2, BLOCKS - 1)
MIDDLE_BLOCKS = tuple(range(2, BLOCKS - 2))
EDGE_PLACES = {0: 0, GROUPS - 1: 1}
MIDDLE_PLACES = {group: group - 1 for group in range(1, GROUPS - 1)}


def sent_rows(from_ref, place, to_ref, to_place):
    for tracer in range(TRACERS):
        for chunk in range(CHUNKS):
            to_ref[to_place, pl.ds((tracer * CHUNKS + chunk) * LEV, LEV), :] = from_ref[
                place, pl.ds(group_row(tracer, chunk, SEGS - 1), LEV), :
            ]


def halves_kernel(state_ref, head_ref, tail_ref):
    head_ref[...] = state_ref[:, :, :, :HALO]
    tail_ref[...] = state_ref[:, :, :, WIDTH - HALO :]


def halves(state):
    half = shape(SEGS, TRACERS, LEV, HALO)
    return call(halves_kernel, "edge_columns", 0, (half, half), [], state)


def first_own_kernel(
    every_column, state_ref, table_in, mixing_in, light_in, kappa_in, wet_in,
    edge_ref, middle_ref, inverse_ref, carry_ref, ratio_ref, table_ref, mixing_ref, light_ref, wet_ref,
    xs_ref, acc_ref, by_rows_ref, kappa_ref, sems,
):
    order = (0, GROUPS - 1) + tuple(range(1, GROUPS - 1))
    parts = [(slice(None),) * 3 + (pl.ds(group * HALO, HALO),) for group in order]
    of_mixing = [(mixing_in.at[part], mixing_ref.at[part]) for part in parts]
    pairs = [(table_in, table_ref), (light_in, light_ref), (kappa_in, kappa_ref), (wet_in, wet_ref)]
    pairs = pairs[:2] + of_mixing[:1] + pairs[2:] + of_mixing[1:]
    copies = [pltpu.make_async_copy(*pair, sems.at[i]) for i, pair in enumerate(pairs)]
    for copy in copies:
        copy.start()
    read = natural_reader(state_ref)
    for tile in range(BLOCKS):
        split_tile(read, tile * TILE, xs_ref, tile)

    def ready(block):
        if block == 0:
            for copy in copies[:3]:
                copy.wait()
        elif block == BLOCKS - 2:
            copies[3].wait()
            copies[4].wait()
            factorize(kappa_ref, wet_ref, by_rows_ref, inverse_ref, carry_ref, ratio_ref)
            for copy in copies[5:]:
                copy.wait()

    own_blocks(every_column, EDGE_BLOCKS, read, table_ref, mixing_ref, light_ref, xs_ref, edge_ref, EDGE_PLACES, ready)
    own_blocks(every_column, MIDDLE_BLOCKS, read, table_ref, mixing_ref, light_ref, xs_ref, acc_ref, MIDDLE_PLACES, ready)
    for group, place in MIDDLE_PLACES.items():
        solve(acc_ref, place, inverse_ref, carry_ref, ratio_ref, group, into_group(middle_ref, place))


def second_reader(head_ref, middle_ref, tail_ref):
    return group_reader([(head_ref, 0)] + [(middle_ref, i) for i in range(GROUPS - 2)] + [(tail_ref, 0)])


def second_middle_kernel(
    every_column, head_ref, middle_in_ref, tail_ref, table_ref, mixing_ref, light_ref, inverse_ref, carry_ref, ratio_ref,
    middle_ref, sent_ref, xs_ref,
    acc_ref,
):
    read = second_reader(head_ref, middle_in_ref, tail_ref)
    for tile in range(BLOCKS):
        split_tile(read, tile * TILE, xs_ref, tile)
    own_blocks(every_column, MIDDLE_BLOCKS, read, table_ref, mixing_ref, light_ref, xs_ref, acc_ref, MIDDLE_PLACES)
    for group, place in MIDDLE_PLACES.items():
        solve(acc_ref, place, inverse_ref, carry_ref, ratio_ref, group, into_group(middle_ref, place))
        sent_rows(middle_ref, place, sent_ref, place)


def second_edge_kernel(every_column, head_ref, middle_ref, tail_ref, table_ref, mixing_ref, light_ref, xs_ref, edge_ref):
    read = second_reader(head_ref, middle_ref, tail_ref)
    own_blocks(every_column, EDGE_BLOCKS, read, table_ref, mixing_ref, light_ref, xs_ref, edge_ref, EDGE_PLACES)


def edge_kernel(
    first, every_column, left_ref, right_ref, table_ref, mixing_ref, edge_in_ref, inverse_ref, carry_ref, ratio_ref,
    *outs_and_scratch,
):
    head_ref, tail_ref, *sent, xs_ref, acc_ref = outs_and_scratch
    for side, ref in enumerate((left_ref, right_ref)):
        read = natural_reader(ref) if first else group_reader([(ref, 0)])
        for tile in range(HALO // TILE):
            split_tile(read, tile * TILE, xs_ref, side * 2 + tile)
    uses = ((0, 0, (0, 1)), (1, 0, (1,)), (BLOCKS - 2, 1, (2,)), (BLOCKS - 1, 1, (2, 3)))
    offsets = (-HALO, -TILE, WIDTH, WIDTH + TILE)
    for block, side, places in uses:
        start = block * TILE
        total = moved_part(
            xs_ref,
            places,
            [offsets[place] for place in places],
            lambda k: table_row(every_column, table_ref, k, start),
            lambda seg, k: mixing_ref[seg, k, :, pl.ds(start, TILE)],
        )
        for seg in range(SEGS):
            for tracer in range(TRACERS):
                value = total[seg * TRACERS + tracer]
                for h in range(TILE // LANE):
                    row = pl.ds(group_row(tracer, block % 2 * 2 + h, seg), LEV)
                    acc_ref[side, row, :] = edge_in_ref[side, row, :] + value[:, h * LANE : (h + 1) * LANE]
    for side, (group, ref) in enumerate(((0, head_ref), (GROUPS - 1, tail_ref))):
        solve(acc_ref, side, inverse_ref, carry_ref, ratio_ref, group, into_group(ref, 0))
        if sent:
            sent_rows(ref, 0, sent[0], side)


EDGE = shape(2, GROUP_ROWS, LANE)
MIDDLE = shape(GROUPS - 2, GROUP_ROWS, LANE)
SENT = shape(2, GROUP_ROWS // SEGS, LANE)
ONE = shape(1, GROUP_ROWS, LANE)


def call(kernel, name, flops, outs, scratch, *operands):
    return pl.pallas_call(
        kernel,
        out_shape=outs,
        in_specs=[VMEM] * len(operands),
        out_specs=jax.tree.map(lambda _: VMEM, outs),
        scratch_shapes=scratch,
        compiler_params=PARAMS,
        cost_estimate=pl.CostEstimate(flops=flops, bytes_accessed=4_000_000, transcendentals=0),
        name=name,
    )(*operands)


def first_own(every_column, state, table, mixing, light, kappa, wet):
    factors = shape(GROUPS, LEV, CHUNKS * SEGS, LANE)
    like = [jax.ShapeDtypeStruct(one.shape, one.dtype) for one in (table, mixing, light, wet)]
    return pl.pallas_call(
        functools.partial(first_own_kernel, every_column),
        out_shape=(EDGE, MIDDLE, factors, factors, factors, *like),
        in_specs=[VMEM] + [HBM] * 5,
        out_specs=(VMEM,) * 9,
        scratch_shapes=[
            pltpu.VMEM((BLOCKS, 2 * ROWS, TILE), bf16),
            pltpu.VMEM((GROUPS - 2, GROUP_ROWS, LANE), f32),
            pltpu.VMEM((GROUPS * CHUNKS * SEGS * LEV, LANE), f32),
            pltpu.VMEM((SEGS, LEV, WIDTH), f32),
            pltpu.SemaphoreType.DMA((4 + GROUPS,)),
        ],
        compiler_params=PARAMS,
        cost_estimate=pl.CostEstimate(flops=6_000_000_000, bytes_accessed=4_000_000, transcendentals=0),
        name="first_step_own",
    )(state, *[pltpu.with_memory_space_constraint(one, pltpu.HBM) for one in (table, mixing, light, kappa, wet)])


def second_middle(every_column, head, middle, tail, table, mixing, light, factors):
    return call(
        functools.partial(second_middle_kernel, every_column), "second_step_middle", 3_500_000_000,
        (MIDDLE, SENT, jax.ShapeDtypeStruct((BLOCKS, 2 * ROWS, TILE), bf16)),
        [pltpu.VMEM((GROUPS - 2, GROUP_ROWS, LANE), f32)],
        head, middle, tail, table, mixing, light, *factors,
    )


def second_edge(every_column, head, middle, tail, table, mixing, light, xs):
    return call(
        functools.partial(second_edge_kernel, every_column), "second_step_edges_own", 2_500_000_000, EDGE, [],
        head, middle, tail, table, mixing, light, xs,
    )


def edges(first, every_column, left, right, table, mixing, edge, factors):
    return call(
        functools.partial(edge_kernel, first, every_column),
        "first_step_edges" if first else "second_step_edges", 1_000_000_000,
        (ONE, ONE) if first else (ONE, ONE, SENT),
        [pltpu.VMEM((4, 2 * ROWS, TILE), bf16), pltpu.VMEM((2, GROUP_ROWS, LANE), f32)],
        left, right, table, mixing, edge, *factors,
    )


PAIRS = [(i, j) for i in range(BASIS) for j in range(i, BASIS)]


def residual_of(groups, segs, state_ref, wet_ref, basis_ref, before_of, write, sums, products):
    level = lax.broadcasted_iota(jnp.int32, (8, LANE), 0)
    for group in groups:
        for chunk in range(CHUNKS):
            lanes = pl.ds(group * HALO + chunk * LANE, LANE)
            wet = jnp.broadcast_to(wet_ref[pl.ds(group * CHUNKS + chunk, 1), :], (8, LANE))
            for seg in segs:
                for tracer in range(TRACERS):
                    for part in range(LEV // 8):
                        rows = pl.ds(part * 8, 8)
                        before = before_of(group, chunk, seg, tracer, part * 8)
                        own = state_ref[seg, tracer, rows, lanes]
                        here = jnp.where(wet > level + part * 8, own - before, 0.0)
                        write(group, chunk, seg, tracer, rows, here)
                        vectors = [basis_ref[i, seg, tracer, rows, lanes] for i in range(BASIS)]
                        for i in range(BASIS):
                            sums[i] = sums[i] + vectors[i] * here
                        sums[BASIS] = sums[BASIS] + here * here
                        if products:
                            for at, (i, j) in enumerate(PAIRS):
                                sums[BASIS + 1 + at] = sums[BASIS + 1 + at] + vectors[i] * vectors[j]


def early_kernel(
    state_ref, wet_ref, basis_ref, head_ref, middle_ref, tail_ref, came_ref, out_ref, residual_ref, sums_ref, sems
):
    refs = [(head_ref, 0)] + [(middle_ref, i) for i in range(GROUPS - 2)] + [(tail_ref, 0)]
    sums = [jnp.zeros((8, LANE), f32) for _ in range(BASIS + 1 + len(PAIRS))]

    def before_of(group, chunk, seg, tracer, level):
        if seg:
            ref, place = refs[group]
            return ref[place, pl.ds(group_row(tracer, chunk, seg - 1) + level, 8), :]
        return came_ref[group - 1, pl.ds((tracer * CHUNKS + chunk) * LEV + level, 8), :]

    def write(group, chunk, seg, tracer, rows, value):
        residual_ref[seg, tracer, rows, pl.ds(group * HALO + chunk * LANE, LANE)] = value

    residual_of(range(GROUPS), range(1, SEGS), state_ref, wet_ref, basis_ref, before_of, write, sums, True)
    parts = [(slice(1, SEGS),), (slice(0, 1), slice(None), slice(None), pl.ds(HALO, WIDTH - 2 * HALO))]
    copies = [pltpu.make_async_copy(residual_ref.at[part], out_ref.at[part], sems.at[i]) for i, part in enumerate(parts)]
    copies[0].start()
    residual_of(range(1, GROUPS - 1), (0,), state_ref, wet_ref, basis_ref, before_of, write, sums, True)
    copies[1].start()
    for group in (0, GROUPS - 1):
        for chunk in range(CHUNKS):
            lanes = pl.ds(group * HALO + chunk * LANE, LANE)
            for tracer in range(TRACERS):
                for part in range(LEV // 8):
                    vectors = [basis_ref[i, 0, tracer, pl.ds(part * 8, 8), lanes] for i in range(BASIS)]
                    for at, (i, j) in enumerate(PAIRS):
                        sums[BASIS + 1 + at] = sums[BASIS + 1 + at] + vectors[i] * vectors[j]
    for i, one in enumerate(sums):
        sums_ref[i] = one
    for copy in copies:
        copy.wait()


def late_kernel(
    state_ref, wet_ref, basis_ref, came_ref, early_ref, unused_ref, residual_ref, sums_ref, pieces_ref, sems
):
    sums = [early_ref[i] for i in range(BASIS + 1 + len(PAIRS))]

    def before_of(group, chunk, seg, tracer, level):
        return came_ref[EDGE_PLACES[group], pl.ds((tracer * CHUNKS + chunk) * LEV + level, 8), :]

    def write(group, chunk, seg, tracer, rows, value):
        pieces_ref[EDGE_PLACES[group], tracer, rows, pl.ds(chunk * LANE, LANE)] = value

    copies = []
    for group, place in EDGE_PLACES.items():
        residual_of((group,), (0,), state_ref, wet_ref, basis_ref, before_of, write, sums, False)
        copy = pltpu.make_async_copy(
            pieces_ref.at[place], residual_ref.at[0, :, :, pl.ds(group * HALO, HALO)], sems.at[place]
        )
        copy.start()
        copies.append(copy)
    rows = [jnp.sum(one, axis=0, keepdims=True) for one in sums]
    rows.append(jnp.zeros((16 - len(rows), LANE), f32))
    sums_ref[...] = jnp.concatenate(rows, axis=0)
    for copy in copies:
        copy.wait()


def early(state, wet, basis, head, middle, tail, came):
    whole = shape(SEGS, TRACERS, LEV, WIDTH)
    return pl.pallas_call(
        early_kernel,
        out_shape=(whole, whole, shape(BASIS + 1 + len(PAIRS), 8, LANE)),
        in_specs=[VMEM] * 7,
        out_specs=(HBM, VMEM, VMEM),
        scratch_shapes=[pltpu.SemaphoreType.DMA((2,))],
        compiler_params=PARAMS,
        cost_estimate=pl.CostEstimate(flops=10_000_000, bytes_accessed=4_000_000, transcendentals=0),
        name="residual_known",
    )(state, wet, basis, head, middle, tail, came)


def late(state, wet, basis, came, sums, residual):
    return pl.pallas_call(
        late_kernel,
        out_shape=(shape(SEGS, TRACERS, LEV, WIDTH), shape(16, LANE), shape(2, TRACERS, LEV, HALO)),
        in_specs=[VMEM] * 5 + [HBM],
        out_specs=(HBM, VMEM, VMEM),
        scratch_shapes=[pltpu.SemaphoreType.DMA((2,))],
        input_output_aliases={5: 0},
        compiler_params=PARAMS,
        cost_estimate=pl.CostEstimate(flops=3_000_000, bytes_accessed=4_000_000, transcendentals=0),
        name="residual_last",
    )(state, wet, basis, came, sums, residual)


def scaled_kernel(count, residual_ref, pieces_ref, basis_ref, sums_ref, new_ref, coefficients_ref):
    sums = jnp.sum(sums_ref[...], axis=1, keepdims=True)
    one = [sums[i : i + 1] for i in range(16)]
    first, square, products = one[:BASIS], one[BASIS], iter(one[BASIS + 1 :])
    gram = [[None] * BASIS for _ in range(BASIS)]
    for i in range(BASIS):
        for j in range(i, BASIS):
            gram[i][j] = gram[j][i] = next(products)
    second = [first[i] - sum(gram[i][j] * first[j] for j in range(BASIS)) for i in range(BASIS)]
    both = [first[i] + second[i] for i in range(BASIS)]
    for i in range(BASIS):
        square = square - both[i] * (2.0 * first[i] - sum(gram[i][j] * both[j] for j in range(BASIS)))
    spread = jnp.sqrt(square / count + epsilon)
    lane = lax.broadcasted_iota(jnp.int32, (8, LANE), 1)
    result = jnp.zeros((8, LANE), f32)
    for i, value in enumerate(both + [spread]):
        result = jnp.where(lane == i, value, result)
    coefficients_ref[...] = result
    scale = 1.0 / spread
    weights = [jnp.broadcast_to(-value * scale, (LEV, LANE)) for value in both]
    scale = jnp.broadcast_to(scale, (LEV, LANE))
    for seg in range(SEGS):
        for tracer in range(TRACERS):
            for chunk in range(WIDTH // LANE):
                lanes = pl.ds(chunk * LANE, LANE)
                group = chunk // CHUNKS
                if seg == 0 and group in EDGE_PLACES:
                    here = pieces_ref[EDGE_PLACES[group], tracer, :, pl.ds(chunk % CHUNKS * LANE, LANE)]
                else:
                    here = residual_ref[seg, tracer, :, lanes]
                total = here * scale
                for i in range(BASIS):
                    total = total + weights[i] * basis_ref[i, seg, tracer, :, lanes]
                new_ref[seg, tracer, :, lanes] = total


def scaled(count, residual, pieces, basis, sums):
    return call(
        functools.partial(scaled_kernel, count), "orthogonal_and_scaled", 4_000_000,
        (shape(SEGS, TRACERS, LEV, WIDTH), shape(8, LANE)), [], residual, pieces, basis, sums,
    )


def shifted(block, axis, distance):
    count = lax.axis_size(axis)
    return lax.ppermute(block, axis, [(i, (i + distance) % count) for i in range(count)])


def summed_everywhere(value):
    for axis in ("seg", "col"):
        count = lax.axis_size(axis)
        done = 1
        while done < count:
            flip = done if done in (1, 2, 4, 8) else done
            value = value + lax.ppermute(value, axis, [(i, i ^ FLIPS[axis][flip]) for i in range(count)])
            done *= 2
    return value


FLIPS = {"seg": {1: 1, 2: 2, 4: 6}, "col": {1: 1, 2: 3, 4: 4, 8: 12}}


def per_device(segment_state, light, mixing, kappa, neighbour_columns, wet_levels, basis):
    every_column = lax.axis_size("col") * WIDTH
    state = pltpu.with_memory_space_constraint(segment_state, pltpu.VMEM)
    head, tail = halves(state)
    left = shifted(tail, "col", 1)
    right = shifted(head, "col", -1)
    table = neighbour_columns.T
    wet = wet_levels.reshape(WIDTH // LANE, LANE)
    edge, middle, *kept = first_own(every_column, state, table, mixing, light, kappa, wet)
    *factors, table, mixing, light, wet = kept
    head, tail = edges(True, every_column, left, right, table, mixing, edge, factors)
    left = shifted(tail, "col", 1)
    right = shifted(head, "col", -1)
    end_middle, sent, xs = second_middle(every_column, head, middle, tail, table, mixing, light, factors)
    came_middle = shifted(sent, "seg", 1)
    edge = second_edge(every_column, head, middle, tail, table, mixing, light, xs)
    head, tail, sent = edges(False, every_column, left, right, table, mixing, edge, factors)
    came_edge = shifted(sent, "seg", 1)
    residual, held, sums = early(state, wet, basis, head, end_middle, tail, came_middle)
    residual, sums, pieces = late(state, wet, basis, came_edge, sums, residual)
    count = lax.axis_size("seg") * SEGS * TRACERS * LEV * every_column
    new_vector, coefficients = scaled(count, held, pieces, basis, summed_everywhere(sums))
    return (residual, new_vector, coefficients[0, : BASIS + 1])


def solution(mesh):
    return jax.shard_map(
        per_device,
        mesh=mesh,
        in_specs=(
            P("seg", None, None, "col"),
            P("seg", None, "col"),
            P("seg", None, None, "col"),
            P("seg", None, "col"),
            P("col", None),
            P("col"),
            P(None, "seg", None, None, "col"),
        ),
        out_specs=(P("seg", None, None, "col"), P("seg", None, None, "col"), P()),
        check_vma=False,
    )
```

time: 102 us -> 71.9 us (0.70)
  Pallas kernels: 41.9 us -> 25 us
  waiting for transfers between devices: 34.5 us -> 28.1 us
  local copies, waits for them, and re-layouts: 8.04 us -> 1.74 us
  other arithmetic: 2.23 us -> 0.02 us
  starting transfers between devices: 14 us -> 16.1 us
    pallas_call x6 -> x9, Pallas kernels: 41.9 us -> 25 us  [the longest x6 13.4 us: call(): pl.pallas_call(kernel, out_shape=outs, in_specs=[VMEM] * len(operands), o...]
    ppermute x5 -> x6, waiting for transfers between devices: 9.81 us -> 3.81 us  [shifted(): lax.ppermute(block, axis, [(i, (i + distance) % count) for i in range(cou...]
    slice x4 -> x0, local copies, waits for them, and re-layouts: 3.88 us -> none  [the longest x3 2.8 us: sent_segment(): groups.reshape(count, TRACERS * CHUNKS, SEGS, LEV, LANE)[:, :, SEGS - 1]]
    ppermute x5 -> x6, starting transfers between devices: 11.8 us -> 13.6 us  [shifted(): lax.ppermute(block, axis, [(i, (i + distance) % count) for i in range(cou...]
    add x7, other arithmetic: 1.31 us -> 0.02 us  [summed_everywhere(): value + lax.ppermute(value, axis, [(i, i ^ FLIPS[axis][flip]) for i in ra...]
    unnamed x10 -> x6, local copies, waits for them, and re-layouts: 2.35 us -> 1.23 us
  transfers between devices with their start and end apart: 12 -> 13, of which waited for: 8 -> 9; matrix products, arithmetic and copies ran while one was open for 2% -> 0% of each run, Pallas kernels for 22% -> 29%
where the time goes in v2:
time: 71.9 us; the launch traced here: 71.7 us
  waiting for transfers between devices  28.1 us (39%)
  Pallas kernels  25 us (35%)
  starting transfers between devices  16.1 us (22%)
  local copies, waits for them, and re-layouts  1.74 us (2%)
  between operations  0.78 us (1%)
    ppermute x7, waiting for transfers between devices, summed_everywhere(): lax.ppermute(value, axis, [(i, i ^ FLIPS[axis][flip]) for i in range(coun...  24.3 us
    ppermute x6, starting transfers between devices, shifted(): lax.ppermute(block, axis, [(i, (i + distance) % count) for i in range(cou...  13.6 us
    pallas_call x6, Pallas kernels, call(): pl.pallas_call(kernel, out_shape=outs, in_specs=[VMEM] * len(operands), o...  13.4 us
    pallas_call x1, Pallas kernels, first_own(): pl.pallas_call(functools.partial(first_own_kernel, every_column), out_sha...  9.28 us
    ppermute x6, waiting for transfers between devices, shifted(): lax.ppermute(block, axis, [(i, (i + distance) % count) for i in range(cou...  3.81 us
    ppermute x7, starting transfers between devices, summed_everywhere(): lax.ppermute(value, axis, [(i, i ^ FLIPS[axis][flip]) for i in range(coun...  2.5 us
    pallas_call x1, Pallas kernels, early(): pl.pallas_call(early_kernel, out_shape=(whole, whole, shape(BASIS + 1 + l...  1.53 us
  transfers between devices with their start and end apart: 13, of which 9 were waited for; matrix products, arithmetic and copies ran while one was open for 0% of the time, Pallas kernels for 29%

profile of v2, /device:TPU:0, one launch (start us, length us, event | category | flops | bytes accessed | tf_op | source)
XLA Modules:
  0.0 71.7 jit_solution(5071422338275589593)
XLA Ops:
  0.6 0.0 copy-start.1
  0.6 1.2 %copy-done.1 = f32[2,2,32,2048]{3,2,1,0:T(8,128)S(1)} copy-done((f32[2,2,32,2048]{3,2,1,0:T(8,128)S(1)}, f32[2,2,32,2048]{3,2,1,0:T(8,128)}, u32[]{:S(2)}) %copy-start.1) | copy-done | bytes 1048600
  1.9 2.1 %collective-permute-start = (f32[2,2,32,512]{3,2,1,0:T(8,128)S(1)}, f32[2,2,32,512]{3,2,1,0:T(8,128)S(1)}, u32[]{:S(2)}, u32[]{:S(2)}) collective-permute-start(f32[2,2,32,512]{3,2,1,0:T(8,128)S(1)} %get-tuple-element.31), channel_id=1, source_target_pairs={{0,1},{1,2},{2,3},{3,4},{4,5},{5,6},{6,7},{7,8},{8,9},{9,10},{10,1... | collective-permute-start | bytes 786440 | tf_op jit(solution)/shard_map/ppermute | solution.py:538
  4.0 4.4 %collective-permute-start.1 = (f32[2,2,32,512]{3,2,1,0:T(8,128)S(1)}, f32[2,2,32,512]{3,2,1,0:T(8,128)S(1)}, u32[]{:S(2)}, u32[]{:S(2)}) collective-permute-start(f32[2,2,32,512]{3,2,1,0:T(8,128)S(1)} %get-tuple-element.32), channel_id=1, source_target_pairs={{0,15},{1,0},{2,1},{3,2},{4,3},{5,4},{6,5},{7,6},{8,7},{9,8},{10,9... | collective-permute-start | bytes 786440 | tf_op jit(solution)/shard_map/ppermute | solution.py:538
  8.4 9.3 %first_step_own.1 = (f32[2,512,128]{2,1,0:T(8,128)S(1)}, f32[2,512,128]{2,1,0:T(8,128)S(1)}, f32[4,32,8,128]{3,2,1,0:T(8,128)S(1)}, f32[4,32,8,128]{3,2,1,0:T(8,...) custom-call(f32[2,2,32,2048]{3,2,1,0:T(8,128)S(1)} %copy-done.1, ...), custom_call_target="tpu_custom_call" | custom-call | flops 6000000000 | bytes 4000000 | tf_op jit(solution)/shard_map/first_step_own/pallas_call | solution.py:334
  17.7 0.0 collective-permute-done.left_ref
  17.7 0.0 collective-permute-done.1.right_ref
  17.7 2.0 %first_step_edges.1 = (f32[1,512,128]{2,1,0:T(8,128)S(1)}, f32[1,512,128]{2,1,0:T(8,128)S(1)}) custom-call(f32[2,2,32,512]{3,2,1,0:T(8,128)S(1)} %collective-permute-done.left_ref, f32[2,2,32,512]{3,2,1,0:T(8,128)S(1)} %collective-permute-done.1.right_ref, s32[6,2048]{1,0:T(8,128)S(1)} %get-tuple-element.33.table_ref, ...), custom_call_target="tpu_custom_call" | custom-call | flops 1000000000 | bytes 4000000 | tf_op jit(solution)/shard_map/first_step_edges/pallas_call | solution.py:319
  19.7 0.1 collective-permute-start.2
  19.8 5.3 %collective-permute-start.3 = (f32[1,512,128]{2,1,0:T(8,128)S(1)}, f32[1,512,128]{2,1,0:T(8,128)S(1)}, u32[]{:S(2)}, u32[]{:S(2)}) collective-permute-start(f32[1,512,128]{2,1,0:T(8,128)S(1)} %get-tuple-element.40.head_ref), channel_id=1, source_target_pairs={{0,15},{1,0},{2,1},{3,2},{4,3},{5,4},{6,5},{7,6},{8,7},{9,8},{10,9... | collective-permute-start | bytes 786440 | tf_op jit(solution)/shard_map/ppermute | solution.py:538
  25.1 4.7 %second_step_middle.1 = (f32[2,512,128]{2,1,0:T(8,128)S(1)}, f32[2,256,128]{2,1,0:T(8,128)S(1)}, bf16[8,256,256]{2,1,0:T(8,128)(2,1)S(1)}) custom-call(f32[1,512,128]{2,1,0:T(8,128)S(1)} %get-tuple-element.40.head_ref, f32[2,512,128]{2,1,0:T(8,128)S(1)} %get-tuple-element.41.middle_in_ref.middle_ref, f32[1,512,128]{2,1,0:T(8,128)S(1)} %get-tuple-element.39.tail_ref, ...), custom_call_target="tpu_custom_call" | custom-call | flops 3500000000 | bytes 4000000 | tf_op jit(solution)/shard_map/second_step_middle/pallas_call | solution.py:319
  29.9 0.0 collective-permute-start.5
  29.9 3.0 %second_step_edges_own.1.edge_in_ref = f32[2,512,128]{2,1,0:T(8,128)S(1)} custom-call(f32[1,512,128]{2,1,0:T(8,128)S(1)} %get-tuple-element.40.head_ref, f32[2,512,128]{2,1,0:T(8,128)S(1)} %get-tuple-element.41.middle_in_ref.middle_ref, f32[1,512,128]{2,1,0:T(8,128)S(1)} %get-tuple-element.39.tail_ref, s32[6,2048]{1,0:T(8,128)S(1)} %get-tuple-element.33.table_ref, ...), custom_call_target="tpu_custom_call" | custom-call | flops 2500000000 | bytes 4000000 | tf_op jit(solution)/shard_map/second_step_edges_own/pallas_call | solution.py:319
  32.9 0.0 copy-start
  32.9 0.0 copy-start.2
  32.9 0.0 collective-permute-done.2.left_ref
  32.9 0.0 collective-permute-done.3.right_ref
  33.0 2.1 %second_step_edges.1 = (f32[1,512,128]{2,1,0:T(8,128)S(1)}, f32[1,512,128]{2,1,0:T(8,128)S(1)}, f32[2,256,128]{2,1,0:T(8,128)S(1)}) custom-call(f32[1,512,128]{2,1,0:T(8,128)S(1)} %collective-permute-done.2.left_ref, f32[1,512,128]{2,1,0:T(8,128)S(1)} %collective-permute-done.3.right_ref, s32[6,2048]{1,0:T(8,128)S(1)} %get-tuple-element.33.table_ref, ...), custom_call_target="tpu_custom_call" | custom-call | flops 1000000000 | bytes 4000000 | tf_op jit(solution)/shard_map/second_step_edges/pallas_call | solution.py:319
  35.0 1.7 %collective-permute-start.4 = (f32[2,256,128]{2,1,0:T(8,128)S(1)}, f32[2,256,128]{2,1,0:T(8,128)S(1)}, u32[]{:S(2)}, u32[]{:S(2)}) collective-permute-start(f32[2,256,128]{2,1,0:T(8,128)S(1)} %get-tuple-element.44), channel_id=1, source_target_pairs={{0,16},{16,32},{32,48},{48,64},{64,80},{80,96},{96,112},{112,0},{1... | collective-permute-start | bytes 786440 | tf_op jit(solution)/shard_map/ppermute | solution.py:538
  36.7 0.2 collective-permute-done.5.came_ref
  36.9 0.0 copy-done
  36.9 0.0 copy-done.2
  36.9 1.5 %residual_known.1 = (f32[2,2,32,2048]{3,2,1,0:T(8,128)}, f32[2,2,32,2048]{3,2,1,0:T(8,128)S(1)}, f32[15,8,128]{2,1,0:T(8,128)S(1)}) custom-call(f32[2,2,32,2048]{3,2,1,0:T(8,128)S(1)} %copy-done.2, s32[16,128]{1,0:T(8,128)S(1)} %get-tuple-element.30.wet_ref, f32[4,2,2,32,2048]{4,3,2,1,0:T(8,128)S(1)} %copy-done, ...), custom_call_target="tpu_custom_call" | custom-call | flops 10000000 | bytes 4000000 | tf_op jit(solution)/shard_map/residual_known/pallas_call | solution.py:467
  38.4 3.6 %collective-permute-done.4.came_ref = f32[2,256,128]{2,1,0:T(8,128)S(1)} collective-permute-done((f32[2,256,128]{2,1,0:T(8,128)S(1)}, f32[2,256,128]{2,1,0:T(8,128)S(1)}, u32[]{:S(2)}, u32[]{:S(2)}) %collective-permute-start.4) | collective-permute-done | bytes 262176 | tf_op jit(solution)/shard_map/ppermute | solution.py:538
  42.0 0.8 %residual_last.1 = (f32[2,2,32,2048]{3,2,1,0:T(8,128)}, f32[16,128]{1,0:T(8,128)S(1)}, f32[2,2,32,512]{3,2,1,0:T(8,128)S(1)}) custom-call(f32[2,2,32,2048]{3,2,1,0:T(8,128)S(1)} %copy-done.2, s32[16,128]{1,0:T(8,128)S(1)} %get-tuple-element.30.wet_ref, f32[4,2,2,32,2048]{4,3,2,1,0:T(8,128)S(1)} %copy-done, ...), custom_call_target="tpu_custom_call", output_to_operand_aliasing={{0}: (5, {})} | custom-call | flops 3000000 | bytes 4000000 | tf_op jit(solution)/shard_map/residual_last/pallas_call | solution.py:480
  42.9 0.1 collective-permute-start.6
  43.0 1.2 %collective-permute-done.6 = f32[16,128]{1,0:T(8,128)S(1)} collective-permute-done((f32[16,128]{1,0:T(8,128)S(1)}, f32[16,128]{1,0:T(8,128)S(1)}, u32[]{:S(2)}, u32[]{:S(2)}) %collective-permute-start.6) | collective-permute-done | bytes 8224 | tf_op jit(solution)/shard_map/ppermute | solution.py:547
  44.1 0.3 collective-permute-start.7
  44.5 3.3 %collective-permute-done.7 = f32[16,128]{1,0:T(8,128)S(1)} collective-permute-done((f32[16,128]{1,0:T(8,128)S(1)}, f32[16,128]{1,0:T(8,128)S(1)}, u32[]{:S(2)}, u32[]{:S(2)}) %collective-permute-start.7) | collective-permute-done | bytes 8224 | tf_op jit(solution)/shard_map/ppermute | solution.py:547
  47.8 1.8 %collective-permute-start.8 = (f32[16,128]{1,0:T(8,128)S(1)}, f32[16,128]{1,0:T(8,128)S(1)}, u32[]{:S(2)}, u32[]{:S(2)}) collective-permute-start(f32[16,128]{1,0:T(8,128)S(1)} %add.22), channel_id=1, source_target_pairs={{0,96},{16,112},{32,64},{48,80},{64,32},{80,48},{96,0},{112,16},{1... | collective-permute-start | bytes 24584 | tf_op jit(solution)/shard_map/ppermute | solution.py:547
  49.6 3.1 %collective-permute-done.8 = f32[16,128]{1,0:T(8,128)S(1)} collective-permute-done((f32[16,128]{1,0:T(8,128)S(1)}, f32[16,128]{1,0:T(8,128)S(1)}, u32[]{:S(2)}, u32[]{:S(2)}) %collective-permute-start.8) | collective-permute-done | bytes 8224 | tf_op jit(solution)/shard_map/ppermute | solution.py:547
  52.6 0.0 collective-permute-start.9
  52.6 3.6 %collective-permute-done.9 = f32[16,128]{1,0:T(8,128)S(1)} collective-permute-done((f32[16,128]{1,0:T(8,128)S(1)}, f32[16,128]{1,0:T(8,128)S(1)}, u32[]{:S(2)}, u32[]{:S(2)}) %collective-permute-start.9) | collective-permute-done | bytes 8224 | tf_op jit(solution)/shard_map/ppermute | solution.py:547
  56.3 0.0 collective-permute-start.10
  56.3 4.9 %collective-permute-done.10 = f32[16,128]{1,0:T(8,128)S(1)} collective-permute-done((f32[16,128]{1,0:T(8,128)S(1)}, f32[16,128]{1,0:T(8,128)S(1)}, u32[]{:S(2)}, u32[]{:S(2)}) %collective-permute-start.10) | collective-permute-done | bytes 8224 | tf_op jit(solution)/shard_map/ppermute | solution.py:547
  61.2 0.0 collective-permute-start.11
  61.2 3.6 %collective-permute-done.11 = f32[16,128]{1,0:T(8,128)S(1)} collective-permute-done((f32[16,128]{1,0:T(8,128)S(1)}, f32[16,128]{1,0:T(8,128)S(1)}, u32[]{:S(2)}, u32[]{:S(2)}) %collective-permute-start.11) | collective-permute-done | bytes 8224 | tf_op jit(solution)/shard_map/ppermute | solution.py:547
  64.8 0.3 collective-permute-start.12
  65.1 4.6 %collective-permute-done.12 = f32[16,128]{1,0:T(8,128)S(1)} collective-permute-done((f32[16,128]{1,0:T(8,128)S(1)}, f32[16,128]{1,0:T(8,128)S(1)}, u32[]{:S(2)}, u32[]{:S(2)}) %collective-permute-start.12) | collective-permute-done | bytes 8224 | tf_op jit(solution)/shard_map/ppermute | solution.py:547
  69.7 1.6 %orthogonal_and_scaled.1 = (f32[2,2,32,2048]{3,2,1,0:T(8,128)}, f32[8,128]{1,0:T(8,128)S(1)}) custom-call(f32[2,2,32,2048]{3,2,1,0:T(8,128)S(1)} %get-tuple-element.52.residual_ref, f32[2,2,32,512]{3,2,1,0:T(8,128)S(1)} %get-tuple-element.53.pieces_ref, f32[4,2,2,32,2048]{4,3,2,1,0:T(8,128)S(1)} %copy-done, f32[16,128]{1,0:T(8,128)S(1)} %add.27.sums_ref), custom_call_target="tpu_custom_call" | custom-call | flops 4000000 | bytes 4000000 | tf_op jit(solution)/shard_map/orthogonal_and_scaled/pallas_call | solution.py:319
  71.2 0.5 slice_bitcast_fusion
  (8 shorter events, 0.1 us)
Async XLA Ops:
  0.6 1.2 %copy-start.1 = (f32[2,2,32,2048]{3,2,1,0:T(8,128)S(1)}, f32[2,2,32,2048]{3,2,1,0:T(8,128)}, u32[]{:S(2)}) copy-start(f32[2,2,32,2048]{3,2,1,0:T(8,128)} %state_ref.7) | copy-start | bytes 3145732
  1.9 15.8 %collective-permute-start = (f32[2,2,32,512]{3,2,1,0:T(8,128)S(1)}, f32[2,2,32,512]{3,2,1,0:T(8,128)S(1)}, u32[]{:S(2)}, u32[]{:S(2)}) collective-permute-start(f32[2,2,32,512]{3,2,1,0:T(8,128)S(1)} %get-tuple-element.31), channel_id=1, source_target_pairs={{0,1},{1,2},{2,3},{3,4},{4,5},{5,6},{6,7},{7,8},{8,9},{9,10},{10,1... | collective-permute-start | bytes 786440 | tf_op jit(solution)/shard_map/ppermute | solution.py:538
  4.0 13.7 %collective-permute-start.1 = (f32[2,2,32,512]{3,2,1,0:T(8,128)S(1)}, f32[2,2,32,512]{3,2,1,0:T(8,128)S(1)}, u32[]{:S(2)}, u32[]{:S(2)}) collective-permute-start(f32[2,2,32,512]{3,2,1,0:T(8,128)S(1)} %get-tuple-element.32), channel_id=1, source_target_pairs={{0,15},{1,0},{2,1},{3,2},{4,3},{5,4},{6,5},{7,6},{8,7},{9,8},{10,9... | collective-permute-start | bytes 786440 | tf_op jit(solution)/shard_map/ppermute | solution.py:538
  19.7 13.2 %collective-permute-start.2 = (f32[1,512,128]{2,1,0:T(8,128)S(1)}, f32[1,512,128]{2,1,0:T(8,128)S(1)}, u32[]{:S(2)}, u32[]{:S(2)}) collective-permute-start(f32[1,512,128]{2,1,0:T(8,128)S(1)} %get-tuple-element.39.tail_ref), channel_id=1, source_target_pairs={{0,1},{1,2},{2,3},{3,4},{4,5},{5,6},{6,7},{7,8},{8,9},{9,10},{10,1... | collective-permute-start | bytes 786440 | tf_op jit(solution)/shard_map/ppermute | solution.py:538
  19.8 13.2 %collective-permute-start.3 = (f32[1,512,128]{2,1,0:T(8,128)S(1)}, f32[1,512,128]{2,1,0:T(8,128)S(1)}, u32[]{:S(2)}, u32[]{:S(2)}) collective-permute-start(f32[1,512,128]{2,1,0:T(8,128)S(1)} %get-tuple-element.40.head_ref), channel_id=1, source_target_pairs={{0,15},{1,0},{2,1},{3,2},{4,3},{5,4},{6,5},{7,6},{8,7},{9,8},{10,9... | collective-permute-start | bytes 786440 | tf_op jit(solution)/shard_map/ppermute | solution.py:538
  29.9 7.0 %collective-permute-start.5 = (f32[2,256,128]{2,1,0:T(8,128)S(1)}, f32[2,256,128]{2,1,0:T(8,128)S(1)}, u32[]{:S(2)}, u32[]{:S(2)}) collective-permute-start(f32[2,256,128]{2,1,0:T(8,128)S(1)} %get-tuple-element.48), channel_id=1, source_target_pairs={{0,16},{16,32},{32,48},{48,64},{64,80},{80,96},{96,112},{112,0},{1... | collective-permute-start | bytes 786440 | tf_op jit(solution)/shard_map/ppermute | solution.py:538
  32.9 4.0 %copy-start = (f32[4,2,2,32,2048]{4,3,2,1,0:T(8,128)S(1)}, f32[4,2,2,32,2048]{4,3,2,1,0:T(8,128)}, u32[]{:S(2)}) copy-start(f32[4,2,2,32,2048]{4,3,2,1,0:T(8,128)} %basis_ref.5) | copy-start | bytes 12582916
  32.9 4.0 %copy-start.2 = (f32[2,2,32,2048]{3,2,1,0:T(8,128)S(1)}, f32[2,2,32,2048]{3,2,1,0:T(8,128)}, u32[]{:S(2)}) copy-start(f32[2,2,32,2048]{3,2,1,0:T(8,128)} %state_ref.7) | copy-start | bytes 3145732
  35.0 7.0 %collective-permute-start.4 = (f32[2,256,128]{2,1,0:T(8,128)S(1)}, f32[2,256,128]{2,1,0:T(8,128)S(1)}, u32[]{:S(2)}, u32[]{:S(2)}) collective-permute-start(f32[2,256,128]{2,1,0:T(8,128)S(1)} %get-tuple-element.44), channel_id=1, source_target_pairs={{0,16},{16,32},{32,48},{48,64},{64,80},{80,96},{96,112},{112,0},{1... | collective-permute-start | bytes 786440 | tf_op jit(solution)/shard_map/ppermute | solution.py:538
  42.9 1.3 %collective-permute-start.6 = (f32[16,128]{1,0:T(8,128)S(1)}, f32[16,128]{1,0:T(8,128)S(1)}, u32[]{:S(2)}, u32[]{:S(2)}) collective-permute-start(f32[16,128]{1,0:T(8,128)S(1)} %get-tuple-element.54), channel_id=1, source_target_pairs={{0,16},{16,0},{32,48},{48,32},{64,80},{80,64},{96,112},{112,96},{1... | collective-permute-start | bytes 24584 | tf_op jit(solution)/shard_map/ppermute | solution.py:547
  44.1 3.7 %collective-permute-start.7 = (f32[16,128]{1,0:T(8,128)S(1)}, f32[16,128]{1,0:T(8,128)S(1)}, u32[]{:S(2)}, u32[]{:S(2)}) collective-permute-start(f32[16,128]{1,0:T(8,128)S(1)} %add.21), channel_id=1, source_target_pairs={{0,32},{16,48},{32,0},{48,16},{64,96},{80,112},{96,64},{112,80},{1... | collective-permute-start | bytes 24584 | tf_op jit(solution)/shard_map/ppermute | solution.py:547
  47.8 4.9 %collective-permute-start.8 = (f32[16,128]{1,0:T(8,128)S(1)}, f32[16,128]{1,0:T(8,128)S(1)}, u32[]{:S(2)}, u32[]{:S(2)}) collective-permute-start(f32[16,128]{1,0:T(8,128)S(1)} %add.22), channel_id=1, source_target_pairs={{0,96},{16,112},{32,64},{48,80},{64,32},{80,48},{96,0},{112,16},{1... | collective-permute-start | bytes 24584 | tf_op jit(solution)/shard_map/ppermute | solution.py:547
  52.6 3.7 %collective-permute-start.9 = (f32[16,128]{1,0:T(8,128)S(1)}, f32[16,128]{1,0:T(8,128)S(1)}, u32[]{:S(2)}, u32[]{:S(2)}) collective-permute-start(f32[16,128]{1,0:T(8,128)S(1)} %add.23), channel_id=1, source_target_pairs={{0,1},{1,0},{2,3},{3,2},{4,5},{5,4},{6,7},{7,6},{8,9},{9,8},{10,11... | collective-permute-start | bytes 24584 | tf_op jit(solution)/shard_map/ppermute | solution.py:547
  56.3 4.9 %collective-permute-start.10 = (f32[16,128]{1,0:T(8,128)S(1)}, f32[16,128]{1,0:T(8,128)S(1)}, u32[]{:S(2)}, u32[]{:S(2)}) collective-permute-start(f32[16,128]{1,0:T(8,128)S(1)} %add.24), channel_id=1, source_target_pairs={{0,3},{1,2},{2,1},{3,0},{4,7},{5,6},{6,5},{7,4},{8,11},{9,10},{10,... | collective-permute-start | bytes 24584 | tf_op jit(solution)/shard_map/ppermute | solution.py:547
  61.2 3.7 %collective-permute-start.11 = (f32[16,128]{1,0:T(8,128)S(1)}, f32[16,128]{1,0:T(8,128)S(1)}, u32[]{:S(2)}, u32[]{:S(2)}) collective-permute-start(f32[16,128]{1,0:T(8,128)S(1)} %add.25), channel_id=1, source_target_pairs={{0,4},{1,5},{2,6},{3,7},{4,0},{5,1},{6,2},{7,3},{8,12},{9,13},{10,... | collective-permute-start | bytes 24584 | tf_op jit(solution)/shard_map/ppermute | solution.py:547
  64.8 4.9 %collective-permute-start.12 = (f32[16,128]{1,0:T(8,128)S(1)}, f32[16,128]{1,0:T(8,128)S(1)}, u32[]{:S(2)}, u32[]{:S(2)}) collective-permute-start(f32[16,128]{1,0:T(8,128)S(1)} %add.26), channel_id=1, source_target_pairs={{0,12},{1,13},{2,14},{3,15},{4,8},{5,9},{6,10},{7,11},{8,4},{9,5},... | collective-permute-start | bytes 24584 | tf_op jit(solution)/shard_map/ppermute | solution.py:547

commit v3 on v2

--- a/solution.py
+++ b/solution.py
@@ -455,9 +455,12 @@
         )
         copy.start()
         copies.append(copy)
-    rows = [jnp.sum(one, axis=0, keepdims=True) for one in sums]
-    rows.append(jnp.zeros((16 - len(rows), LANE), f32))
-    sums_ref[...] = jnp.concatenate(rows, axis=0)
+    lane = lax.broadcasted_iota(jnp.int32, (8, LANE), 1)
+    row = jnp.zeros((8, LANE), f32)
+    for i, one in enumerate(sums):
+        row = jnp.where(lane == i, jnp.sum(jnp.sum(one, axis=0, keepdims=True), axis=1, keepdims=True), row)
+    for i in range(sums_ref.shape[0] // 8):
+        sums_ref[pl.ds(8 * i, 8), :] = row
     for copy in copies:
         copy.wait()
 
@@ -476,10 +479,10 @@
     )(state, wet, basis, head, middle, tail, came)
 
 
-def late(state, wet, basis, came, sums, residual):
+def late(devices, state, wet, basis, came, sums, residual):
     return pl.pallas_call(
         late_kernel,
-        out_shape=(shape(SEGS, TRACERS, LEV, WIDTH), shape(16, LANE), shape(2, TRACERS, LEV, HALO)),
+        out_shape=(shape(SEGS, TRACERS, LEV, WIDTH), shape(devices, LANE), shape(2, TRACERS, LEV, HALO)),
         in_specs=[VMEM] * 5 + [HBM],
         out_specs=(HBM, VMEM, VMEM),
         scratch_shapes=[pltpu.SemaphoreType.DMA((2,))],
@@ -491,8 +494,8 @@
 
 
 def scaled_kernel(count, residual_ref, pieces_ref, basis_ref, sums_ref, new_ref, coefficients_ref):
-    sums = jnp.sum(sums_ref[...], axis=1, keepdims=True)
-    one = [sums[i : i + 1] for i in range(16)]
+    sums = jnp.sum(sums_ref[...], axis=0, keepdims=True)
+    one = [sums[:, i : i + 1] for i in range(BASIS + 1 + len(PAIRS))]
     first, square, products = one[:BASIS], one[BASIS], iter(one[BASIS + 1 :])
     gram = [[None] * BASIS for _ in range(BASIS)]
     for i in range(BASIS):
@@ -538,20 +541,6 @@
     return lax.ppermute(block, axis, [(i, (i + distance) % count) for i in range(count)])
 
 
-def summed_everywhere(value):
-    for axis in ("seg", "col"):
-        count = lax.axis_size(axis)
-        done = 1
-        while done < count:
-            flip = done if done in (1, 2, 4, 8) else done
-            value = value + lax.ppermute(value, axis, [(i, i ^ FLIPS[axis][flip]) for i in range(count)])
-            done *= 2
-    return value
-
-
-FLIPS = {"seg": {1: 1, 2: 2, 4: 6}, "col": {1: 1, 2: 3, 4: 4, 8: 12}}
-
-
 def per_device(segment_state, light, mixing, kappa, neighbour_columns, wet_levels, basis):
     every_column = lax.axis_size("col") * WIDTH
     state = pltpu.with_memory_space_constraint(segment_state, pltpu.VMEM)
@@ -571,9 +560,11 @@
     head, tail, sent = edges(False, every_column, left, right, table, mixing, edge, factors)
     came_edge = shifted(sent, "seg", 1)
     residual, held, sums = early(state, wet, basis, head, end_middle, tail, came_middle)
-    residual, sums, pieces = late(state, wet, basis, came_edge, sums, residual)
+    devices = lax.axis_size("seg") * lax.axis_size("col")
+    residual, sums, pieces = late(devices, state, wet, basis, came_edge, sums, residual)
+    sums = lax.all_to_all(sums, ("seg", "col"), 0, 0, tiled=True)
     count = lax.axis_size("seg") * SEGS * TRACERS * LEV * every_column
-    new_vector, coefficients = scaled(count, held, pieces, basis, summed_everywhere(sums))
+    new_vector, coefficients = scaled(count, held, pieces, basis, sums)
     return (residual, new_vector, coefficients[0, : BASIS + 1])
 
 

time: 71.9 us -> 61.7 us (0.86)
  waiting for transfers between devices: 28.1 us -> 3.81 us
  blocking collectives: 0 us -> 15.6 us
  starting transfers between devices: 16.1 us -> 13.6 us
    ppermute x7 -> x0, waiting for transfers between devices: 24.3 us -> none  [summed_everywhere(): lax.ppermute(value, axis, [(i, i ^ FLIPS[axis][flip]) for i in range(coun...]
    all_to_all x0 -> x1, blocking collectives: none -> 15.6 us  [per_device(): sums = lax.all_to_all(sums, ('seg', 'col'), 0, 0, tiled=True)]
    ppermute x7 -> x0, starting transfers between devices: 2.5 us -> none  [summed_everywhere(): lax.ppermute(value, axis, [(i, i ^ FLIPS[axis][flip]) for i in range(coun...]
  transfers between devices with their start and end apart: 13 -> 6, of which waited for: 9 -> 2; matrix products, arithmetic and copies ran while one was open for 0% -> 0% of each run, Pallas kernels for 29% -> 34%
where the time goes in v3:
time: 61.7 us; the launch traced here: 61.1 us
  Pallas kernels  25.6 us (41%)
  blocking collectives  15.6 us (25%)
  starting transfers between devices  13.6 us (22%)
  waiting for transfers between devices  3.81 us (6%)
  local copies, waits for them, and re-layouts  1.74 us (3%)
  between operations  0.76 us (1%)
    all_to_all x1, blocking collectives, per_device(): sums = lax.all_to_all(sums, ('seg', 'col'), 0, 0, tiled=True)  15.6 us
    pallas_call x6, Pallas kernels, call(): pl.pallas_call(kernel, out_shape=outs, in_specs=[VMEM] * len(operands), o...  14 us
    ppermute x6, starting transfers between devices, shifted(): lax.ppermute(block, axis, [(i, (i + distance) % count) for i in range(cou...  13.6 us
    pallas_call x1, Pallas kernels, first_own(): pl.pallas_call(functools.partial(first_own_kernel, every_column), out_sha...  9.28 us
    ppermute x6, waiting for transfers between devices, shifted(): lax.ppermute(block, axis, [(i, (i + distance) % count) for i in range(cou...  3.81 us
    pallas_call x1, Pallas kernels, early(): pl.pallas_call(early_kernel, out_shape=(whole, whole, shape(BASIS + 1 + l...  1.53 us
  transfers between devices with their start and end apart: 6, of which 2 were waited for; matrix products, arithmetic and copies ran while one was open for 0% of the time, Pallas kernels for 34%

profile of v3, /device:TPU:0, one launch (start us, length us, event | category | flops | bytes accessed | tf_op | source)
XLA Modules:
  0.0 61.1 jit_solution(1358340007366749993)
XLA Ops:
  0.6 0.0 copy-start.1
  0.6 1.2 %copy-done.1 = f32[2,2,32,2048]{3,2,1,0:T(8,128)S(1)} copy-done((f32[2,2,32,2048]{3,2,1,0:T(8,128)S(1)}, f32[2,2,32,2048]{3,2,1,0:T(8,128)}, u32[]{:S(2)}) %copy-start.1) | copy-done | bytes 1048600
  1.9 2.1 %collective-permute-start = (f32[2,2,32,512]{3,2,1,0:T(8,128)S(1)}, f32[2,2,32,512]{3,2,1,0:T(8,128)S(1)}, u32[]{:S(2)}, u32[]{:S(2)}) collective-permute-start(f32[2,2,32,512]{3,2,1,0:T(8,128)S(1)} %get-tuple-element.31), channel_id=1, source_target_pairs={{0,1},{1,2},{2,3},{3,4},{4,5},{5,6},{6,7},{7,8},{8,9},{9,10},{10,1... | collective-permute-start | bytes 786440 | tf_op jit(solution)/shard_map/ppermute | solution.py:541
  4.0 4.4 %collective-permute-start.1 = (f32[2,2,32,512]{3,2,1,0:T(8,128)S(1)}, f32[2,2,32,512]{3,2,1,0:T(8,128)S(1)}, u32[]{:S(2)}, u32[]{:S(2)}) collective-permute-start(f32[2,2,32,512]{3,2,1,0:T(8,128)S(1)} %get-tuple-element.32), channel_id=1, source_target_pairs={{0,15},{1,0},{2,1},{3,2},{4,3},{5,4},{6,5},{7,6},{8,7},{9,8},{10,9... | collective-permute-start | bytes 786440 | tf_op jit(solution)/shard_map/ppermute | solution.py:541
  8.4 9.3 %first_step_own.1 = (f32[2,512,128]{2,1,0:T(8,128)S(1)}, f32[2,512,128]{2,1,0:T(8,128)S(1)}, f32[4,32,8,128]{3,2,1,0:T(8,128)S(1)}, f32[4,32,8,128]{3,2,1,0:T(8,...) custom-call(f32[2,2,32,2048]{3,2,1,0:T(8,128)S(1)} %copy-done.1, ...), custom_call_target="tpu_custom_call" | custom-call | flops 6000000000 | bytes 4000000 | tf_op jit(solution)/shard_map/first_step_own/pallas_call | solution.py:334
  17.7 0.0 collective-permute-done.left_ref
  17.7 0.0 collective-permute-done.1.right_ref
  17.7 2.0 %first_step_edges.1 = (f32[1,512,128]{2,1,0:T(8,128)S(1)}, f32[1,512,128]{2,1,0:T(8,128)S(1)}) custom-call(f32[2,2,32,512]{3,2,1,0:T(8,128)S(1)} %collective-permute-done.left_ref, f32[2,2,32,512]{3,2,1,0:T(8,128)S(1)} %collective-permute-done.1.right_ref, s32[6,2048]{1,0:T(8,128)S(1)} %get-tuple-element.33.table_ref, ...), custom_call_target="tpu_custom_call" | custom-call | flops 1000000000 | bytes 4000000 | tf_op jit(solution)/shard_map/first_step_edges/pallas_call | solution.py:319
  19.7 0.1 collective-permute-start.2
  19.8 5.3 %collective-permute-start.3 = (f32[1,512,128]{2,1,0:T(8,128)S(1)}, f32[1,512,128]{2,1,0:T(8,128)S(1)}, u32[]{:S(2)}, u32[]{:S(2)}) collective-permute-start(f32[1,512,128]{2,1,0:T(8,128)S(1)} %get-tuple-element.40.head_ref), channel_id=1, source_target_pairs={{0,15},{1,0},{2,1},{3,2},{4,3},{5,4},{6,5},{7,6},{8,7},{9,8},{10,9... | collective-permute-start | bytes 786440 | tf_op jit(solution)/shard_map/ppermute | solution.py:541
  25.1 4.7 %second_step_middle.1 = (f32[2,512,128]{2,1,0:T(8,128)S(1)}, f32[2,256,128]{2,1,0:T(8,128)S(1)}, bf16[8,256,256]{2,1,0:T(8,128)(2,1)S(1)}) custom-call(f32[1,512,128]{2,1,0:T(8,128)S(1)} %get-tuple-element.40.head_ref, f32[2,512,128]{2,1,0:T(8,128)S(1)} %get-tuple-element.41.middle_in_ref.middle_ref, f32[1,512,128]{2,1,0:T(8,128)S(1)} %get-tuple-element.39.tail_ref, ...), custom_call_target="tpu_custom_call" | custom-call | flops 3500000000 | bytes 4000000 | tf_op jit(solution)/shard_map/second_step_middle/pallas_call | solution.py:319
  29.9 0.0 collective-permute-start.5
  29.9 3.0 %second_step_edges_own.1.edge_in_ref = f32[2,512,128]{2,1,0:T(8,128)S(1)} custom-call(f32[1,512,128]{2,1,0:T(8,128)S(1)} %get-tuple-element.40.head_ref, f32[2,512,128]{2,1,0:T(8,128)S(1)} %get-tuple-element.41.middle_in_ref.middle_ref, f32[1,512,128]{2,1,0:T(8,128)S(1)} %get-tuple-element.39.tail_ref, s32[6,2048]{1,0:T(8,128)S(1)} %get-tuple-element.33.table_ref, ...), custom_call_target="tpu_custom_call" | custom-call | flops 2500000000 | bytes 4000000 | tf_op jit(solution)/shard_map/second_step_edges_own/pallas_call | solution.py:319
  32.9 0.0 copy-start
  32.9 0.0 copy-start.2
  32.9 0.0 collective-permute-done.2.left_ref
  32.9 0.0 collective-permute-done.3.right_ref
  33.0 2.1 %second_step_edges.1 = (f32[1,512,128]{2,1,0:T(8,128)S(1)}, f32[1,512,128]{2,1,0:T(8,128)S(1)}, f32[2,256,128]{2,1,0:T(8,128)S(1)}) custom-call(f32[1,512,128]{2,1,0:T(8,128)S(1)} %collective-permute-done.2.left_ref, f32[1,512,128]{2,1,0:T(8,128)S(1)} %collective-permute-done.3.right_ref, s32[6,2048]{1,0:T(8,128)S(1)} %get-tuple-element.33.table_ref, ...), custom_call_target="tpu_custom_call" | custom-call | flops 1000000000 | bytes 4000000 | tf_op jit(solution)/shard_map/second_step_edges/pallas_call | solution.py:319
  35.0 1.7 %collective-permute-start.4 = (f32[2,256,128]{2,1,0:T(8,128)S(1)}, f32[2,256,128]{2,1,0:T(8,128)S(1)}, u32[]{:S(2)}, u32[]{:S(2)}) collective-permute-start(f32[2,256,128]{2,1,0:T(8,128)S(1)} %get-tuple-element.44), channel_id=1, source_target_pairs={{0,16},{16,32},{32,48},{48,64},{64,80},{80,96},{96,112},{112,0},{1... | collective-permute-start | bytes 786440 | tf_op jit(solution)/shard_map/ppermute | solution.py:541
  36.7 0.2 collective-permute-done.5.came_ref
  36.9 0.0 copy-done
  36.9 0.0 copy-done.2
  36.9 1.5 %residual_known.1 = (f32[2,2,32,2048]{3,2,1,0:T(8,128)}, f32[2,2,32,2048]{3,2,1,0:T(8,128)S(1)}, f32[15,8,128]{2,1,0:T(8,128)S(1)}) custom-call(f32[2,2,32,2048]{3,2,1,0:T(8,128)S(1)} %copy-done.2, s32[16,128]{1,0:T(8,128)S(1)} %get-tuple-element.30.wet_ref, f32[4,2,2,32,2048]{4,3,2,1,0:T(8,128)S(1)} %copy-done, ...), custom_call_target="tpu_custom_call" | custom-call | flops 10000000 | bytes 4000000 | tf_op jit(solution)/shard_map/residual_known/pallas_call | solution.py:470
  38.4 3.6 %collective-permute-done.4.came_ref = f32[2,256,128]{2,1,0:T(8,128)S(1)} collective-permute-done((f32[2,256,128]{2,1,0:T(8,128)S(1)}, f32[2,256,128]{2,1,0:T(8,128)S(1)}, u32[]{:S(2)}, u32[]{:S(2)}) %collective-permute-start.4) | collective-permute-done | bytes 262176 | tf_op jit(solution)/shard_map/ppermute | solution.py:541
  42.0 0.8 %residual_last.1 = (f32[2,2,32,2048]{3,2,1,0:T(8,128)}, f32[128,128]{1,0:T(8,128)S(1)}, f32[2,2,32,512]{3,2,1,0:T(8,128)S(1)}) custom-call(f32[2,2,32,2048]{3,2,1,0:T(8,128)S(1)} %copy-done.2, s32[16,128]{1,0:T(8,128)S(1)} %get-tuple-element.30.wet_ref, f32[4,2,2,32,2048]{4,3,2,1,0:T(8,128)S(1)} %copy-done, ...), custom_call_target="tpu_custom_call", output_to_operand_aliasing={{0}: (5, {})} | custom-call | flops 3000000 | bytes 4000000 | tf_op jit(solution)/shard_map/residual_last/pallas_call | solution.py:483
  42.9 15.6 %all_to_all.11 = f32[128,1,128]{2,1,0:T(1,128)S(1)} all-to-all(f32[128,1,128]{2,1,0:T(1,128)S(1)} %bitcast.9), channel_id=1, replica_groups=mesh['seg'=8,'col'=16] {'seg','col'}, dimensions={0} | all-to-all | bytes 131072 | tf_op jit(solution)/shard_map/all_to_all | solution.py:565
  58.5 2.1 %orthogonal_and_scaled.1 = (f32[2,2,32,2048]{3,2,1,0:T(8,128)}, f32[8,128]{1,0:T(8,128)S(1)}) custom-call(f32[2,2,32,2048]{3,2,1,0:T(8,128)S(1)} %get-tuple-element.52.residual_ref, f32[2,2,32,512]{3,2,1,0:T(8,128)S(1)} %get-tuple-element.53.pieces_ref, f32[4,2,2,32,2048]{4,3,2,1,0:T(8,128)S(1)} %copy-done, f32[128,128]{1,0:T(8,128)S(1)} %bitcast.8), custom_call_target="tpu_custom_call" | custom-call | flops 4000000 | bytes 4000000 | tf_op jit(solution)/shard_map/orthogonal_and_scaled/pallas_call | solution.py:319
  60.6 0.5 slice_bitcast_fusion
  (1 shorter events, 0.0 us)
Async XLA Ops:
  0.6 1.2 %copy-start.1 = (f32[2,2,32,2048]{3,2,1,0:T(8,128)S(1)}, f32[2,2,32,2048]{3,2,1,0:T(8,128)}, u32[]{:S(2)}) copy-start(f32[2,2,32,2048]{3,2,1,0:T(8,128)} %state_ref.7) | copy-start | bytes 3145732
  1.9 15.8 %collective-permute-start = (f32[2,2,32,512]{3,2,1,0:T(8,128)S(1)}, f32[2,2,32,512]{3,2,1,0:T(8,128)S(1)}, u32[]{:S(2)}, u32[]{:S(2)}) collective-permute-start(f32[2,2,32,512]{3,2,1,0:T(8,128)S(1)} %get-tuple-element.31), channel_id=1, source_target_pairs={{0,1},{1,2},{2,3},{3,4},{4,5},{5,6},{6,7},{7,8},{8,9},{9,10},{10,1... | collective-permute-start | bytes 786440 | tf_op jit(solution)/shard_map/ppermute | solution.py:541
  4.0 13.7 %collective-permute-start.1 = (f32[2,2,32,512]{3,2,1,0:T(8,128)S(1)}, f32[2,2,32,512]{3,2,1,0:T(8,128)S(1)}, u32[]{:S(2)}, u32[]{:S(2)}) collective-permute-start(f32[2,2,32,512]{3,2,1,0:T(8,128)S(1)} %get-tuple-element.32), channel_id=1, source_target_pairs={{0,15},{1,0},{2,1},{3,2},{4,3},{5,4},{6,5},{7,6},{8,7},{9,8},{10,9... | collective-permute-start | bytes 786440 | tf_op jit(solution)/shard_map/ppermute | solution.py:541
  19.7 13.2 %collective-permute-start.2 = (f32[1,512,128]{2,1,0:T(8,128)S(1)}, f32[1,512,128]{2,1,0:T(8,128)S(1)}, u32[]{:S(2)}, u32[]{:S(2)}) collective-permute-start(f32[1,512,128]{2,1,0:T(8,128)S(1)} %get-tuple-element.39.tail_ref), channel_id=1, source_target_pairs={{0,1},{1,2},{2,3},{3,4},{4,5},{5,6},{6,7},{7,8},{8,9},{9,10},{10,1... | collective-permute-start | bytes 786440 | tf_op jit(solution)/shard_map/ppermute | solution.py:541
  19.8 13.2 %collective-permute-start.3 = (f32[1,512,128]{2,1,0:T(8,128)S(1)}, f32[1,512,128]{2,1,0:T(8,128)S(1)}, u32[]{:S(2)}, u32[]{:S(2)}) collective-permute-start(f32[1,512,128]{2,1,0:T(8,128)S(1)} %get-tuple-element.40.head_ref), channel_id=1, source_target_pairs={{0,15},{1,0},{2,1},{3,2},{4,3},{5,4},{6,5},{7,6},{8,7},{9,8},{10,9... | collective-permute-start | bytes 786440 | tf_op jit(solution)/shard_map/ppermute | solution.py:541
  29.9 7.0 %collective-permute-start.5 = (f32[2,256,128]{2,1,0:T(8,128)S(1)}, f32[2,256,128]{2,1,0:T(8,128)S(1)}, u32[]{:S(2)}, u32[]{:S(2)}) collective-permute-start(f32[2,256,128]{2,1,0:T(8,128)S(1)} %get-tuple-element.48), channel_id=1, source_target_pairs={{0,16},{16,32},{32,48},{48,64},{64,80},{80,96},{96,112},{112,0},{1... | collective-permute-start | bytes 786440 | tf_op jit(solution)/shard_map/ppermute | solution.py:541
  32.9 4.0 %copy-start = (f32[4,2,2,32,2048]{4,3,2,1,0:T(8,128)S(1)}, f32[4,2,2,32,2048]{4,3,2,1,0:T(8,128)}, u32[]{:S(2)}) copy-start(f32[4,2,2,32,2048]{4,3,2,1,0:T(8,128)} %basis_ref.5) | copy-start | bytes 12582916
  32.9 4.0 %copy-start.2 = (f32[2,2,32,2048]{3,2,1,0:T(8,128)S(1)}, f32[2,2,32,2048]{3,2,1,0:T(8,128)}, u32[]{:S(2)}) copy-start(f32[2,2,32,2048]{3,2,1,0:T(8,128)} %state_ref.7) | copy-start | bytes 3145732
  35.0 7.0 %collective-permute-start.4 = (f32[2,256,128]{2,1,0:T(8,128)S(1)}, f32[2,256,128]{2,1,0:T(8,128)S(1)}, u32[]{:S(2)}, u32[]{:S(2)}) collective-permute-start(f32[2,256,128]{2,1,0:T(8,128)S(1)} %get-tuple-element.44), channel_id=1, source_target_pairs={{0,16},{16,32},{32,48},{48,64},{64,80},{80,96},{96,112},{112,0},{1... | collective-permute-start | bytes 786440 | tf_op jit(solution)/shard_map/ppermute | solution.py:541

commit v4 on v3

--- a/solution.py
+++ b/solution.py
@@ -47,7 +47,10 @@
     def read(seg, tracer, start):
         return ref[seg, tracer, :, pl.ds(start, TILE)]
 
-    return read
+    def one(seg, tracer, level, start):
+        return ref[seg, tracer, pl.ds(level, 8), pl.ds(start, LANE)]
+
+    return read, one
 
 
 def group_reader(refs):
@@ -57,7 +60,11 @@
         parts = [ref[place, pl.ds(group_row(tracer, chunk + h, seg), LEV), :] for h in range(TILE // LANE)]
         return jnp.concatenate(parts, axis=1)
 
-    return read
+    def one(seg, tracer, level, start):
+        ref, place = refs[start // HALO]
+        return ref[place, pl.ds(group_row(tracer, start % HALO // LANE, seg) + level, 8), :]
+
+    return read, one
 
 
 def split_tile(read, start, xs_ref, place):
@@ -76,7 +83,7 @@
     away = table_ref[pl.ds(k, 1), columns] - table_ref[pl.ds(0, 1), columns]
     away = jnp.where(away > HALO, away - every_column, away)
     away = jnp.where(away < -HALO, away + every_column, away)
-    return away + lax.broadcasted_iota(jnp.int32, (1, TILE), 1) + start
+    return away + lax.broadcasted_iota(jnp.int32, (1, TILE), 1)
 
 
 def picked(xs_ref, places, offsets, index):
@@ -89,10 +96,31 @@
     return total[:ROWS] + total[ROWS:]
 
 
-def moved_part(xs_ref, places, offsets, index_of, mixing_of):
+def gathered(one, chunks, index):
+    halves = []
+    for h in range(TILE // LANE):
+        at = jnp.broadcast_to(index[:, h * LANE : (h + 1) * LANE], (8, LANE))
+        lane = at & (LANE - 1)
+        usable = [(start, first) for start, first in chunks if abs(first - h * LANE) <= HALO]
+        chosen = [at - lane == first for _, first in usable]
+        rows = []
+        for seg in range(SEGS):
+            for tracer in range(TRACERS):
+                for level in range(0, LEV, 8):
+                    total = jnp.zeros((8, LANE), f32)
+                    for (start, _), here in zip(usable, chosen):
+                        value = jnp.take_along_axis(one(seg, tracer, level, start), lane, axis=1, mode="promise_in_bounds")
+                        total = jnp.where(here, value, total)
+                    rows.append(total)
+        halves.append(jnp.concatenate(rows, axis=0))
+    return jnp.concatenate(halves, axis=1)
+
+
+def moved_part(xs_ref, places, offsets, index_of, mixing_of, one, chunks, by_lane):
     total = [None] * (SEGS * TRACERS)
     for k in range(1, NBR):
-        value = picked(xs_ref, places, offsets, index_of(k))
+        index = index_of(k)
+        value = gathered(one, chunks, index) if k in by_lane else picked(xs_ref, places, offsets, index)
         for seg in range(SEGS):
             mix = mixing_of(seg, k)
             for tracer in range(TRACERS):
@@ -168,7 +196,8 @@
     return write
 
 
-def own_blocks(every_column, blocks, read, table_ref, mixing_ref, light_ref, xs_ref, acc_ref, places, ready=None):
+def own_blocks(every_column, blocks, readers, table_ref, mixing_ref, light_ref, xs_ref, acc_ref, places, ready=None):
+    read, one = readers
     for block in blocks:
         if ready is not None:
             ready(block)
@@ -177,9 +206,12 @@
         total = moved_part(
             xs_ref,
             tiles,
-            [tile * TILE for tile in tiles],
+            [tile * TILE - start for tile in tiles],
             lambda k: table_row(every_column, table_ref, k, start),
             lambda seg, k: mixing_ref[seg, k, :, pl.ds(start, TILE)],
+            one,
+            [(tile * TILE + h, tile * TILE + h - start) for tile in tiles for h in range(0, TILE, LANE)],
+            by_lane(block),
         )
         for seg in range(SEGS):
             columns = pl.ds(start, TILE)
@@ -194,6 +226,10 @@
                 for h in range(TILE // LANE):
                     row = group_row(tracer, block % 2 * 2 + h, seg)
                     acc_ref[places[block // 2], pl.ds(row, LEV), :] = result[:, h * LANE : (h + 1) * LANE]
+
+
+def by_lane(block):
+    return (4, 5) if block % 2 else (5,)
 
 
 EDGE_BLOCKS = (0, 1, BLOCKS - 2, BLOCKS - 1)
@@ -235,7 +271,7 @@
         copy.start()
     read = natural_reader(state_ref)
     for tile in range(BLOCKS):
-        split_tile(read, tile * TILE, xs_ref, tile)
+        split_tile(read[0], tile * TILE, xs_ref, tile)
 
     def ready(block):
         if block == 0:
@@ -265,7 +301,7 @@
 ):
     read = second_reader(head_ref, middle_in_ref, tail_ref)
     for tile in range(BLOCKS):
-        split_tile(read, tile * TILE, xs_ref, tile)
+        split_tile(read[0], tile * TILE, xs_ref, tile)
     own_blocks(every_column, MIDDLE_BLOCKS, read, table_ref, mixing_ref, light_ref, xs_ref, acc_ref, MIDDLE_PLACES)
     for group, place in MIDDLE_PLACES.items():
         solve(acc_ref, place, inverse_ref, carry_ref, ratio_ref, group, into_group(middle_ref, place))
@@ -282,10 +318,11 @@
     *outs_and_scratch,
 ):
     head_ref, tail_ref, *sent, xs_ref, acc_ref = outs_and_scratch
+    readers = []
     for side, ref in enumerate((left_ref, right_ref)):
-        read = natural_reader(ref) if first else group_reader([(ref, 0)])
+        readers.append(natural_reader(ref) if first else group_reader([(ref, 0)]))
         for tile in range(HALO // TILE):
-            split_tile(read, tile * TILE, xs_ref, side * 2 + tile)
+            split_tile(readers[side][0], tile * TILE, xs_ref, side * 2 + tile)
     uses = ((0, 0, (0, 1)), (1, 0, (1,)), (BLOCKS - 2, 1, (2,)), (BLOCKS - 1, 1, (2, 3)))
     offsets = (-HALO, -TILE, WIDTH, WIDTH + TILE)
     for block, side, places in uses:
@@ -293,9 +330,12 @@
         total = moved_part(
             xs_ref,
             places,
-            [offsets[place] for place in places],
+            [offsets[place] - start for place in places],
             lambda k: table_row(every_column, table_ref, k, start),
             lambda seg, k: mixing_ref[seg, k, :, pl.ds(start, TILE)],
+            readers[side][1],
+            [(place % 2 * TILE + h, offsets[place] + h - start) for place in places for h in range(0, TILE, LANE)],
+            by_lane(block),
         )
         for seg in range(SEGS):
             for tracer in range(TRACERS):
@@ -493,7 +533,7 @@
     )(state, wet, basis, came, sums, residual)
 
 
-def scaled_kernel(count, residual_ref, pieces_ref, basis_ref, sums_ref, new_ref, coefficients_ref):
+def scaled_kernel(count, residual_ref, pieces_ref, basis_ref, sums_ref, new_out_ref, coefficients_ref, new_ref, sems):
     sums = jnp.sum(sums_ref[...], axis=0, keepdims=True)
     one = [sums[:, i : i + 1] for i in range(BASIS + 1 + len(PAIRS))]
     first, square, products = one[:BASIS], one[BASIS], iter(one[BASIS + 1 :])
@@ -505,15 +545,16 @@
     both = [first[i] + second[i] for i in range(BASIS)]
     for i in range(BASIS):
         square = square - both[i] * (2.0 * first[i] - sum(gram[i][j] * both[j] for j in range(BASIS)))
-    spread = jnp.sqrt(square / count + epsilon)
+    spread = jnp.sqrt(jnp.maximum(square, 0.0) / count + epsilon)
     lane = lax.broadcasted_iota(jnp.int32, (8, LANE), 1)
     result = jnp.zeros((8, LANE), f32)
     for i, value in enumerate(both + [spread]):
         result = jnp.where(lane == i, value, result)
-    coefficients_ref[...] = result
+    coefficients_ref[...] = result[0, : BASIS + 1]
     scale = 1.0 / spread
     weights = [jnp.broadcast_to(-value * scale, (LEV, LANE)) for value in both]
     scale = jnp.broadcast_to(scale, (LEV, LANE))
+    copies = []
     for seg in range(SEGS):
         for tracer in range(TRACERS):
             for chunk in range(WIDTH // LANE):
@@ -527,13 +568,26 @@
                 for i in range(BASIS):
                     total = total + weights[i] * basis_ref[i, seg, tracer, :, lanes]
                 new_ref[seg, tracer, :, lanes] = total
+            at = seg * TRACERS + tracer
+            copy = pltpu.make_async_copy(new_ref.at[seg, tracer], new_out_ref.at[seg, tracer], sems.at[at])
+            copy.start()
+            copies.append(copy)
+    for copy in copies:
+        copy.wait()
 
 
 def scaled(count, residual, pieces, basis, sums):
-    return call(
-        functools.partial(scaled_kernel, count), "orthogonal_and_scaled", 4_000_000,
-        (shape(SEGS, TRACERS, LEV, WIDTH), shape(8, LANE)), [], residual, pieces, basis, sums,
-    )
+    whole = (SEGS, TRACERS, LEV, WIDTH)
+    return pl.pallas_call(
+        functools.partial(scaled_kernel, count),
+        out_shape=(shape(*whole), shape(BASIS + 1)),
+        in_specs=[VMEM] * 4,
+        out_specs=(HBM, VMEM),
+        scratch_shapes=[pltpu.VMEM(whole, f32), pltpu.SemaphoreType.DMA((SEGS * TRACERS,))],
+        compiler_params=PARAMS,
+        cost_estimate=pl.CostEstimate(flops=4_000_000, bytes_accessed=4_000_000, transcendentals=0),
+        name="orthogonal_and_scaled",
+    )(residual, pieces, basis, sums)
 
 
 def shifted(block, axis, distance):
@@ -565,7 +619,7 @@
     sums = lax.all_to_all(sums, ("seg", "col"), 0, 0, tiled=True)
     count = lax.axis_size("seg") * SEGS * TRACERS * LEV * every_column
     new_vector, coefficients = scaled(count, held, pieces, basis, sums)
-    return (residual, new_vector, coefficients[0, : BASIS + 1])
+    return (residual, new_vector, coefficients)
 
 
 def solution(mesh):

time: 61.7 us -> 59.9 us (0.971)
  Pallas kernels: 25.6 us -> 22.7 us
  blocking collectives: 15.6 us -> 17.1 us
    pallas_call x6 -> x5, Pallas kernels: 14 us -> 9.96 us  [call(): pl.pallas_call(kernel, out_shape=outs, in_specs=[VMEM] * len(operands), o...]
    pallas_call x0 -> x1, Pallas kernels: none -> 2.37 us  [scaled(): pl.pallas_call(functools.partial(scaled_kernel, count), out_shape=(shape(...]
    all_to_all x1, blocking collectives: 15.6 us -> 17.1 us  [per_device(): sums = lax.all_to_all(sums, ('seg', 'col'), 0, 0, tiled=True)]
    pallas_call x1, Pallas kernels: 9.28 us -> 8 us  [first_own(): pl.pallas_call(functools.partial(first_own_kernel, every_column), out_sha...]
  transfers between devices with their start and end apart: 6 -> 6, of which waited for: 2 -> 2; matrix products, arithmetic and copies ran while one was open for 0% -> 0% of each run, Pallas kernels for 34% -> 30%
where the time goes in v4:
time: 59.9 us; the launch traced here: 59.3 us
  Pallas kernels  22.7 us (38%)
  blocking collectives  17.1 us (29%)
  starting transfers between devices  13.6 us (23%)
  waiting for transfers between devices  3.8 us (6%)
  local copies, waits for them, and re-layouts  1.23 us (2%)
  between operations  0.92 us (2%)
    all_to_all x1, blocking collectives, per_device(): sums = lax.all_to_all(sums, ('seg', 'col'), 0, 0, tiled=True)  17.1 us
    ppermute x6, starting transfers between devices, shifted(): lax.ppermute(block, axis, [(i, (i + distance) % count) for i in range(cou...  13.6 us
    pallas_call x5, Pallas kernels, call(): pl.pallas_call(kernel, out_shape=outs, in_specs=[VMEM] * len(operands), o...  9.96 us
    pallas_call x1, Pallas kernels, first_own(): pl.pallas_call(functools.partial(first_own_kernel, every_column), out_sha...  8 us
    ppermute x6, waiting for transfers between devices, shifted(): lax.ppermute(block, axis, [(i, (i + distance) % count) for i in range(cou...  3.8 us
    pallas_call x1, Pallas kernels, scaled(): pl.pallas_call(functools.partial(scaled_kernel, count), out_shape=(shape(...  2.37 us
    pallas_call x1, Pallas kernels, early(): pl.pallas_call(early_kernel, out_shape=(whole, whole, shape(BASIS + 1 + l...  1.53 us
    unnamed x6, local copies, waits for them, and re-layouts  1.23 us
  transfers between devices with their start and end apart: 6, of which 2 were waited for; matrix products, arithmetic and copies ran while one was open for 0% of the time, Pallas kernels for 30%

profile of v4, /device:TPU:0, one launch (start us, length us, event | category | flops | bytes accessed | tf_op | source)
XLA Modules:
  0.0 59.3 jit_solution(10455586119588512679)
XLA Ops:
  0.6 0.0 copy-start.1
  0.6 1.2 %copy-done.1 = f32[2,2,32,2048]{3,2,1,0:T(8,128)S(1)} copy-done((f32[2,2,32,2048]{3,2,1,0:T(8,128)S(1)}, f32[2,2,32,2048]{3,2,1,0:T(8,128)}, u32[]{:S(2)}) %copy-start.1) | copy-done | bytes 1048600
  1.9 2.1 %collective-permute-start = (f32[2,2,32,512]{3,2,1,0:T(8,128)S(1)}, f32[2,2,32,512]{3,2,1,0:T(8,128)S(1)}, u32[]{:S(2)}, u32[]{:S(2)}) collective-permute-start(f32[2,2,32,512]{3,2,1,0:T(8,128)S(1)} %get-tuple-element.31), channel_id=1, source_target_pairs={{0,1},{1,2},{2,3},{3,4},{4,5},{5,6},{6,7},{7,8},{8,9},{9,10},{10,1... | collective-permute-start | bytes 786440 | tf_op jit(solution)/shard_map/ppermute | solution.py:595
  4.0 4.4 %collective-permute-start.1 = (f32[2,2,32,512]{3,2,1,0:T(8,128)S(1)}, f32[2,2,32,512]{3,2,1,0:T(8,128)S(1)}, u32[]{:S(2)}, u32[]{:S(2)}) collective-permute-start(f32[2,2,32,512]{3,2,1,0:T(8,128)S(1)} %get-tuple-element.32), channel_id=1, source_target_pairs={{0,15},{1,0},{2,1},{3,2},{4,3},{5,4},{6,5},{7,6},{8,7},{9,8},{10,9... | collective-permute-start | bytes 786440 | tf_op jit(solution)/shard_map/ppermute | solution.py:595
  8.4 8.0 %first_step_own.1 = (f32[2,512,128]{2,1,0:T(8,128)S(1)}, f32[2,512,128]{2,1,0:T(8,128)S(1)}, f32[4,32,8,128]{3,2,1,0:T(8,128)S(1)}, f32[4,32,8,128]{3,2,1,0:T(8,...) custom-call(f32[2,2,32,2048]{3,2,1,0:T(8,128)S(1)} %copy-done.1, ...), custom_call_target="tpu_custom_call" | custom-call | flops 6000000000 | bytes 4000000 | tf_op jit(solution)/shard_map/first_step_own/pallas_call | solution.py:374
  16.4 0.0 collective-permute-done.left_ref
  16.4 0.0 collective-permute-done.1.right_ref
  16.4 1.8 %first_step_edges.1 = (f32[1,512,128]{2,1,0:T(8,128)S(1)}, f32[1,512,128]{2,1,0:T(8,128)S(1)}) custom-call(f32[2,2,32,512]{3,2,1,0:T(8,128)S(1)} %collective-permute-done.left_ref, f32[2,2,32,512]{3,2,1,0:T(8,128)S(1)} %collective-permute-done.1.right_ref, s32[6,2048]{1,0:T(8,128)S(1)} %get-tuple-element.33.table_ref, ...), custom_call_target="tpu_custom_call" | custom-call | flops 1000000000 | bytes 4000000 | tf_op jit(solution)/shard_map/first_step_edges/pallas_call | solution.py:359
  18.2 0.1 collective-permute-start.2
  18.3 5.3 %collective-permute-start.3 = (f32[1,512,128]{2,1,0:T(8,128)S(1)}, f32[1,512,128]{2,1,0:T(8,128)S(1)}, u32[]{:S(2)}, u32[]{:S(2)}) collective-permute-start(f32[1,512,128]{2,1,0:T(8,128)S(1)} %get-tuple-element.40.head_ref), channel_id=1, source_target_pairs={{0,15},{1,0},{2,1},{3,2},{4,3},{5,4},{6,5},{7,6},{8,7},{9,8},{10,9... | collective-permute-start | bytes 786440 | tf_op jit(solution)/shard_map/ppermute | solution.py:595
  23.6 3.9 %second_step_middle.1 = (f32[2,512,128]{2,1,0:T(8,128)S(1)}, f32[2,256,128]{2,1,0:T(8,128)S(1)}, bf16[8,256,256]{2,1,0:T(8,128)(2,1)S(1)}) custom-call(f32[1,512,128]{2,1,0:T(8,128)S(1)} %get-tuple-element.40.head_ref, f32[2,512,128]{2,1,0:T(8,128)S(1)} %get-tuple-element.41.middle_in_ref.middle_ref, f32[1,512,128]{2,1,0:T(8,128)S(1)} %get-tuple-element.39.tail_ref, ...), custom_call_target="tpu_custom_call" | custom-call | flops 3500000000 | bytes 4000000 | tf_op jit(solution)/shard_map/second_step_middle/pallas_call | solution.py:359
  27.5 0.0 collective-permute-start.5
  27.6 2.4 %second_step_edges_own.1.edge_in_ref = f32[2,512,128]{2,1,0:T(8,128)S(1)} custom-call(f32[1,512,128]{2,1,0:T(8,128)S(1)} %get-tuple-element.40.head_ref, f32[2,512,128]{2,1,0:T(8,128)S(1)} %get-tuple-element.41.middle_in_ref.middle_ref, f32[1,512,128]{2,1,0:T(8,128)S(1)} %get-tuple-element.39.tail_ref, s32[6,2048]{1,0:T(8,128)S(1)} %get-tuple-element.33.table_ref, ...), custom_call_target="tpu_custom_call" | custom-call | flops 2500000000 | bytes 4000000 | tf_op jit(solution)/shard_map/second_step_edges_own/pallas_call | solution.py:359
  29.9 0.0 copy-start
  29.9 0.0 copy-start.2
  30.0 0.0 collective-permute-done.2.left_ref
  30.0 0.0 collective-permute-done.3.right_ref
  30.0 1.8 %second_step_edges.1 = (f32[1,512,128]{2,1,0:T(8,128)S(1)}, f32[1,512,128]{2,1,0:T(8,128)S(1)}, f32[2,256,128]{2,1,0:T(8,128)S(1)}) custom-call(f32[1,512,128]{2,1,0:T(8,128)S(1)} %collective-permute-done.2.left_ref, f32[1,512,128]{2,1,0:T(8,128)S(1)} %collective-permute-done.3.right_ref, s32[6,2048]{1,0:T(8,128)S(1)} %get-tuple-element.33.table_ref, ...), custom_call_target="tpu_custom_call" | custom-call | flops 1000000000 | bytes 4000000 | tf_op jit(solution)/shard_map/second_step_edges/pallas_call | solution.py:359
  31.8 1.7 %collective-permute-start.4 = (f32[2,256,128]{2,1,0:T(8,128)S(1)}, f32[2,256,128]{2,1,0:T(8,128)S(1)}, u32[]{:S(2)}, u32[]{:S(2)}) collective-permute-start(f32[2,256,128]{2,1,0:T(8,128)S(1)} %get-tuple-element.44), channel_id=1, source_target_pairs={{0,16},{16,32},{32,48},{48,64},{64,80},{80,96},{96,112},{112,0},{1... | collective-permute-start | bytes 786440 | tf_op jit(solution)/shard_map/ppermute | solution.py:595
  33.5 1.0 %collective-permute-done.5.came_ref = f32[2,256,128]{2,1,0:T(8,128)S(1)} collective-permute-done((f32[2,256,128]{2,1,0:T(8,128)S(1)}, f32[2,256,128]{2,1,0:T(8,128)S(1)}, u32[]{:S(2)}, u32[]{:S(2)}) %collective-permute-start.5) | collective-permute-done | bytes 262176 | tf_op jit(solution)/shard_map/ppermute | solution.py:595
  34.6 0.0 copy-done
  34.6 0.0 copy-done.2
  34.6 1.5 %residual_known.1 = (f32[2,2,32,2048]{3,2,1,0:T(8,128)}, f32[2,2,32,2048]{3,2,1,0:T(8,128)S(1)}, f32[15,8,128]{2,1,0:T(8,128)S(1)}) custom-call(f32[2,2,32,2048]{3,2,1,0:T(8,128)S(1)} %copy-done.2, s32[16,128]{1,0:T(8,128)S(1)} %get-tuple-element.30.wet_ref, f32[4,2,2,32,2048]{4,3,2,1,0:T(8,128)S(1)} %copy-done, ...), custom_call_target="tpu_custom_call" | custom-call | flops 10000000 | bytes 4000000 | tf_op jit(solution)/shard_map/residual_known/pallas_call | solution.py:510
  36.1 2.7 %collective-permute-done.4.came_ref = f32[2,256,128]{2,1,0:T(8,128)S(1)} collective-permute-done((f32[2,256,128]{2,1,0:T(8,128)S(1)}, f32[2,256,128]{2,1,0:T(8,128)S(1)}, u32[]{:S(2)}, u32[]{:S(2)}) %collective-permute-start.4) | collective-permute-done | bytes 262176 | tf_op jit(solution)/shard_map/ppermute | solution.py:595
  38.9 0.8 %residual_last.1 = (f32[2,2,32,2048]{3,2,1,0:T(8,128)}, f32[128,128]{1,0:T(8,128)S(1)}, f32[2,2,32,512]{3,2,1,0:T(8,128)S(1)}) custom-call(f32[2,2,32,2048]{3,2,1,0:T(8,128)S(1)} %copy-done.2, s32[16,128]{1,0:T(8,128)S(1)} %get-tuple-element.30.wet_ref, f32[4,2,2,32,2048]{4,3,2,1,0:T(8,128)S(1)} %copy-done, ...), custom_call_target="tpu_custom_call", output_to_operand_aliasing={{0}: (5, {})} | custom-call | flops 3000000 | bytes 4000000 | tf_op jit(solution)/shard_map/residual_last/pallas_call | solution.py:523
  39.7 17.1 %all_to_all.11 = f32[128,1,128]{2,1,0:T(1,128)S(1)} all-to-all(f32[128,1,128]{2,1,0:T(1,128)S(1)} %bitcast.7), channel_id=1, replica_groups=mesh['seg'=8,'col'=16] {'seg','col'}, dimensions={0} | all-to-all | bytes 131072 | tf_op jit(solution)/shard_map/all_to_all | solution.py:619
  56.8 2.4 %orthogonal_and_scaled.1 = (f32[2,2,32,2048]{3,2,1,0:T(8,128)}, f32[5]{0:T(128)}) custom-call(f32[2,2,32,2048]{3,2,1,0:T(8,128)S(1)} %get-tuple-element.52.residual_ref, f32[2,2,32,512]{3,2,1,0:T(8,128)S(1)} %get-tuple-element.53.pieces_ref, f32[4,2,2,32,2048]{4,3,2,1,0:T(8,128)S(1)} %copy-done, f32[128,128]{1,0:T(8,128)S(1)} %bitcast.6), custom_call_target="tpu_custom_call" | custom-call | flops 4000000 | bytes 4000000 | tf_op jit(solution)/shard_map/orthogonal_and_scaled/pallas_call | solution.py:581
  (1 shorter events, 0.0 us)
Async XLA Ops:
  0.6 1.2 %copy-start.1 = (f32[2,2,32,2048]{3,2,1,0:T(8,128)S(1)}, f32[2,2,32,2048]{3,2,1,0:T(8,128)}, u32[]{:S(2)}) copy-start(f32[2,2,32,2048]{3,2,1,0:T(8,128)} %state_ref.7) | copy-start | bytes 3145732
  1.9 14.5 %collective-permute-start = (f32[2,2,32,512]{3,2,1,0:T(8,128)S(1)}, f32[2,2,32,512]{3,2,1,0:T(8,128)S(1)}, u32[]{:S(2)}, u32[]{:S(2)}) collective-permute-start(f32[2,2,32,512]{3,2,1,0:T(8,128)S(1)} %get-tuple-element.31), channel_id=1, source_target_pairs={{0,1},{1,2},{2,3},{3,4},{4,5},{5,6},{6,7},{7,8},{8,9},{9,10},{10,1... | collective-permute-start | bytes 786440 | tf_op jit(solution)/shard_map/ppermute | solution.py:595
  4.0 12.4 %collective-permute-start.1 = (f32[2,2,32,512]{3,2,1,0:T(8,128)S(1)}, f32[2,2,32,512]{3,2,1,0:T(8,128)S(1)}, u32[]{:S(2)}, u32[]{:S(2)}) collective-permute-start(f32[2,2,32,512]{3,2,1,0:T(8,128)S(1)} %get-tuple-element.32), channel_id=1, source_target_pairs={{0,15},{1,0},{2,1},{3,2},{4,3},{5,4},{6,5},{7,6},{8,7},{9,8},{10,9... | collective-permute-start | bytes 786440 | tf_op jit(solution)/shard_map/ppermute | solution.py:595
  18.2 11.7 %collective-permute-start.2 = (f32[1,512,128]{2,1,0:T(8,128)S(1)}, f32[1,512,128]{2,1,0:T(8,128)S(1)}, u32[]{:S(2)}, u32[]{:S(2)}) collective-permute-start(f32[1,512,128]{2,1,0:T(8,128)S(1)} %get-tuple-element.39.tail_ref), channel_id=1, source_target_pairs={{0,1},{1,2},{2,3},{3,4},{4,5},{5,6},{6,7},{7,8},{8,9},{9,10},{10,1... | collective-permute-start | bytes 786440 | tf_op jit(solution)/shard_map/ppermute | solution.py:595
  18.3 11.7 %collective-permute-start.3 = (f32[1,512,128]{2,1,0:T(8,128)S(1)}, f32[1,512,128]{2,1,0:T(8,128)S(1)}, u32[]{:S(2)}, u32[]{:S(2)}) collective-permute-start(f32[1,512,128]{2,1,0:T(8,128)S(1)} %get-tuple-element.40.head_ref), channel_id=1, source_target_pairs={{0,15},{1,0},{2,1},{3,2},{4,3},{5,4},{6,5},{7,6},{8,7},{9,8},{10,9... | collective-permute-start | bytes 786440 | tf_op jit(solution)/shard_map/ppermute | solution.py:595
  27.5 7.0 %collective-permute-start.5 = (f32[2,256,128]{2,1,0:T(8,128)S(1)}, f32[2,256,128]{2,1,0:T(8,128)S(1)}, u32[]{:S(2)}, u32[]{:S(2)}) collective-permute-start(f32[2,256,128]{2,1,0:T(8,128)S(1)} %get-tuple-element.48), channel_id=1, source_target_pairs={{0,16},{16,32},{32,48},{48,64},{64,80},{80,96},{96,112},{112,0},{1... | collective-permute-start | bytes 786440 | tf_op jit(solution)/shard_map/ppermute | solution.py:595
  29.9 4.6 %copy-start = (f32[4,2,2,32,2048]{4,3,2,1,0:T(8,128)S(1)}, f32[4,2,2,32,2048]{4,3,2,1,0:T(8,128)}, u32[]{:S(2)}) copy-start(f32[4,2,2,32,2048]{4,3,2,1,0:T(8,128)} %basis_ref.5) | copy-start | bytes 12582916
  29.9 4.6 %copy-start.2 = (f32[2,2,32,2048]{3,2,1,0:T(8,128)S(1)}, f32[2,2,32,2048]{3,2,1,0:T(8,128)}, u32[]{:S(2)}) copy-start(f32[2,2,32,2048]{3,2,1,0:T(8,128)} %state_ref.7) | copy-start | bytes 3145732
  31.8 7.0 %collective-permute-start.4 = (f32[2,256,128]{2,1,0:T(8,128)S(1)}, f32[2,256,128]{2,1,0:T(8,128)S(1)}, u32[]{:S(2)}, u32[]{:S(2)}) collective-permute-start(f32[2,256,128]{2,1,0:T(8,128)S(1)} %get-tuple-element.44), channel_id=1, source_target_pairs={{0,16},{16,32},{32,48},{48,64},{64,80},{80,96},{96,112},{112,0},{1... | collective-permute-start | bytes 786440 | tf_op jit(solution)/shard_map/ppermute | solution.py:595

commit v5 on v4

--- a/solution.py
+++ b/solution.py
@@ -196,11 +196,9 @@
     return write
 
 
-def own_blocks(every_column, blocks, readers, table_ref, mixing_ref, light_ref, xs_ref, acc_ref, places, ready=None):
+def own_blocks(every_column, blocks, readers, table_ref, mixing_ref, light_ref, xs_ref, acc_ref, places):
     read, one = readers
     for block in blocks:
-        if ready is not None:
-            ready(block)
         start = block * TILE
         tiles = list(range(max(0, block - 2), min(BLOCKS, block + 3)))
         total = moved_part(
@@ -246,46 +244,64 @@
             ]
 
 
-def halves_kernel(state_ref, head_ref, tail_ref):
+QUARTER = (slice(None), slice(None), slice(None), pl.ds(0, HALO))
+
+
+def halves_kernel(
+    state_in, table_in, light_in, mixing_in,
+    head_ref, tail_ref, state_ref, table_ref, light_ref, mixing_ref,
+    sems,
+):
+    pairs = [(state_in, state_ref), (table_in, table_ref), (light_in, light_ref), (mixing_in.at[QUARTER], mixing_ref)]
+    copies = [pltpu.make_async_copy(*pair, sems.at[i]) for i, pair in enumerate(pairs)]
+    for copy in copies:
+        copy.start()
+    copies[0].wait()
     head_ref[...] = state_ref[:, :, :, :HALO]
     tail_ref[...] = state_ref[:, :, :, WIDTH - HALO :]
-
-
-def halves(state):
+    for copy in copies[1:]:
+        copy.wait()
+
+
+def in_hbm(*arrays):
+    return [pltpu.with_memory_space_constraint(one, pltpu.HBM) for one in arrays]
+
+
+def halves(state, table, light, mixing):
     half = shape(SEGS, TRACERS, LEV, HALO)
-    return call(halves_kernel, "edge_columns", 0, (half, half), [], state)
+    like = [jax.ShapeDtypeStruct(one.shape, one.dtype) for one in (state, table, light)]
+    return pl.pallas_call(
+        halves_kernel,
+        out_shape=(half, half, *like, shape(SEGS, NBR, LEV, HALO)),
+        in_specs=[HBM] * 4,
+        out_specs=(VMEM,) * 6,
+        scratch_shapes=[pltpu.SemaphoreType.DMA((4,))],
+        compiler_params=PARAMS,
+        cost_estimate=pl.CostEstimate(flops=0, bytes_accessed=4_000_000, transcendentals=0),
+        name="edge_columns",
+    )(*in_hbm(state, table, light, mixing))
 
 
 def first_own_kernel(
-    every_column, state_ref, table_in, mixing_in, light_in, kappa_in, wet_in,
-    edge_ref, middle_ref, inverse_ref, carry_ref, ratio_ref, table_ref, mixing_ref, light_ref, wet_ref,
+    every_column, state_ref, table_ref, light_ref, quarter_ref, mixing_in, kappa_in, wet_in,
+    edge_ref, middle_ref, inverse_ref, carry_ref, ratio_ref, mixing_ref, wet_ref,
     xs_ref, acc_ref, by_rows_ref, kappa_ref, sems,
 ):
-    order = (0, GROUPS - 1) + tuple(range(1, GROUPS - 1))
+    order = (GROUPS - 1,) + tuple(range(1, GROUPS - 1)) + (0,)
     parts = [(slice(None),) * 3 + (pl.ds(group * HALO, HALO),) for group in order]
-    of_mixing = [(mixing_in.at[part], mixing_ref.at[part]) for part in parts]
-    pairs = [(table_in, table_ref), (light_in, light_ref), (kappa_in, kappa_ref), (wet_in, wet_ref)]
-    pairs = pairs[:2] + of_mixing[:1] + pairs[2:] + of_mixing[1:]
+    pairs = [(kappa_in, kappa_ref), (wet_in, wet_ref)] + [(mixing_in.at[part], mixing_ref.at[part]) for part in parts]
     copies = [pltpu.make_async_copy(*pair, sems.at[i]) for i, pair in enumerate(pairs)]
     for copy in copies:
         copy.start()
     read = natural_reader(state_ref)
     for tile in range(BLOCKS):
         split_tile(read[0], tile * TILE, xs_ref, tile)
-
-    def ready(block):
-        if block == 0:
-            for copy in copies[:3]:
-                copy.wait()
-        elif block == BLOCKS - 2:
-            copies[3].wait()
-            copies[4].wait()
-            factorize(kappa_ref, wet_ref, by_rows_ref, inverse_ref, carry_ref, ratio_ref)
-            for copy in copies[5:]:
-                copy.wait()
-
-    own_blocks(every_column, EDGE_BLOCKS, read, table_ref, mixing_ref, light_ref, xs_ref, edge_ref, EDGE_PLACES, ready)
-    own_blocks(every_column, MIDDLE_BLOCKS, read, table_ref, mixing_ref, light_ref, xs_ref, acc_ref, MIDDLE_PLACES, ready)
+    own_blocks(every_column, EDGE_BLOCKS[:2], read, table_ref, quarter_ref, light_ref, xs_ref, edge_ref, EDGE_PLACES)
+    for copy in copies:
+        copy.wait()
+    factorize(kappa_ref, wet_ref, by_rows_ref, inverse_ref, carry_ref, ratio_ref)
+    own_blocks(every_column, EDGE_BLOCKS[2:], read, table_ref, mixing_ref, light_ref, xs_ref, edge_ref, EDGE_PLACES)
+    own_blocks(every_column, MIDDLE_BLOCKS, read, table_ref, mixing_ref, light_ref, xs_ref, acc_ref, MIDDLE_PLACES)
     for group, place in MIDDLE_PLACES.items():
         solve(acc_ref, place, inverse_ref, carry_ref, ratio_ref, group, into_group(middle_ref, place))
 
@@ -368,25 +384,25 @@
     )(*operands)
 
 
-def first_own(every_column, state, table, mixing, light, kappa, wet):
+def first_own(every_column, state, table, light, quarter, mixing, kappa, wet):
     factors = shape(GROUPS, LEV, CHUNKS * SEGS, LANE)
-    like = [jax.ShapeDtypeStruct(one.shape, one.dtype) for one in (table, mixing, light, wet)]
+    like = [jax.ShapeDtypeStruct(one.shape, one.dtype) for one in (mixing, wet)]
     return pl.pallas_call(
         functools.partial(first_own_kernel, every_column),
         out_shape=(EDGE, MIDDLE, factors, factors, factors, *like),
-        in_specs=[VMEM] + [HBM] * 5,
-        out_specs=(VMEM,) * 9,
+        in_specs=[VMEM] * 4 + [HBM] * 3,
+        out_specs=(VMEM,) * 7,
         scratch_shapes=[
             pltpu.VMEM((BLOCKS, 2 * ROWS, TILE), bf16),
             pltpu.VMEM((GROUPS - 2, GROUP_ROWS, LANE), f32),
             pltpu.VMEM((GROUPS * CHUNKS * SEGS * LEV, LANE), f32),
             pltpu.VMEM((SEGS, LEV, WIDTH), f32),
-            pltpu.SemaphoreType.DMA((4 + GROUPS,)),
+            pltpu.SemaphoreType.DMA((2 + GROUPS,)),
         ],
         compiler_params=PARAMS,
         cost_estimate=pl.CostEstimate(flops=6_000_000_000, bytes_accessed=4_000_000, transcendentals=0),
         name="first_step_own",
-    )(state, *[pltpu.with_memory_space_constraint(one, pltpu.HBM) for one in (table, mixing, light, kappa, wet)])
+    )(state, table, light, quarter, *in_hbm(mixing, kappa, wet))
 
 
 def second_middle(every_column, head, middle, tail, table, mixing, light, factors):
@@ -416,102 +432,151 @@
 
 
 PAIRS = [(i, j) for i in range(BASIS) for j in range(i, BASIS)]
-
-
-def residual_of(groups, segs, state_ref, wet_ref, basis_ref, before_of, write, sums, products):
-    level = lax.broadcasted_iota(jnp.int32, (8, LANE), 0)
-    for group in groups:
-        for chunk in range(CHUNKS):
-            lanes = pl.ds(group * HALO + chunk * LANE, LANE)
-            wet = jnp.broadcast_to(wet_ref[pl.ds(group * CHUNKS + chunk, 1), :], (8, LANE))
-            for seg in segs:
-                for tracer in range(TRACERS):
-                    for part in range(LEV // 8):
-                        rows = pl.ds(part * 8, 8)
-                        before = before_of(group, chunk, seg, tracer, part * 8)
-                        own = state_ref[seg, tracer, rows, lanes]
-                        here = jnp.where(wet > level + part * 8, own - before, 0.0)
-                        write(group, chunk, seg, tracer, rows, here)
-                        vectors = [basis_ref[i, seg, tracer, rows, lanes] for i in range(BASIS)]
-                        for i in range(BASIS):
-                            sums[i] = sums[i] + vectors[i] * here
-                        sums[BASIS] = sums[BASIS] + here * here
-                        if products:
-                            for at, (i, j) in enumerate(PAIRS):
-                                sums[BASIS + 1 + at] = sums[BASIS + 1 + at] + vectors[i] * vectors[j]
+SUMS = BASIS + 1 + len(PAIRS)
+KNOWN = ((range(GROUPS), range(1, SEGS)), (range(1, GROUPS - 1), (0,)))
+UNKNOWN = (((0, GROUPS - 1), (0,)),)
+
+
+def pieces_of(areas):
+    for groups, segs in areas:
+        for group in groups:
+            for chunk in range(CHUNKS):
+                lanes = pl.ds(group * HALO + chunk * LANE, LANE)
+                for seg in segs:
+                    for tracer in range(TRACERS):
+                        for level in range(0, LEV, 8):
+                            yield group, chunk, seg, tracer, level, pl.ds(level, 8), lanes
+
+
+def residual_at(place, state_ref, wet_ref, before):
+    group, chunk, seg, tracer, level, rows, lanes = place
+    wet = jnp.broadcast_to(wet_ref[pl.ds(group * CHUNKS + chunk, 1), :], (8, LANE))
+    here = wet > lax.broadcasted_iota(jnp.int32, (8, LANE), 0) + level
+    return jnp.where(here, state_ref[seg, tracer, rows, lanes] - before, 0.0)
+
+
+def basis_at(place, basis_ref):
+    _, _, seg, tracer, _, rows, lanes = place
+    return [basis_ref[i, seg, tracer, rows, lanes] for i in range(BASIS)]
+
+
+def add_products(sums, vectors):
+    for at, (i, j) in enumerate(PAIRS):
+        sums[at] = sums[at] + vectors[i] * vectors[j]
+
+
+def add_rest(sums, vectors, value, guess):
+    for i in range(BASIS):
+        value = value - guess[i] * vectors[i]
+    for i in range(BASIS):
+        sums[i] = sums[i] + vectors[i] * value
+    sums[BASIS] = sums[BASIS] + value * value
+
+
+def symmetric(values):
+    matrix = [[None] * BASIS for _ in range(BASIS)]
+    for (i, j), value in zip(PAIRS, values):
+        matrix[i][j] = matrix[j][i] = value
+    return matrix
+
+
+def whole_sum(value):
+    return jnp.sum(jnp.sum(value, axis=0, keepdims=True), axis=1, keepdims=True)
+
+
+def least_squares(products, right):
+    gram = symmetric(products)
+    factor = [[None] * BASIS for _ in range(BASIS)]
+    pivots, inverses, weights = [], [], []
+    for i in range(BASIS):
+        for j in range(i):
+            value = gram[i][j]
+            for k in range(j):
+                value = value - factor[i][k] * pivots[k] * factor[j][k]
+            factor[i][j] = value * inverses[j]
+        pivot = gram[i][i]
+        for k in range(i):
+            pivot = pivot - factor[i][k] * factor[i][k] * pivots[k]
+        usable = (pivot > 1e-3 * gram[i][i]) & (pivot > 1e-30)
+        pivots.append(pivot)
+        inverses.append(jnp.where(usable, 1.0 / jnp.where(usable, pivot, 1.0), 0.0))
+        value = right[i]
+        for k in range(i):
+            value = value - factor[i][k] * weights[k]
+        weights.append(value)
+    for i in range(BASIS - 1, -1, -1):
+        value = weights[i] * inverses[i]
+        for k in range(i + 1, BASIS):
+            value = value - factor[k][i] * weights[k]
+        weights[i] = value
+    return weights
 
 
 def early_kernel(
-    state_ref, wet_ref, basis_ref, head_ref, middle_ref, tail_ref, came_ref, out_ref, residual_ref, sums_ref, sems
+    state_ref, wet_ref, basis_ref, head_ref, middle_ref, tail_ref, came_ref,
+    out_ref, residual_ref, sums_ref, guess_ref, sems,
 ):
     refs = [(head_ref, 0)] + [(middle_ref, i) for i in range(GROUPS - 2)] + [(tail_ref, 0)]
-    sums = [jnp.zeros((8, LANE), f32) for _ in range(BASIS + 1 + len(PAIRS))]
-
-    def before_of(group, chunk, seg, tracer, level):
+    zero = jnp.zeros((8, LANE), f32)
+    first = [zero] * BASIS
+    products = [zero] * len(PAIRS)
+    for place in pieces_of(KNOWN):
+        group, chunk, seg, tracer, level, rows, lanes = place
         if seg:
-            ref, place = refs[group]
-            return ref[place, pl.ds(group_row(tracer, chunk, seg - 1) + level, 8), :]
-        return came_ref[group - 1, pl.ds((tracer * CHUNKS + chunk) * LEV + level, 8), :]
-
-    def write(group, chunk, seg, tracer, rows, value):
-        residual_ref[seg, tracer, rows, pl.ds(group * HALO + chunk * LANE, LANE)] = value
-
-    residual_of(range(GROUPS), range(1, SEGS), state_ref, wet_ref, basis_ref, before_of, write, sums, True)
+            ref, at = refs[group]
+            before = ref[at, pl.ds(group_row(tracer, chunk, seg - 1) + level, 8), :]
+        else:
+            before = came_ref[group - 1, pl.ds((tracer * CHUNKS + chunk) * LEV + level, 8), :]
+        value = residual_at(place, state_ref, wet_ref, before)
+        residual_ref[seg, tracer, rows, lanes] = value
+        vectors = basis_at(place, basis_ref)
+        for i in range(BASIS):
+            first[i] = first[i] + vectors[i] * value
+        add_products(products, vectors)
     parts = [(slice(1, SEGS),), (slice(0, 1), slice(None), slice(None), pl.ds(HALO, WIDTH - 2 * HALO))]
     copies = [pltpu.make_async_copy(residual_ref.at[part], out_ref.at[part], sems.at[i]) for i, part in enumerate(parts)]
-    copies[0].start()
-    residual_of(range(1, GROUPS - 1), (0,), state_ref, wet_ref, basis_ref, before_of, write, sums, True)
-    copies[1].start()
-    for group in (0, GROUPS - 1):
-        for chunk in range(CHUNKS):
-            lanes = pl.ds(group * HALO + chunk * LANE, LANE)
-            for tracer in range(TRACERS):
-                for part in range(LEV // 8):
-                    vectors = [basis_ref[i, 0, tracer, pl.ds(part * 8, 8), lanes] for i in range(BASIS)]
-                    for at, (i, j) in enumerate(PAIRS):
-                        sums[BASIS + 1 + at] = sums[BASIS + 1 + at] + vectors[i] * vectors[j]
-    for i, one in enumerate(sums):
+    for copy in copies:
+        copy.start()
+    weights = least_squares([whole_sum(one) for one in products], [whole_sum(one) for one in first])
+    guess = [jnp.broadcast_to(weight, (8, LANE)) for weight in weights]
+    sums = [zero] * (BASIS + 1)
+    for place in pieces_of(KNOWN):
+        _, _, seg, tracer, _, rows, lanes = place
+        add_rest(sums, basis_at(place, basis_ref), residual_ref[seg, tracer, rows, lanes], guess)
+    for place in pieces_of(UNKNOWN):
+        add_products(products, basis_at(place, basis_ref))
+    for i, one in enumerate(sums + products):
         sums_ref[i] = one
+    for i, one in enumerate(guess):
+        guess_ref[i] = one
     for copy in copies:
         copy.wait()
 
 
-def late_kernel(
-    state_ref, wet_ref, basis_ref, came_ref, early_ref, unused_ref, residual_ref, sums_ref, pieces_ref, sems
-):
-    sums = [early_ref[i] for i in range(BASIS + 1 + len(PAIRS))]
-
-    def before_of(group, chunk, seg, tracer, level):
-        return came_ref[EDGE_PLACES[group], pl.ds((tracer * CHUNKS + chunk) * LEV + level, 8), :]
-
-    def write(group, chunk, seg, tracer, rows, value):
+def late_kernel(state_ref, wet_ref, basis_ref, came_ref, early_ref, guess_ref, pieces_ref, sums_ref):
+    guess = [guess_ref[i] for i in range(BASIS)]
+    sums = [early_ref[i] for i in range(SUMS)]
+    for place in pieces_of(UNKNOWN):
+        group, chunk, seg, tracer, level, rows, lanes = place
+        before = came_ref[EDGE_PLACES[group], pl.ds((tracer * CHUNKS + chunk) * LEV + level, 8), :]
+        value = residual_at(place, state_ref, wet_ref, before)
         pieces_ref[EDGE_PLACES[group], tracer, rows, pl.ds(chunk * LANE, LANE)] = value
-
-    copies = []
-    for group, place in EDGE_PLACES.items():
-        residual_of((group,), (0,), state_ref, wet_ref, basis_ref, before_of, write, sums, False)
-        copy = pltpu.make_async_copy(
-            pieces_ref.at[place], residual_ref.at[0, :, :, pl.ds(group * HALO, HALO)], sems.at[place]
-        )
-        copy.start()
-        copies.append(copy)
+        add_rest(sums, basis_at(place, basis_ref), value, guess)
     lane = lax.broadcasted_iota(jnp.int32, (8, LANE), 1)
     row = jnp.zeros((8, LANE), f32)
-    for i, one in enumerate(sums):
-        row = jnp.where(lane == i, jnp.sum(jnp.sum(one, axis=0, keepdims=True), axis=1, keepdims=True), row)
+    for i, one in enumerate([whole_sum(one) for one in sums] + guess):
+        row = jnp.where(lane == i, one, row)
     for i in range(sums_ref.shape[0] // 8):
         sums_ref[pl.ds(8 * i, 8), :] = row
-    for copy in copies:
-        copy.wait()
 
 
 def early(state, wet, basis, head, middle, tail, came):
     whole = shape(SEGS, TRACERS, LEV, WIDTH)
     return pl.pallas_call(
         early_kernel,
-        out_shape=(whole, whole, shape(BASIS + 1 + len(PAIRS), 8, LANE)),
+        out_shape=(whole, whole, shape(SUMS, 8, LANE), shape(BASIS, 8, LANE)),
         in_specs=[VMEM] * 7,
-        out_specs=(HBM, VMEM, VMEM),
+        out_specs=(HBM, VMEM, VMEM, VMEM),
         scratch_shapes=[pltpu.SemaphoreType.DMA((2,))],
         compiler_params=PARAMS,
         cost_estimate=pl.CostEstimate(flops=10_000_000, bytes_accessed=4_000_000, transcendentals=0),
@@ -519,33 +584,45 @@
     )(state, wet, basis, head, middle, tail, came)
 
 
-def late(devices, state, wet, basis, came, sums, residual):
-    return pl.pallas_call(
-        late_kernel,
-        out_shape=(shape(SEGS, TRACERS, LEV, WIDTH), shape(devices, LANE), shape(2, TRACERS, LEV, HALO)),
-        in_specs=[VMEM] * 5 + [HBM],
-        out_specs=(HBM, VMEM, VMEM),
-        scratch_shapes=[pltpu.SemaphoreType.DMA((2,))],
-        input_output_aliases={5: 0},
-        compiler_params=PARAMS,
-        cost_estimate=pl.CostEstimate(flops=3_000_000, bytes_accessed=4_000_000, transcendentals=0),
-        name="residual_last",
-    )(state, wet, basis, came, sums, residual)
-
-
-def scaled_kernel(count, residual_ref, pieces_ref, basis_ref, sums_ref, new_out_ref, coefficients_ref, new_ref, sems):
-    sums = jnp.sum(sums_ref[...], axis=0, keepdims=True)
-    one = [sums[:, i : i + 1] for i in range(BASIS + 1 + len(PAIRS))]
-    first, square, products = one[:BASIS], one[BASIS], iter(one[BASIS + 1 :])
-    gram = [[None] * BASIS for _ in range(BASIS)]
+def late(devices, state, wet, basis, came, sums, guess):
+    return call(
+        late_kernel, "residual_last", 3_000_000, (shape(2, TRACERS, LEV, HALO), shape(devices, LANE)), [],
+        state, wet, basis, came, sums, guess,
+    )
+
+
+def scaled_kernel(
+    count, residual_ref, pieces_ref, basis_ref, sums_ref, unused_ref,
+    out_ref, new_out_ref, coefficients_ref, new_ref, sems,
+):
+    copies = []
+
+    def send(from_ref, to_ref):
+        copies.append(pltpu.make_async_copy(from_ref, to_ref, sems.at[len(copies)]))
+        copies[-1].start()
+
+    for group, place in EDGE_PLACES.items():
+        send(pieces_ref.at[place], out_ref.at[0, :, :, pl.ds(group * HALO, HALO)])
+    sums = sums_ref[...]
+    if sums.shape[0] < LANE:
+        sums = jnp.concatenate([sums, jnp.zeros((LANE - sums.shape[0], LANE), f32)], axis=0)
+    sums = sums.T
+    row = [sums[i : i + 1] for i in range(SUMS + BASIS)]
+    of_rest, squares, products, guess = row[:BASIS], row[BASIS], row[BASIS + 1 : SUMS], row[SUMS:]
+    gram = symmetric(products)
+    first = [of_rest[i] + sum(gram[i][j] * guess[j] for j in range(BASIS)) for i in range(BASIS)]
+    totals = jnp.concatenate(first + products + [jnp.zeros((2, LANE), f32)], axis=0)
+    totals = jnp.sum(totals, axis=1, keepdims=True)
+    one = [totals[i : i + 1] for i in range(SUMS)]
+    first, products = one[:BASIS], one[BASIS : SUMS - 1]
+    whole_gram = symmetric(products)
+    second = [first[i] - sum(whole_gram[i][j] * first[j] for j in range(BASIS)) for i in range(BASIS)]
+    both = [first[i] + second[i] for i in range(BASIS)]
+    away = [both[i] - guess[i] for i in range(BASIS)]
     for i in range(BASIS):
-        for j in range(i, BASIS):
-            gram[i][j] = gram[j][i] = next(products)
-    second = [first[i] - sum(gram[i][j] * first[j] for j in range(BASIS)) for i in range(BASIS)]
-    both = [first[i] + second[i] for i in range(BASIS)]
-    for i in range(BASIS):
-        square = square - both[i] * (2.0 * first[i] - sum(gram[i][j] * both[j] for j in range(BASIS)))
-    spread = jnp.sqrt(jnp.maximum(square, 0.0) / count + epsilon)
+        squares = squares + away[i] * (sum(gram[i][j] * away[j] for j in range(BASIS)) - 2.0 * of_rest[i])
+    square = jnp.maximum(jnp.sum(squares, axis=1, keepdims=True), 0.0)
+    spread = jnp.sqrt(square / count + epsilon)
     lane = lax.broadcasted_iota(jnp.int32, (8, LANE), 1)
     result = jnp.zeros((8, LANE), f32)
     for i, value in enumerate(both + [spread]):
@@ -554,7 +631,6 @@
     scale = 1.0 / spread
     weights = [jnp.broadcast_to(-value * scale, (LEV, LANE)) for value in both]
     scale = jnp.broadcast_to(scale, (LEV, LANE))
-    copies = []
     for seg in range(SEGS):
         for tracer in range(TRACERS):
             for chunk in range(WIDTH // LANE):
@@ -568,26 +644,24 @@
                 for i in range(BASIS):
                     total = total + weights[i] * basis_ref[i, seg, tracer, :, lanes]
                 new_ref[seg, tracer, :, lanes] = total
-            at = seg * TRACERS + tracer
-            copy = pltpu.make_async_copy(new_ref.at[seg, tracer], new_out_ref.at[seg, tracer], sems.at[at])
-            copy.start()
-            copies.append(copy)
+            send(new_ref.at[seg, tracer], new_out_ref.at[seg, tracer])
     for copy in copies:
         copy.wait()
 
 
-def scaled(count, residual, pieces, basis, sums):
+def scaled(count, residual, pieces, basis, sums, out):
     whole = (SEGS, TRACERS, LEV, WIDTH)
     return pl.pallas_call(
         functools.partial(scaled_kernel, count),
-        out_shape=(shape(*whole), shape(BASIS + 1)),
-        in_specs=[VMEM] * 4,
-        out_specs=(HBM, VMEM),
-        scratch_shapes=[pltpu.VMEM(whole, f32), pltpu.SemaphoreType.DMA((SEGS * TRACERS,))],
+        out_shape=(shape(*whole), shape(*whole), shape(BASIS + 1)),
+        in_specs=[VMEM] * 4 + [HBM],
+        out_specs=(HBM, HBM, VMEM),
+        scratch_shapes=[pltpu.VMEM(whole, f32), pltpu.SemaphoreType.DMA((2 + SEGS * TRACERS,))],
+        input_output_aliases={4: 0},
         compiler_params=PARAMS,
         cost_estimate=pl.CostEstimate(flops=4_000_000, bytes_accessed=4_000_000, transcendentals=0),
         name="orthogonal_and_scaled",
-    )(residual, pieces, basis, sums)
+    )(residual, pieces, basis, sums, out)
 
 
 def shifted(block, axis, distance):
@@ -597,14 +671,12 @@
 
 def per_device(segment_state, light, mixing, kappa, neighbour_columns, wet_levels, basis):
     every_column = lax.axis_size("col") * WIDTH
-    state = pltpu.with_memory_space_constraint(segment_state, pltpu.VMEM)
-    head, tail = halves(state)
+    table = neighbour_columns.T
+    wet = wet_levels.reshape(WIDTH // LANE, LANE)
+    head, tail, state, table, light, quarter = halves(segment_state, table, light, mixing)
     left = shifted(tail, "col", 1)
     right = shifted(head, "col", -1)
-    table = neighbour_columns.T
-    wet = wet_levels.reshape(WIDTH // LANE, LANE)
-    edge, middle, *kept = first_own(every_column, state, table, mixing, light, kappa, wet)
-    *factors, table, mixing, light, wet = kept
+    edge, middle, *factors, mixing, wet = first_own(every_column, state, table, light, quarter, mixing, kappa, wet)
     head, tail = edges(True, every_column, left, right, table, mixing, edge, factors)
     left = shifted(tail, "col", 1)
     right = shifted(head, "col", -1)
@@ -613,13 +685,12 @@
     edge = second_edge(every_column, head, middle, tail, table, mixing, light, xs)
     head, tail, sent = edges(False, every_column, left, right, table, mixing, edge, factors)
     came_edge = shifted(sent, "seg", 1)
-    residual, held, sums = early(state, wet, basis, head, end_middle, tail, came_middle)
+    residual, held, sums, guess = early(state, wet, basis, head, end_middle, tail, came_middle)
     devices = lax.axis_size("seg") * lax.axis_size("col")
-    residual, sums, pieces = late(devices, state, wet, basis, came_edge, sums, residual)
+    pieces, sums = late(devices, state, wet, basis, came_edge, sums, guess)
     sums = lax.all_to_all(sums, ("seg", "col"), 0, 0, tiled=True)
     count = lax.axis_size("seg") * SEGS * TRACERS * LEV * every_column
-    new_vector, coefficients = scaled(count, held, pieces, basis, sums)
-    return (residual, new_vector, coefficients)
+    return scaled(count, held, pieces, basis, sums, residual)
 
 
 def solution(mesh):

time: 59.9 us -> 59 us (0.985)
  Pallas kernels: 22.7 us -> 24.3 us
  local copies, waits for them, and re-layouts: 1.23 us -> 0.01 us
  waiting for transfers between devices: 3.8 us -> 2.87 us
    pallas_call x2, Pallas kernels: 2.36 us -> 4.13 us  [the longest x1 2.44 us: early(): pl.pallas_call(early_kernel, out_shape=(whole, whole, shape(SUMS, 8, LANE...]
    unnamed x6 -> x2, local copies, waits for them, and re-layouts: 1.23 us -> 0.01 us
    ppermute x6, waiting for transfers between devices: 3.8 us -> 2.87 us  [shifted(): lax.ppermute(block, axis, [(i, (i + distance) % count) for i in range(cou...]
    pallas_call x5, Pallas kernels: 9.96 us -> 10.6 us  [call(): pl.pallas_call(kernel, out_shape=outs, in_specs=[VMEM] * len(operands), o...]
  transfers between devices with their start and end apart: 6 -> 6, of which waited for: 2 -> 2; matrix products, arithmetic and copies ran while one was open for 0% -> 0% of each run, Pallas kernels for 30% -> 31%
where the time goes in v5:
time: 59 us; the launch traced here: 58.4 us
  Pallas kernels  24.3 us (41%)
  blocking collectives  16.8 us (28%)
  starting transfers between devices  13.6 us (23%)
  waiting for transfers between devices  2.87 us (5%)
  between operations  0.91 us (2%)
    all_to_all x1, blocking collectives, per_device(): sums = lax.all_to_all(sums, ('seg', 'col'), 0, 0, tiled=True)  16.8 us
    ppermute x6, starting transfers between devices, shifted(): lax.ppermute(block, axis, [(i, (i + distance) % count) for i in range(cou...  13.6 us
    pallas_call x5, Pallas kernels, call(): pl.pallas_call(kernel, out_shape=outs, in_specs=[VMEM] * len(operands), o...  10.6 us
    pallas_call x1, Pallas kernels, first_own(): pl.pallas_call(functools.partial(first_own_kernel, every_column), out_sha...  7.47 us
    ppermute x6, waiting for transfers between devices, shifted(): lax.ppermute(block, axis, [(i, (i + distance) % count) for i in range(cou...  2.87 us
    pallas_call x1, Pallas kernels, early(): pl.pallas_call(early_kernel, out_shape=(whole, whole, shape(SUMS, 8, LANE...  2.44 us
    pallas_call x1, Pallas kernels, scaled(): pl.pallas_call(functools.partial(scaled_kernel, count), out_shape=(shape(...  2.05 us
    pallas_call x1, Pallas kernels, halves(): pl.pallas_call(halves_kernel, out_shape=(half, half, *like, shape(SEGS, N...  1.69 us
  transfers between devices with their start and end apart: 6, of which 2 were waited for; matrix products, arithmetic and copies ran while one was open for 0% of the time, Pallas kernels for 31%

profile of v5, /device:TPU:0, one launch (start us, length us, event | category | flops | bytes accessed | tf_op | source)
XLA Modules:
  0.0 58.4 jit_solution(17617210027348625126)
XLA Ops:
  0.6 1.7 %edge_columns.1 = (f32[2,2,32,512]{3,2,1,0:T(8,128)S(1)}, f32[2,2,32,512]{3,2,1,0:T(8,128)S(1)}, f32[2,2,32,2048]{3,2,1,0:T(8,128)S(1)}, s32[6,2048]{1,0:T(8,128...) custom-call(f32[2,2,32,2048]{3,2,1,0:T(8,128)} %state_in.1, s32[6,2048]{1,0:T(8,128)} %bitcast.8, ...), custom_call_target="tpu_custom_call" | custom-call | bytes 4000000 | tf_op jit(solution)/shard_map/edge_columns/pallas_call | solution.py:273
  2.3 2.1 %collective-permute-start = (f32[2,2,32,512]{3,2,1,0:T(8,128)S(1)}, f32[2,2,32,512]{3,2,1,0:T(8,128)S(1)}, u32[]{:S(2)}, u32[]{:S(2)}) collective-permute-start(f32[2,2,32,512]{3,2,1,0:T(8,128)S(1)} %get-tuple-element.35), channel_id=1, source_target_pairs={{0,1},{1,2},{2,3},{3,4},{4,5},{5,6},{6,7},{7,8},{8,9},{9,10},{10,1... | collective-permute-start | bytes 786440 | tf_op jit(solution)/shard_map/ppermute | solution.py:669
  4.4 4.4 %collective-permute-start.1 = (f32[2,2,32,512]{3,2,1,0:T(8,128)S(1)}, f32[2,2,32,512]{3,2,1,0:T(8,128)S(1)}, u32[]{:S(2)}, u32[]{:S(2)}) collective-permute-start(f32[2,2,32,512]{3,2,1,0:T(8,128)S(1)} %get-tuple-element.36), channel_id=1, source_target_pairs={{0,15},{1,0},{2,1},{3,2},{4,3},{5,4},{6,5},{7,6},{8,7},{9,8},{10,9... | collective-permute-start | bytes 786440 | tf_op jit(solution)/shard_map/ppermute | solution.py:669
  8.8 7.5 %first_step_own.1 = (f32[2,512,128]{2,1,0:T(8,128)S(1)}, f32[2,512,128]{2,1,0:T(8,128)S(1)}, f32[4,32,8,128]{3,2,1,0:T(8,128)S(1)}, f32[4,32,8,128]{3,2,1,0:T(8,...) custom-call(f32[2,2,32,2048]{3,2,1,0:T(8,128)S(1)} %get-tuple-element.30.state_ref, ...), custom_call_target="tpu_custom_call" | custom-call | flops 6000000000 | bytes 4000000 | tf_op jit(solution)/shard_map/first_step_own/pallas_call | solution.py:390
  16.3 0.0 collective-permute-done.left_ref
  16.3 0.0 collective-permute-done.1.right_ref
  16.3 1.8 %first_step_edges.1 = (f32[1,512,128]{2,1,0:T(8,128)S(1)}, f32[1,512,128]{2,1,0:T(8,128)S(1)}) custom-call(f32[2,2,32,512]{3,2,1,0:T(8,128)S(1)} %collective-permute-done.left_ref, f32[2,2,32,512]{3,2,1,0:T(8,128)S(1)} %collective-permute-done.1.right_ref, s32[6,2048]{1,0:T(8,128)S(1)} %get-tuple-element.31.table_ref, ...), custom_call_target="tpu_custom_call" | custom-call | flops 1000000000 | bytes 4000000 | tf_op jit(solution)/shard_map/first_step_edges/pallas_call | solution.py:375
  18.1 0.1 collective-permute-start.2
  18.2 5.3 %collective-permute-start.3 = (f32[1,512,128]{2,1,0:T(8,128)S(1)}, f32[1,512,128]{2,1,0:T(8,128)S(1)}, u32[]{:S(2)}, u32[]{:S(2)}) collective-permute-start(f32[1,512,128]{2,1,0:T(8,128)S(1)} %get-tuple-element.43.head_ref), channel_id=1, source_target_pairs={{0,15},{1,0},{2,1},{3,2},{4,3},{5,4},{6,5},{7,6},{8,7},{9,8},{10,9... | collective-permute-start | bytes 786440 | tf_op jit(solution)/shard_map/ppermute | solution.py:669
  23.5 4.0 %second_step_middle.1 = (f32[2,512,128]{2,1,0:T(8,128)S(1)}, f32[2,256,128]{2,1,0:T(8,128)S(1)}, bf16[8,256,256]{2,1,0:T(8,128)(2,1)S(1)}) custom-call(f32[1,512,128]{2,1,0:T(8,128)S(1)} %get-tuple-element.43.head_ref, f32[2,512,128]{2,1,0:T(8,128)S(1)} %get-tuple-element.44.middle_in_ref.middle_ref, f32[1,512,128]{2,1,0:T(8,128)S(1)} %get-tuple-element.42.tail_ref, ...), custom_call_target="tpu_custom_call" | custom-call | flops 3500000000 | bytes 4000000 | tf_op jit(solution)/shard_map/second_step_middle/pallas_call | solution.py:375
  27.6 0.0 collective-permute-start.4
  27.6 2.6 %second_step_edges_own.1.edge_in_ref = f32[2,512,128]{2,1,0:T(8,128)S(1)} custom-call(f32[1,512,128]{2,1,0:T(8,128)S(1)} %get-tuple-element.43.head_ref, f32[2,512,128]{2,1,0:T(8,128)S(1)} %get-tuple-element.44.middle_in_ref.middle_ref, f32[1,512,128]{2,1,0:T(8,128)S(1)} %get-tuple-element.42.tail_ref, s32[6,2048]{1,0:T(8,128)S(1)} %get-tuple-element.31.table_ref, ...), custom_call_target="tpu_custom_call" | custom-call | flops 2500000000 | bytes 4000000 | tf_op jit(solution)/shard_map/second_step_edges_own/pallas_call | solution.py:375
  30.2 0.0 copy-start
  30.2 0.0 collective-permute-done.2.left_ref
  30.2 0.0 collective-permute-done.3.right_ref
  30.2 1.9 %second_step_edges.1 = (f32[1,512,128]{2,1,0:T(8,128)S(1)}, f32[1,512,128]{2,1,0:T(8,128)S(1)}, f32[2,256,128]{2,1,0:T(8,128)S(1)}) custom-call(f32[1,512,128]{2,1,0:T(8,128)S(1)} %collective-permute-done.2.left_ref, f32[1,512,128]{2,1,0:T(8,128)S(1)} %collective-permute-done.3.right_ref, s32[6,2048]{1,0:T(8,128)S(1)} %get-tuple-element.31.table_ref, ...), custom_call_target="tpu_custom_call" | custom-call | flops 1000000000 | bytes 4000000 | tf_op jit(solution)/shard_map/second_step_edges/pallas_call | solution.py:375
  32.1 1.7 %collective-permute-start.5 = (f32[2,256,128]{2,1,0:T(8,128)S(1)}, f32[2,256,128]{2,1,0:T(8,128)S(1)}, u32[]{:S(2)}, u32[]{:S(2)}) collective-permute-start(f32[2,256,128]{2,1,0:T(8,128)S(1)} %get-tuple-element.51), channel_id=1, source_target_pairs={{0,16},{16,32},{32,48},{48,64},{64,80},{80,96},{96,112},{112,0},{1... | collective-permute-start | bytes 786440 | tf_op jit(solution)/shard_map/ppermute | solution.py:669
  33.8 0.8 %collective-permute-done.4.came_ref = f32[2,256,128]{2,1,0:T(8,128)S(1)} collective-permute-done((f32[2,256,128]{2,1,0:T(8,128)S(1)}, f32[2,256,128]{2,1,0:T(8,128)S(1)}, u32[]{:S(2)}, u32[]{:S(2)}) %collective-permute-start.4) | collective-permute-done | bytes 262176 | tf_op jit(solution)/shard_map/ppermute | solution.py:669
  34.6 0.0 copy-done
  34.6 2.4 %residual_known.1 = (f32[2,2,32,2048]{3,2,1,0:T(8,128)}, f32[2,2,32,2048]{3,2,1,0:T(8,128)S(1)}, f32[15,8,128]{2,1,0:T(8,128)S(1)}, f32[4,8,128]{2,1,0:T(8,128)S(1)}) custom-call(f32[2,2,32,2048]{3,2,1,0:T(8,128)S(1)} %get-tuple-element.30.state_ref, s32[16,128]{1,0:T(8,128)S(1)} %get-tuple-element.34.wet_ref, f32[4,2,2,32,2048]{4,3,2,1,0:T(8,128)S(1)} %copy-done, ...), custom_call_target="tpu_custom_call" | custom-call | flops 10000000 | bytes 4000000 | tf_op jit(solution)/shard_map/residual_known/pallas_call | solution.py:575
  37.0 2.0 %collective-permute-done.5.came_ref = f32[2,256,128]{2,1,0:T(8,128)S(1)} collective-permute-done((f32[2,256,128]{2,1,0:T(8,128)S(1)}, f32[2,256,128]{2,1,0:T(8,128)S(1)}, u32[]{:S(2)}, u32[]{:S(2)}) %collective-permute-start.5) | collective-permute-done | bytes 262176 | tf_op jit(solution)/shard_map/ppermute | solution.py:669
  39.1 0.4 residual_last.1
  39.5 16.8 %all_to_all.11 = f32[128,1,128]{2,1,0:T(1,128)S(1)} all-to-all(f32[128,1,128]{2,1,0:T(1,128)S(1)} %bitcast.7), channel_id=1, replica_groups=mesh['seg'=8,'col'=16] {'seg','col'}, dimensions={0} | all-to-all | bytes 131072 | tf_op jit(solution)/shard_map/all_to_all | solution.py:691
  56.2 2.1 %orthogonal_and_scaled.1 = (f32[2,2,32,2048]{3,2,1,0:T(8,128)}, f32[2,2,32,2048]{3,2,1,0:T(8,128)}, f32[5]{0:T(128)}) custom-call(f32[2,2,32,2048]{3,2,1,0:T(8,128)S(1)} %get-tuple-element.50.residual_ref, f32[2,2,32,512]{3,2,1,0:T(8,128)S(1)} %get-tuple-element.54.pieces_ref, f32[4,2,2,32,2048]{4,3,2,1,0:T(8,128)S(1)} %copy-done, ...), custom_call_target="tpu_custom_call", output_to_operand_aliasing={{0}: (4, {})} | custom-call | flops 4000000 | bytes 4000000 | tf_op jit(solution)/shard_map/orthogonal_and_scaled/pallas_call | solution.py:654
Async XLA Ops:
  2.3 13.9 %collective-permute-start = (f32[2,2,32,512]{3,2,1,0:T(8,128)S(1)}, f32[2,2,32,512]{3,2,1,0:T(8,128)S(1)}, u32[]{:S(2)}, u32[]{:S(2)}) collective-permute-start(f32[2,2,32,512]{3,2,1,0:T(8,128)S(1)} %get-tuple-element.35), channel_id=1, source_target_pairs={{0,1},{1,2},{2,3},{3,4},{4,5},{5,6},{6,7},{7,8},{8,9},{9,10},{10,1... | collective-permute-start | bytes 786440 | tf_op jit(solution)/shard_map/ppermute | solution.py:669
  4.4 11.9 %collective-permute-start.1 = (f32[2,2,32,512]{3,2,1,0:T(8,128)S(1)}, f32[2,2,32,512]{3,2,1,0:T(8,128)S(1)}, u32[]{:S(2)}, u32[]{:S(2)}) collective-permute-start(f32[2,2,32,512]{3,2,1,0:T(8,128)S(1)} %get-tuple-element.36), channel_id=1, source_target_pairs={{0,15},{1,0},{2,1},{3,2},{4,3},{5,4},{6,5},{7,6},{8,7},{9,8},{10,9... | collective-permute-start | bytes 786440 | tf_op jit(solution)/shard_map/ppermute | solution.py:669
  18.1 12.1 %collective-permute-start.2 = (f32[1,512,128]{2,1,0:T(8,128)S(1)}, f32[1,512,128]{2,1,0:T(8,128)S(1)}, u32[]{:S(2)}, u32[]{:S(2)}) collective-permute-start(f32[1,512,128]{2,1,0:T(8,128)S(1)} %get-tuple-element.42.tail_ref), channel_id=1, source_target_pairs={{0,1},{1,2},{2,3},{3,4},{4,5},{5,6},{6,7},{7,8},{8,9},{9,10},{10,1... | collective-permute-start | bytes 786440 | tf_op jit(solution)/shard_map/ppermute | solution.py:669
  18.2 12.0 %collective-permute-start.3 = (f32[1,512,128]{2,1,0:T(8,128)S(1)}, f32[1,512,128]{2,1,0:T(8,128)S(1)}, u32[]{:S(2)}, u32[]{:S(2)}) collective-permute-start(f32[1,512,128]{2,1,0:T(8,128)S(1)} %get-tuple-element.43.head_ref), channel_id=1, source_target_pairs={{0,15},{1,0},{2,1},{3,2},{4,3},{5,4},{6,5},{7,6},{8,7},{9,8},{10,9... | collective-permute-start | bytes 786440 | tf_op jit(solution)/shard_map/ppermute | solution.py:669
  27.6 7.0 %collective-permute-start.4 = (f32[2,256,128]{2,1,0:T(8,128)S(1)}, f32[2,256,128]{2,1,0:T(8,128)S(1)}, u32[]{:S(2)}, u32[]{:S(2)}) collective-permute-start(f32[2,256,128]{2,1,0:T(8,128)S(1)} %get-tuple-element.49), channel_id=1, source_target_pairs={{0,16},{16,32},{32,48},{48,64},{64,80},{80,96},{96,112},{112,0},{1... | collective-permute-start | bytes 786440 | tf_op jit(solution)/shard_map/ppermute | solution.py:669
  30.2 4.4 %copy-start = (f32[4,2,2,32,2048]{4,3,2,1,0:T(8,128)S(1)}, f32[4,2,2,32,2048]{4,3,2,1,0:T(8,128)}, u32[]{:S(2)}) copy-start(f32[4,2,2,32,2048]{4,3,2,1,0:T(8,128)} %basis_ref.5) | copy-start | bytes 12582916
  32.1 7.0 %collective-permute-start.5 = (f32[2,256,128]{2,1,0:T(8,128)S(1)}, f32[2,256,128]{2,1,0:T(8,128)S(1)}, u32[]{:S(2)}, u32[]{:S(2)}) collective-permute-start(f32[2,256,128]{2,1,0:T(8,128)S(1)} %get-tuple-element.51), channel_id=1, source_target_pairs={{0,16},{16,32},{32,48},{48,64},{64,80},{80,96},{96,112},{112,0},{1... | collective-permute-start | bytes 786440 | tf_op jit(solution)/shard_map/ppermute | solution.py:669

commit v6 on v5

--- a/solution.py
+++ b/solution.py
@@ -88,9 +88,11 @@
 
 def picked(xs_ref, places, offsets, index):
     total = None
-    depth = lax.broadcasted_iota(jnp.int32, (TILE, TILE), 0)
+    depth = lax.broadcasted_iota(jnp.int16, (TILE, TILE), 0)
     for place, offset in zip(places, offsets):
-        chosen = jnp.where(depth == index - offset, f32(1), f32(0)).astype(bf16)
+        wanted = jnp.broadcast_to(index - offset, (16, TILE)).astype(jnp.int16)
+        wanted = jnp.concatenate([wanted] * (TILE // 16), axis=0)
+        chosen = jnp.where(depth == wanted, bf16(1), bf16(0))
         part = jnp.dot(xs_ref[place], chosen, preferred_element_type=f32)
         total = part if total is None else total + part
     return total[:ROWS] + total[ROWS:]
@@ -227,7 +229,7 @@
 
 
 def by_lane(block):
-    return (4, 5) if block % 2 else (5,)
+    return (4, 5)
 
 
 EDGE_BLOCKS = (0, 1, BLOCKS - 2, BLOCKS - 1)
@@ -299,8 +301,8 @@
     own_blocks(every_column, EDGE_BLOCKS[:2], read, table_ref, quarter_ref, light_ref, xs_ref, edge_ref, EDGE_PLACES)
     for copy in copies:
         copy.wait()
+    own_blocks(every_column, EDGE_BLOCKS[2:], read, table_ref, mixing_ref, light_ref, xs_ref, edge_ref, EDGE_PLACES)
     factorize(kappa_ref, wet_ref, by_rows_ref, inverse_ref, carry_ref, ratio_ref)
-    own_blocks(every_column, EDGE_BLOCKS[2:], read, table_ref, mixing_ref, light_ref, xs_ref, edge_ref, EDGE_PLACES)
     own_blocks(every_column, MIDDLE_BLOCKS, read, table_ref, mixing_ref, light_ref, xs_ref, acc_ref, MIDDLE_PLACES)
     for group, place in MIDDLE_PLACES.items():
         solve(acc_ref, place, inverse_ref, carry_ref, ratio_ref, group, into_group(middle_ref, place))

time: 59 us -> 58.3 us (0.988)
  Pallas kernels: 24.3 us -> 23 us
  blocking collectives: 16.8 us -> 17.4 us
    pallas_call x5, Pallas kernels: 10.6 us -> 9.76 us  [call(): pl.pallas_call(kernel, out_shape=outs, in_specs=[VMEM] * len(operands), o...]
    all_to_all x1, blocking collectives: 16.8 us -> 17.4 us  [per_device(): sums = lax.all_to_all(sums, ('seg', 'col'), 0, 0, tiled=True)]
  transfers between devices with their start and end apart: 6 -> 6, of which waited for: 2 -> 2; matrix products, arithmetic and copies ran while one was open for 0% -> 0% of each run, Pallas kernels for 31% -> 30%
where the time goes in v6:
time: 58.3 us; the launch traced here: 57.7 us
  Pallas kernels  23 us (39%)
  blocking collectives  17.4 us (30%)
  starting transfers between devices  13.6 us (23%)
  waiting for transfers between devices  2.87 us (5%)
  between operations  0.9 us (2%)
    all_to_all x1, blocking collectives, per_device(): sums = lax.all_to_all(sums, ('seg', 'col'), 0, 0, tiled=True)  17.4 us
    ppermute x6, starting transfers between devices, shifted(): lax.ppermute(block, axis, [(i, (i + distance) % count) for i in range(cou...  13.6 us
    pallas_call x5, Pallas kernels, call(): pl.pallas_call(kernel, out_shape=outs, in_specs=[VMEM] * len(operands), o...  9.76 us
    pallas_call x1, Pallas kernels, first_own(): pl.pallas_call(functools.partial(first_own_kernel, every_column), out_sha...  7.03 us
    ppermute x6, waiting for transfers between devices, shifted(): lax.ppermute(block, axis, [(i, (i + distance) % count) for i in range(cou...  2.87 us
    pallas_call x1, Pallas kernels, early(): pl.pallas_call(early_kernel, out_shape=(whole, whole, shape(SUMS, 8, LANE...  2.44 us
    pallas_call x1, Pallas kernels, scaled(): pl.pallas_call(functools.partial(scaled_kernel, count), out_shape=(shape(...  2.05 us
    pallas_call x1, Pallas kernels, halves(): pl.pallas_call(halves_kernel, out_shape=(half, half, *like, shape(SEGS, N...  1.69 us
  transfers between devices with their start and end apart: 6, of which 2 were waited for; matrix products, arithmetic and copies ran while one was open for 0% of the time, Pallas kernels for 30%

profile of v6, /device:TPU:0, one launch (start us, length us, event | category | flops | bytes accessed | tf_op | source)
XLA Modules:
  0.0 57.7 jit_solution(2110423448632756006)
XLA Ops:
  0.6 1.7 %edge_columns.1 = (f32[2,2,32,512]{3,2,1,0:T(8,128)S(1)}, f32[2,2,32,512]{3,2,1,0:T(8,128)S(1)}, f32[2,2,32,2048]{3,2,1,0:T(8,128)S(1)}, s32[6,2048]{1,0:T(8,128...) custom-call(f32[2,2,32,2048]{3,2,1,0:T(8,128)} %state_in.1, s32[6,2048]{1,0:T(8,128)} %bitcast.8, ...), custom_call_target="tpu_custom_call" | custom-call | bytes 4000000 | tf_op jit(solution)/shard_map/edge_columns/pallas_call | solution.py:275
  2.3 2.1 %collective-permute-start = (f32[2,2,32,512]{3,2,1,0:T(8,128)S(1)}, f32[2,2,32,512]{3,2,1,0:T(8,128)S(1)}, u32[]{:S(2)}, u32[]{:S(2)}) collective-permute-start(f32[2,2,32,512]{3,2,1,0:T(8,128)S(1)} %get-tuple-element.35), channel_id=1, source_target_pairs={{0,1},{1,2},{2,3},{3,4},{4,5},{5,6},{6,7},{7,8},{8,9},{9,10},{10,1... | collective-permute-start | bytes 786440 | tf_op jit(solution)/shard_map/ppermute | solution.py:671
  4.4 4.4 %collective-permute-start.1 = (f32[2,2,32,512]{3,2,1,0:T(8,128)S(1)}, f32[2,2,32,512]{3,2,1,0:T(8,128)S(1)}, u32[]{:S(2)}, u32[]{:S(2)}) collective-permute-start(f32[2,2,32,512]{3,2,1,0:T(8,128)S(1)} %get-tuple-element.36), channel_id=1, source_target_pairs={{0,15},{1,0},{2,1},{3,2},{4,3},{5,4},{6,5},{7,6},{8,7},{9,8},{10,9... | collective-permute-start | bytes 786440 | tf_op jit(solution)/shard_map/ppermute | solution.py:671
  8.8 7.0 %first_step_own.1 = (f32[2,512,128]{2,1,0:T(8,128)S(1)}, f32[2,512,128]{2,1,0:T(8,128)S(1)}, f32[4,32,8,128]{3,2,1,0:T(8,128)S(1)}, f32[4,32,8,128]{3,2,1,0:T(8,...) custom-call(f32[2,2,32,2048]{3,2,1,0:T(8,128)S(1)} %get-tuple-element.30.state_ref, ...), custom_call_target="tpu_custom_call" | custom-call | flops 6000000000 | bytes 4000000 | tf_op jit(solution)/shard_map/first_step_own/pallas_call | solution.py:392
  15.8 0.0 collective-permute-done.left_ref
  15.8 0.0 collective-permute-done.1.right_ref
  15.9 1.7 %first_step_edges.1 = (f32[1,512,128]{2,1,0:T(8,128)S(1)}, f32[1,512,128]{2,1,0:T(8,128)S(1)}) custom-call(f32[2,2,32,512]{3,2,1,0:T(8,128)S(1)} %collective-permute-done.left_ref, f32[2,2,32,512]{3,2,1,0:T(8,128)S(1)} %collective-permute-done.1.right_ref, s32[6,2048]{1,0:T(8,128)S(1)} %get-tuple-element.31.table_ref, ...), custom_call_target="tpu_custom_call" | custom-call | flops 1000000000 | bytes 4000000 | tf_op jit(solution)/shard_map/first_step_edges/pallas_call | solution.py:377
  17.5 0.1 collective-permute-start.2
  17.6 5.3 %collective-permute-start.3 = (f32[1,512,128]{2,1,0:T(8,128)S(1)}, f32[1,512,128]{2,1,0:T(8,128)S(1)}, u32[]{:S(2)}, u32[]{:S(2)}) collective-permute-start(f32[1,512,128]{2,1,0:T(8,128)S(1)} %get-tuple-element.43.head_ref), channel_id=1, source_target_pairs={{0,15},{1,0},{2,1},{3,2},{4,3},{5,4},{6,5},{7,6},{8,7},{9,8},{10,9... | collective-permute-start | bytes 786440 | tf_op jit(solution)/shard_map/ppermute | solution.py:671
  22.9 3.7 %second_step_middle.1 = (f32[2,512,128]{2,1,0:T(8,128)S(1)}, f32[2,256,128]{2,1,0:T(8,128)S(1)}, bf16[8,256,256]{2,1,0:T(8,128)(2,1)S(1)}) custom-call(f32[1,512,128]{2,1,0:T(8,128)S(1)} %get-tuple-element.43.head_ref, f32[2,512,128]{2,1,0:T(8,128)S(1)} %get-tuple-element.44.middle_in_ref.middle_ref, f32[1,512,128]{2,1,0:T(8,128)S(1)} %get-tuple-element.42.tail_ref, ...), custom_call_target="tpu_custom_call" | custom-call | flops 3500000000 | bytes 4000000 | tf_op jit(solution)/shard_map/second_step_middle/pallas_call | solution.py:377
  26.6 0.0 collective-permute-start.4
  26.7 2.3 %second_step_edges_own.1.edge_in_ref = f32[2,512,128]{2,1,0:T(8,128)S(1)} custom-call(f32[1,512,128]{2,1,0:T(8,128)S(1)} %get-tuple-element.43.head_ref, f32[2,512,128]{2,1,0:T(8,128)S(1)} %get-tuple-element.44.middle_in_ref.middle_ref, f32[1,512,128]{2,1,0:T(8,128)S(1)} %get-tuple-element.42.tail_ref, s32[6,2048]{1,0:T(8,128)S(1)} %get-tuple-element.31.table_ref, ...), custom_call_target="tpu_custom_call" | custom-call | flops 2500000000 | bytes 4000000 | tf_op jit(solution)/shard_map/second_step_edges_own/pallas_call | solution.py:377
  29.0 0.0 copy-start
  29.0 0.0 collective-permute-done.2.left_ref
  29.0 0.0 collective-permute-done.3.right_ref
  29.0 1.7 %second_step_edges.1 = (f32[1,512,128]{2,1,0:T(8,128)S(1)}, f32[1,512,128]{2,1,0:T(8,128)S(1)}, f32[2,256,128]{2,1,0:T(8,128)S(1)}) custom-call(f32[1,512,128]{2,1,0:T(8,128)S(1)} %collective-permute-done.2.left_ref, f32[1,512,128]{2,1,0:T(8,128)S(1)} %collective-permute-done.3.right_ref, s32[6,2048]{1,0:T(8,128)S(1)} %get-tuple-element.31.table_ref, ...), custom_call_target="tpu_custom_call" | custom-call | flops 1000000000 | bytes 4000000 | tf_op jit(solution)/shard_map/second_step_edges/pallas_call | solution.py:377
  30.7 1.7 %collective-permute-start.5 = (f32[2,256,128]{2,1,0:T(8,128)S(1)}, f32[2,256,128]{2,1,0:T(8,128)S(1)}, u32[]{:S(2)}, u32[]{:S(2)}) collective-permute-start(f32[2,256,128]{2,1,0:T(8,128)S(1)} %get-tuple-element.51), channel_id=1, source_target_pairs={{0,16},{16,32},{32,48},{48,64},{64,80},{80,96},{96,112},{112,0},{1... | collective-permute-start | bytes 786440 | tf_op jit(solution)/shard_map/ppermute | solution.py:671
  32.4 1.2 %collective-permute-done.4.came_ref = f32[2,256,128]{2,1,0:T(8,128)S(1)} collective-permute-done((f32[2,256,128]{2,1,0:T(8,128)S(1)}, f32[2,256,128]{2,1,0:T(8,128)S(1)}, u32[]{:S(2)}, u32[]{:S(2)}) %collective-permute-start.4) | collective-permute-done | bytes 262176 | tf_op jit(solution)/shard_map/ppermute | solution.py:671
  33.7 0.0 copy-done
  33.7 2.4 %residual_known.1 = (f32[2,2,32,2048]{3,2,1,0:T(8,128)}, f32[2,2,32,2048]{3,2,1,0:T(8,128)S(1)}, f32[15,8,128]{2,1,0:T(8,128)S(1)}, f32[4,8,128]{2,1,0:T(8,128)S(1)}) custom-call(f32[2,2,32,2048]{3,2,1,0:T(8,128)S(1)} %get-tuple-element.30.state_ref, s32[16,128]{1,0:T(8,128)S(1)} %get-tuple-element.34.wet_ref, f32[4,2,2,32,2048]{4,3,2,1,0:T(8,128)S(1)} %copy-done, ...), custom_call_target="tpu_custom_call" | custom-call | flops 10000000 | bytes 4000000 | tf_op jit(solution)/shard_map/residual_known/pallas_call | solution.py:577
  36.1 1.6 %collective-permute-done.5.came_ref = f32[2,256,128]{2,1,0:T(8,128)S(1)} collective-permute-done((f32[2,256,128]{2,1,0:T(8,128)S(1)}, f32[2,256,128]{2,1,0:T(8,128)S(1)}, u32[]{:S(2)}, u32[]{:S(2)}) %collective-permute-start.5) | collective-permute-done | bytes 262176 | tf_op jit(solution)/shard_map/ppermute | solution.py:671
  37.8 0.4 residual_last.1
  38.1 17.4 %all_to_all.11 = f32[128,1,128]{2,1,0:T(1,128)S(1)} all-to-all(f32[128,1,128]{2,1,0:T(1,128)S(1)} %bitcast.7), channel_id=1, replica_groups=mesh['seg'=8,'col'=16] {'seg','col'}, dimensions={0} | all-to-all | bytes 131072 | tf_op jit(solution)/shard_map/all_to_all | solution.py:693
  55.5 2.1 %orthogonal_and_scaled.1 = (f32[2,2,32,2048]{3,2,1,0:T(8,128)}, f32[2,2,32,2048]{3,2,1,0:T(8,128)}, f32[5]{0:T(128)}) custom-call(f32[2,2,32,2048]{3,2,1,0:T(8,128)S(1)} %get-tuple-element.50.residual_ref, f32[2,2,32,512]{3,2,1,0:T(8,128)S(1)} %get-tuple-element.54.pieces_ref, f32[4,2,2,32,2048]{4,3,2,1,0:T(8,128)S(1)} %copy-done, ...), custom_call_target="tpu_custom_call", output_to_operand_aliasing={{0}: (4, {})} | custom-call | flops 4000000 | bytes 4000000 | tf_op jit(solution)/shard_map/orthogonal_and_scaled/pallas_call | solution.py:656
Async XLA Ops:
  2.3 13.5 %collective-permute-start = (f32[2,2,32,512]{3,2,1,0:T(8,128)S(1)}, f32[2,2,32,512]{3,2,1,0:T(8,128)S(1)}, u32[]{:S(2)}, u32[]{:S(2)}) collective-permute-start(f32[2,2,32,512]{3,2,1,0:T(8,128)S(1)} %get-tuple-element.35), channel_id=1, source_target_pairs={{0,1},{1,2},{2,3},{3,4},{4,5},{5,6},{6,7},{7,8},{8,9},{9,10},{10,1... | collective-permute-start | bytes 786440 | tf_op jit(solution)/shard_map/ppermute | solution.py:671
  4.4 11.5 %collective-permute-start.1 = (f32[2,2,32,512]{3,2,1,0:T(8,128)S(1)}, f32[2,2,32,512]{3,2,1,0:T(8,128)S(1)}, u32[]{:S(2)}, u32[]{:S(2)}) collective-permute-start(f32[2,2,32,512]{3,2,1,0:T(8,128)S(1)} %get-tuple-element.36), channel_id=1, source_target_pairs={{0,15},{1,0},{2,1},{3,2},{4,3},{5,4},{6,5},{7,6},{8,7},{9,8},{10,9... | collective-permute-start | bytes 786440 | tf_op jit(solution)/shard_map/ppermute | solution.py:671
  17.5 11.5 %collective-permute-start.2 = (f32[1,512,128]{2,1,0:T(8,128)S(1)}, f32[1,512,128]{2,1,0:T(8,128)S(1)}, u32[]{:S(2)}, u32[]{:S(2)}) collective-permute-start(f32[1,512,128]{2,1,0:T(8,128)S(1)} %get-tuple-element.42.tail_ref), channel_id=1, source_target_pairs={{0,1},{1,2},{2,3},{3,4},{4,5},{5,6},{6,7},{7,8},{8,9},{9,10},{10,1... | collective-permute-start | bytes 786440 | tf_op jit(solution)/shard_map/ppermute | solution.py:671
  17.6 11.4 %collective-permute-start.3 = (f32[1,512,128]{2,1,0:T(8,128)S(1)}, f32[1,512,128]{2,1,0:T(8,128)S(1)}, u32[]{:S(2)}, u32[]{:S(2)}) collective-permute-start(f32[1,512,128]{2,1,0:T(8,128)S(1)} %get-tuple-element.43.head_ref), channel_id=1, source_target_pairs={{0,15},{1,0},{2,1},{3,2},{4,3},{5,4},{6,5},{7,6},{8,7},{9,8},{10,9... | collective-permute-start | bytes 786440 | tf_op jit(solution)/shard_map/ppermute | solution.py:671
  26.6 7.0 %collective-permute-start.4 = (f32[2,256,128]{2,1,0:T(8,128)S(1)}, f32[2,256,128]{2,1,0:T(8,128)S(1)}, u32[]{:S(2)}, u32[]{:S(2)}) collective-permute-start(f32[2,256,128]{2,1,0:T(8,128)S(1)} %get-tuple-element.49), channel_id=1, source_target_pairs={{0,16},{16,32},{32,48},{48,64},{64,80},{80,96},{96,112},{112,0},{1... | collective-permute-start | bytes 786440 | tf_op jit(solution)/shard_map/ppermute | solution.py:671
  29.0 4.7 %copy-start = (f32[4,2,2,32,2048]{4,3,2,1,0:T(8,128)S(1)}, f32[4,2,2,32,2048]{4,3,2,1,0:T(8,128)}, u32[]{:S(2)}) copy-start(f32[4,2,2,32,2048]{4,3,2,1,0:T(8,128)} %basis_ref.5) | copy-start | bytes 12582916
  30.7 7.0 %collective-permute-start.5 = (f32[2,256,128]{2,1,0:T(8,128)S(1)}, f32[2,256,128]{2,1,0:T(8,128)S(1)}, u32[]{:S(2)}, u32[]{:S(2)}) collective-permute-start(f32[2,256,128]{2,1,0:T(8,128)S(1)} %get-tuple-element.51), channel_id=1, source_target_pairs={{0,16},{16,32},{32,48},{48,64},{64,80},{80,96},{96,112},{112,0},{1... | collective-permute-start | bytes 786440 | tf_op jit(solution)/shard_map/ppermute | solution.py:671

commit v7 on v6

--- a/solution.py
+++ b/solution.py
@@ -246,15 +246,12 @@
             ]
 
 
-QUARTER = (slice(None), slice(None), slice(None), pl.ds(0, HALO))
-
-
 def halves_kernel(
-    state_in, table_in, light_in, mixing_in,
-    head_ref, tail_ref, state_ref, table_ref, light_ref, mixing_ref,
+    state_in, table_in,
+    head_ref, tail_ref, state_ref, table_ref,
     sems,
 ):
-    pairs = [(state_in, state_ref), (table_in, table_ref), (light_in, light_ref), (mixing_in.at[QUARTER], mixing_ref)]
+    pairs = [(state_in, state_ref), (table_in, table_ref)]
     copies = [pltpu.make_async_copy(*pair, sems.at[i]) for i, pair in enumerate(pairs)]
     for copy in copies:
         copy.start()
@@ -269,37 +266,40 @@
     return [pltpu.with_memory_space_constraint(one, pltpu.HBM) for one in arrays]
 
 
-def halves(state, table, light, mixing):
+def halves(state, table):
     half = shape(SEGS, TRACERS, LEV, HALO)
-    like = [jax.ShapeDtypeStruct(one.shape, one.dtype) for one in (state, table, light)]
+    like = [jax.ShapeDtypeStruct(one.shape, one.dtype) for one in (state, table)]
     return pl.pallas_call(
         halves_kernel,
-        out_shape=(half, half, *like, shape(SEGS, NBR, LEV, HALO)),
-        in_specs=[HBM] * 4,
-        out_specs=(VMEM,) * 6,
-        scratch_shapes=[pltpu.SemaphoreType.DMA((4,))],
+        out_shape=(half, half, *like),
+        in_specs=[HBM] * 2,
+        out_specs=(VMEM,) * 4,
+        scratch_shapes=[pltpu.SemaphoreType.DMA((2,))],
         compiler_params=PARAMS,
         cost_estimate=pl.CostEstimate(flops=0, bytes_accessed=4_000_000, transcendentals=0),
         name="edge_columns",
-    )(*in_hbm(state, table, light, mixing))
+    )(*in_hbm(state, table))
 
 
 def first_own_kernel(
-    every_column, state_ref, table_ref, light_ref, quarter_ref, mixing_in, kappa_in, wet_in,
-    edge_ref, middle_ref, inverse_ref, carry_ref, ratio_ref, mixing_ref, wet_ref,
+    every_column, state_ref, table_ref, light_in, mixing_in, kappa_in, wet_in,
+    edge_ref, middle_ref, inverse_ref, carry_ref, ratio_ref, light_ref, mixing_ref, wet_ref,
     xs_ref, acc_ref, by_rows_ref, kappa_ref, sems,
 ):
-    order = (GROUPS - 1,) + tuple(range(1, GROUPS - 1)) + (0,)
+    order = (0, GROUPS - 1) + tuple(range(1, GROUPS - 1))
     parts = [(slice(None),) * 3 + (pl.ds(group * HALO, HALO),) for group in order]
-    pairs = [(kappa_in, kappa_ref), (wet_in, wet_ref)] + [(mixing_in.at[part], mixing_ref.at[part]) for part in parts]
+    pairs = [(mixing_in.at[part], mixing_ref.at[part]) for part in parts]
+    pairs = pairs[:1] + [(light_in, light_ref), (kappa_in, kappa_ref), (wet_in, wet_ref)] + pairs[1:]
     copies = [pltpu.make_async_copy(*pair, sems.at[i]) for i, pair in enumerate(pairs)]
     for copy in copies:
         copy.start()
     read = natural_reader(state_ref)
     for tile in range(BLOCKS):
         split_tile(read[0], tile * TILE, xs_ref, tile)
-    own_blocks(every_column, EDGE_BLOCKS[:2], read, table_ref, quarter_ref, light_ref, xs_ref, edge_ref, EDGE_PLACES)
-    for copy in copies:
+    for copy in copies[:2]:
+        copy.wait()
+    own_blocks(every_column, EDGE_BLOCKS[:2], read, table_ref, mixing_ref, light_ref, xs_ref, edge_ref, EDGE_PLACES)
+    for copy in copies[2:]:
         copy.wait()
     own_blocks(every_column, EDGE_BLOCKS[2:], read, table_ref, mixing_ref, light_ref, xs_ref, edge_ref, EDGE_PLACES)
     factorize(kappa_ref, wet_ref, by_rows_ref, inverse_ref, carry_ref, ratio_ref)
@@ -386,25 +386,25 @@
     )(*operands)
 
 
-def first_own(every_column, state, table, light, quarter, mixing, kappa, wet):
+def first_own(every_column, state, table, light, mixing, kappa, wet):
     factors = shape(GROUPS, LEV, CHUNKS * SEGS, LANE)
-    like = [jax.ShapeDtypeStruct(one.shape, one.dtype) for one in (mixing, wet)]
+    like = [jax.ShapeDtypeStruct(one.shape, one.dtype) for one in (light, mixing, wet)]
     return pl.pallas_call(
         functools.partial(first_own_kernel, every_column),
         out_shape=(EDGE, MIDDLE, factors, factors, factors, *like),
-        in_specs=[VMEM] * 4 + [HBM] * 3,
-        out_specs=(VMEM,) * 7,
+        in_specs=[VMEM] * 2 + [HBM] * 4,
+        out_specs=(VMEM,) * 8,
         scratch_shapes=[
             pltpu.VMEM((BLOCKS, 2 * ROWS, TILE), bf16),
             pltpu.VMEM((GROUPS - 2, GROUP_ROWS, LANE), f32),
             pltpu.VMEM((GROUPS * CHUNKS * SEGS * LEV, LANE), f32),
             pltpu.VMEM((SEGS, LEV, WIDTH), f32),
-            pltpu.SemaphoreType.DMA((2 + GROUPS,)),
+            pltpu.SemaphoreType.DMA((3 + GROUPS,)),
         ],
         compiler_params=PARAMS,
         cost_estimate=pl.CostEstimate(flops=6_000_000_000, bytes_accessed=4_000_000, transcendentals=0),
         name="first_step_own",
-    )(state, table, light, quarter, *in_hbm(mixing, kappa, wet))
+    )(state, table, *in_hbm(light, mixing, kappa, wet))
 
 
 def second_middle(every_column, head, middle, tail, table, mixing, light, factors):
@@ -675,10 +675,10 @@
     every_column = lax.axis_size("col") * WIDTH
     table = neighbour_columns.T
     wet = wet_levels.reshape(WIDTH // LANE, LANE)
-    head, tail, state, table, light, quarter = halves(segment_state, table, light, mixing)
+    head, tail, state, table = halves(segment_state, table)
     left = shifted(tail, "col", 1)
     right = shifted(head, "col", -1)
-    edge, middle, *factors, mixing, wet = first_own(every_column, state, table, light, quarter, mixing, kappa, wet)
+    edge, middle, *factors, light, mixing, wet = first_own(every_column, state, table, light, mixing, kappa, wet)
     head, tail = edges(True, every_column, left, right, table, mixing, edge, factors)
     left = shifted(tail, "col", 1)
     right = shifted(head, "col", -1)

time: 58.3 us -> 58.3 us (level)
  transfers between devices with their start and end apart: 6 -> 6, of which waited for: 2 -> 3; matrix products, arithmetic and copies ran while one was open for 0% -> 0% of each run, Pallas kernels for 30% -> 30%
where the time goes in v7:
time: 58.3 us; the launch traced here: 57.7 us
  Pallas kernels  22.5 us (39%)
  blocking collectives  17.7 us (30%)
  starting transfers between devices  13.4 us (23%)
  waiting for transfers between devices  3.22 us (6%)
  between operations  0.88 us (2%)
    all_to_all x1, blocking collectives, per_device(): sums = lax.all_to_all(sums, ('seg', 'col'), 0, 0, tiled=True)  17.7 us
    ppermute x6, starting transfers between devices, shifted(): lax.ppermute(block, axis, [(i, (i + distance) % count) for i in range(cou...  13.4 us
    pallas_call x5, Pallas kernels, call(): pl.pallas_call(kernel, out_shape=outs, in_specs=[VMEM] * len(operands), o...  9.24 us
    pallas_call x1, Pallas kernels, first_own(): pl.pallas_call(functools.partial(first_own_kernel, every_column), out_sha...  7.47 us
    ppermute x6, waiting for transfers between devices, shifted(): lax.ppermute(block, axis, [(i, (i + distance) % count) for i in range(cou...  3.22 us
    pallas_call x1, Pallas kernels, early(): pl.pallas_call(early_kernel, out_shape=(whole, whole, shape(SUMS, 8, LANE...  2.43 us
    pallas_call x1, Pallas kernels, scaled(): pl.pallas_call(functools.partial(scaled_kernel, count), out_shape=(shape(...  2.05 us
    pallas_call x1, Pallas kernels, halves(): pl.pallas_call(halves_kernel, out_shape=(half, half, *like), in_specs=[HB...  1.28 us
  transfers between devices with their start and end apart: 6, of which 3 were waited for; matrix products, arithmetic and copies ran while one was open for 0% of the time, Pallas kernels for 30%

profile of v7, /device:TPU:0, one launch (start us, length us, event | category | flops | bytes accessed | tf_op | source)
XLA Modules:
  0.0 57.7 jit_solution(7130314451664927500)
XLA Ops:
  0.6 1.3 %edge_columns.1 = (f32[2,2,32,512]{3,2,1,0:T(8,128)S(1)}, f32[2,2,32,512]{3,2,1,0:T(8,128)S(1)}, f32[2,2,32,2048]{3,2,1,0:T(8,128)S(1)}, s32[6,2048]{1,0:T(8,128)S(1)}) custom-call(f32[2,2,32,2048]{3,2,1,0:T(8,128)} %state_in.1, s32[6,2048]{1,0:T(8,128)} %bitcast.8), custom_call_target="tpu_custom_call" | custom-call | bytes 4000000 | tf_op jit(solution)/shard_map/edge_columns/pallas_call | solution.py:272
  1.9 2.1 %collective-permute-start = (f32[2,2,32,512]{3,2,1,0:T(8,128)S(1)}, f32[2,2,32,512]{3,2,1,0:T(8,128)S(1)}, u32[]{:S(2)}, u32[]{:S(2)}) collective-permute-start(f32[2,2,32,512]{3,2,1,0:T(8,128)S(1)} %get-tuple-element.32), channel_id=1, source_target_pairs={{0,1},{1,2},{2,3},{3,4},{4,5},{5,6},{6,7},{7,8},{8,9},{9,10},{10,1... | collective-permute-start | bytes 786440 | tf_op jit(solution)/shard_map/ppermute | solution.py:671
  4.0 4.4 %collective-permute-start.1 = (f32[2,2,32,512]{3,2,1,0:T(8,128)S(1)}, f32[2,2,32,512]{3,2,1,0:T(8,128)S(1)}, u32[]{:S(2)}, u32[]{:S(2)}) collective-permute-start(f32[2,2,32,512]{3,2,1,0:T(8,128)S(1)} %get-tuple-element.33), channel_id=1, source_target_pairs={{0,15},{1,0},{2,1},{3,2},{4,3},{5,4},{6,5},{7,6},{8,7},{9,8},{10,9... | collective-permute-start | bytes 786440 | tf_op jit(solution)/shard_map/ppermute | solution.py:671
  8.4 7.5 %first_step_own.1 = (f32[2,512,128]{2,1,0:T(8,128)S(1)}, f32[2,512,128]{2,1,0:T(8,128)S(1)}, f32[4,32,8,128]{3,2,1,0:T(8,128)S(1)}, f32[4,32,8,128]{3,2,1,0:T(8,...) custom-call(f32[2,2,32,2048]{3,2,1,0:T(8,128)S(1)} %get-tuple-elemen, ...), custom_call_target="tpu_custom_call" | custom-call | flops 6000000000 | bytes 4000000 | tf_op jit(solution)/shard_map/first_step_own/pallas_call | solution.py:392
  15.9 0.0 collective-permute-done.left_ref
  15.9 0.0 collective-permute-done.1.right_ref
  15.9 1.7 %first_step_edges.1 = (f32[1,512,128]{2,1,0:T(8,128)S(1)}, f32[1,512,128]{2,1,0:T(8,128)S(1)}) custom-call(f32[2,2,32,512]{3,2,1,0:T(8,128)S(1)} %collective-permute-done.left_ref, f32[2,2,32,512]{3,2,1,0:T(8,128)S(1)} %collective-permute-done.1.right_ref, s32[6,2048]{1,0:T(8,128)S(1)} %get-tuple-element.30.table_ref, ...), custom_call_target="tpu_custom_call" | custom-call | flops 1000000000 | bytes 4000000 | tf_op jit(solution)/shard_map/first_step_edges/pallas_call | solution.py:377
  17.5 0.1 collective-permute-start.2
  17.6 5.3 %collective-permute-start.3 = (f32[1,512,128]{2,1,0:T(8,128)S(1)}, f32[1,512,128]{2,1,0:T(8,128)S(1)}, u32[]{:S(2)}, u32[]{:S(2)}) collective-permute-start(f32[1,512,128]{2,1,0:T(8,128)S(1)} %get-tuple-element.40.head_ref), channel_id=1, source_target_pairs={{0,15},{1,0},{2,1},{3,2},{4,3},{5,4},{6,5},{7,6},{8,7},{9,8},{10,9... | collective-permute-start | bytes 786440 | tf_op jit(solution)/shard_map/ppermute | solution.py:671
  23.0 3.4 %second_step_middle.1 = (f32[2,512,128]{2,1,0:T(8,128)S(1)}, f32[2,256,128]{2,1,0:T(8,128)S(1)}, bf16[8,256,256]{2,1,0:T(8,128)(2,1)S(1)}) custom-call(f32[1,512,128]{2,1,0:T(8,128)S(1)} %get-tuple-element.40.head_ref, f32[2,512,128]{2,1,0:T(8,128)S(1)} %get-tuple-element.41.middle_in_ref.middle_ref, f32[1,512,128]{2,1,0:T(8,128)S(1)} %get-tuple-element.39.tail_ref, ...), custom_call_target="tpu_custom_call" | custom-call | flops 3500000000 | bytes 4000000 | tf_op jit(solution)/shard_map/second_step_middle/pallas_call | solution.py:377
  26.4 0.0 collective-permute-start.4
  26.4 2.1 %second_step_edges_own.1.edge_in_ref = f32[2,512,128]{2,1,0:T(8,128)S(1)} custom-call(f32[1,512,128]{2,1,0:T(8,128)S(1)} %get-tuple-element.40.head_ref, f32[2,512,128]{2,1,0:T(8,128)S(1)} %get-tuple-element.41.middle_in_ref.middle_ref, f32[1,512,128]{2,1,0:T(8,128)S(1)} %get-tuple-element.39.tail_ref, s32[6,2048]{1,0:T(8,128)S(1)} %get-tuple-element.30.table_ref, ...), custom_call_target="tpu_custom_call" | custom-call | flops 2500000000 | bytes 4000000 | tf_op jit(solution)/shard_map/second_step_edges_own/pallas_call | solution.py:377
  28.5 0.0 copy-start
  28.5 0.2 collective-permute-done.2.left_ref
  28.7 0.0 collective-permute-done.3.right_ref
  28.7 1.7 %second_step_edges.1 = (f32[1,512,128]{2,1,0:T(8,128)S(1)}, f32[1,512,128]{2,1,0:T(8,128)S(1)}, f32[2,256,128]{2,1,0:T(8,128)S(1)}) custom-call(f32[1,512,128]{2,1,0:T(8,128)S(1)} %collective-permute-done.2.left_ref, f32[1,512,128]{2,1,0:T(8,128)S(1)} %collective-permute-done.3.right_ref, s32[6,2048]{1,0:T(8,128)S(1)} %get-tuple-element.30.table_ref, ...), custom_call_target="tpu_custom_call" | custom-call | flops 1000000000 | bytes 4000000 | tf_op jit(solution)/shard_map/second_step_edges/pallas_call | solution.py:377
  30.4 1.5 %collective-permute-start.5 = (f32[2,256,128]{2,1,0:T(8,128)S(1)}, f32[2,256,128]{2,1,0:T(8,128)S(1)}, u32[]{:S(2)}, u32[]{:S(2)}) collective-permute-start(f32[2,256,128]{2,1,0:T(8,128)S(1)} %get-tuple-element.49), channel_id=1, source_target_pairs={{0,16},{16,32},{32,48},{48,64},{64,80},{80,96},{96,112},{112,0},{1... | collective-permute-start | bytes 786440 | tf_op jit(solution)/shard_map/ppermute | solution.py:671
  32.0 1.5 %collective-permute-done.4.came_ref = f32[2,256,128]{2,1,0:T(8,128)S(1)} collective-permute-done((f32[2,256,128]{2,1,0:T(8,128)S(1)}, f32[2,256,128]{2,1,0:T(8,128)S(1)}, u32[]{:S(2)}, u32[]{:S(2)}) %collective-permute-start.4) | collective-permute-done | bytes 262176 | tf_op jit(solution)/shard_map/ppermute | solution.py:671
  33.4 0.0 copy-done
  33.4 2.4 %residual_known.1 = (f32[2,2,32,2048]{3,2,1,0:T(8,128)}, f32[2,2,32,2048]{3,2,1,0:T(8,128)S(1)}, f32[15,8,128]{2,1,0:T(8,128)S(1)}, f32[4,8,128]{2,1,0:T(8,128)S(1)}) custom-call(f32[2,2,32,2048]{3,2,1,0:T(8,128)S(1)} %get-tuple-element.29.state_ref, s32[16,128]{1,0:T(8,128)S(1)} %get-tuple-element.31.wet_ref, f32[4,2,2,32,2048]{4,3,2,1,0:T(8,128)S(1)} %copy-done, ...), custom_call_target="tpu_custom_call" | custom-call | flops 10000000 | bytes 4000000 | tf_op jit(solution)/shard_map/residual_known/pallas_call | solution.py:577
  35.9 1.6 %collective-permute-done.5.came_ref = f32[2,256,128]{2,1,0:T(8,128)S(1)} collective-permute-done((f32[2,256,128]{2,1,0:T(8,128)S(1)}, f32[2,256,128]{2,1,0:T(8,128)S(1)}, u32[]{:S(2)}, u32[]{:S(2)}) %collective-permute-start.5) | collective-permute-done | bytes 262176 | tf_op jit(solution)/shard_map/ppermute | solution.py:671
  37.4 0.4 residual_last.1
  37.8 17.7 %all_to_all.11 = f32[128,1,128]{2,1,0:T(1,128)S(1)} all-to-all(f32[128,1,128]{2,1,0:T(1,128)S(1)} %bitcast.7), channel_id=1, replica_groups=mesh['seg'=8,'col'=16] {'seg','col'}, dimensions={0} | all-to-all | bytes 131072 | tf_op jit(solution)/shard_map/all_to_all | solution.py:693
  55.5 2.1 %orthogonal_and_scaled.1 = (f32[2,2,32,2048]{3,2,1,0:T(8,128)}, f32[2,2,32,2048]{3,2,1,0:T(8,128)}, f32[5]{0:T(128)}) custom-call(f32[2,2,32,2048]{3,2,1,0:T(8,128)S(1)} %get-tuple-element.48.residual_ref, f32[2,2,32,512]{3,2,1,0:T(8,128)S(1)} %get-tuple-element.52.pieces_ref, f32[4,2,2,32,2048]{4,3,2,1,0:T(8,128)S(1)} %copy-done, ...), custom_call_target="tpu_custom_call", output_to_operand_aliasing={{0}: (4, {})} | custom-call | flops 4000000 | bytes 4000000 | tf_op jit(solution)/shard_map/orthogonal_and_scaled/pallas_call | solution.py:656
Async XLA Ops:
  1.9 13.9 %collective-permute-start = (f32[2,2,32,512]{3,2,1,0:T(8,128)S(1)}, f32[2,2,32,512]{3,2,1,0:T(8,128)S(1)}, u32[]{:S(2)}, u32[]{:S(2)}) collective-permute-start(f32[2,2,32,512]{3,2,1,0:T(8,128)S(1)} %get-tuple-element.32), channel_id=1, source_target_pairs={{0,1},{1,2},{2,3},{3,4},{4,5},{5,6},{6,7},{7,8},{8,9},{9,10},{10,1... | collective-permute-start | bytes 786440 | tf_op jit(solution)/shard_map/ppermute | solution.py:671
  4.0 11.9 %collective-permute-start.1 = (f32[2,2,32,512]{3,2,1,0:T(8,128)S(1)}, f32[2,2,32,512]{3,2,1,0:T(8,128)S(1)}, u32[]{:S(2)}, u32[]{:S(2)}) collective-permute-start(f32[2,2,32,512]{3,2,1,0:T(8,128)S(1)} %get-tuple-element.33), channel_id=1, source_target_pairs={{0,15},{1,0},{2,1},{3,2},{4,3},{5,4},{6,5},{7,6},{8,7},{9,8},{10,9... | collective-permute-start | bytes 786440 | tf_op jit(solution)/shard_map/ppermute | solution.py:671
  17.5 11.2 %collective-permute-start.2 = (f32[1,512,128]{2,1,0:T(8,128)S(1)}, f32[1,512,128]{2,1,0:T(8,128)S(1)}, u32[]{:S(2)}, u32[]{:S(2)}) collective-permute-start(f32[1,512,128]{2,1,0:T(8,128)S(1)} %get-tuple-element.39.tail_ref), channel_id=1, source_target_pairs={{0,1},{1,2},{2,3},{3,4},{4,5},{5,6},{6,7},{7,8},{8,9},{9,10},{10,1... | collective-permute-start | bytes 786440 | tf_op jit(solution)/shard_map/ppermute | solution.py:671
  17.6 11.1 %collective-permute-start.3 = (f32[1,512,128]{2,1,0:T(8,128)S(1)}, f32[1,512,128]{2,1,0:T(8,128)S(1)}, u32[]{:S(2)}, u32[]{:S(2)}) collective-permute-start(f32[1,512,128]{2,1,0:T(8,128)S(1)} %get-tuple-element.40.head_ref), channel_id=1, source_target_pairs={{0,15},{1,0},{2,1},{3,2},{4,3},{5,4},{6,5},{7,6},{8,7},{9,8},{10,9... | collective-permute-start | bytes 786440 | tf_op jit(solution)/shard_map/ppermute | solution.py:671
  26.4 7.0 %collective-permute-start.4 = (f32[2,256,128]{2,1,0:T(8,128)S(1)}, f32[2,256,128]{2,1,0:T(8,128)S(1)}, u32[]{:S(2)}, u32[]{:S(2)}) collective-permute-start(f32[2,256,128]{2,1,0:T(8,128)S(1)} %get-tuple-element.47), channel_id=1, source_target_pairs={{0,16},{16,32},{32,48},{48,64},{64,80},{80,96},{96,112},{112,0},{1... | collective-permute-start | bytes 786440 | tf_op jit(solution)/shard_map/ppermute | solution.py:671
  28.5 4.9 %copy-start = (f32[4,2,2,32,2048]{4,3,2,1,0:T(8,128)S(1)}, f32[4,2,2,32,2048]{4,3,2,1,0:T(8,128)}, u32[]{:S(2)}) copy-start(f32[4,2,2,32,2048]{4,3,2,1,0:T(8,128)} %basis_ref.5) | copy-start | bytes 12582916
  30.4 7.0 %collective-permute-start.5 = (f32[2,256,128]{2,1,0:T(8,128)S(1)}, f32[2,256,128]{2,1,0:T(8,128)S(1)}, u32[]{:S(2)}, u32[]{:S(2)}) collective-permute-start(f32[2,256,128]{2,1,0:T(8,128)S(1)} %get-tuple-element.49), channel_id=1, source_target_pairs={{0,16},{16,32},{32,48},{48,64},{64,80},{80,96},{96,112},{112,0},{1... | collective-permute-start | bytes 786440 | tf_op jit(solution)/shard_map/ppermute | solution.py:671
